TPU v7x, 32 devices: a whole 2x2x4 slice. The times are simulated.
32 devices in a mesh: seq: 2 (over core), blk: 16 (over z, y, x).
Axes of the slice: x: 2, y: 2, z: 4, core: 2. Of those that a mesh axis runs over, the one named last changes fastest.
Arguments:
- tokens: bfloat16 [2, 4096, 1024], P('seq', 'blk'), may hold values from -6 to 6
- segments: int32 [2, 4096], P('seq', 'blk'), may hold values from 0 to 6, as said below
- routes: int32 [2, 4096, 8], P('seq', 'blk'), may hold values from 0 to 15, all different within a row; in each aligned block of 256 rows (0 to 255, 256 to 511, ..., all dimensions but the last counted through in order) at most 256 rows name the same one
- route_weight: float32 [2, 4096, 8], P('seq', 'blk'), may hold values from 0.5 to 1.5
- norm1_gain: float32 [1024], replicated, may hold values from 0.5 to 1.5
- w_query: bfloat16 [1024, 1024], replicated, may hold values from -0.1875 to 0.1875
- w_key: bfloat16 [1024, 512], replicated, may hold values from -0.1875 to 0.1875
- w_value: bfloat16 [1024, 512], replicated, may hold values from -0.1875 to 0.1875
- w_out: bfloat16 [1024, 1024], replicated, may hold values from -4 to 4
- norm2_gain: float32 [1024], replicated, may hold values from 0.5 to 1.5
- w_router: bfloat16 [1024, 16], replicated, may hold values from -0.09375 to 0.09375
- w_gate: bfloat16 [16, 1024, 512], P('blk'), may hold values from -0.1875 to 0.1875
- w_up: bfloat16 [16, 1024, 512], P('blk'), may hold values from -0.1875 to 0.1875
- w_down: bfloat16 [16, 512, 1024], P('blk'), may hold values from -1 to 1
- cotangent: bfloat16 [2, 4096, 1024], P('seq', 'blk'), may hold values from -6 to 6
Outputs:
- output: bfloat16 [2, 4096, 1024], P('seq', 'blk')
- tokens_grad: float32 [2, 4096, 1024], P('seq', 'blk')
- norm1_gain_grad: float32 [1024], replicated
- w_query_grad: float32 [1024, 1024], replicated
- w_key_grad: float32 [1024, 512], replicated
- w_value_grad: float32 [1024, 512], replicated
- w_out_grad: float32 [1024, 1024], replicated
- norm2_gain_grad: float32 [1024], replicated
- w_router_grad: float32 [1024, 16], replicated
- w_gate_grad: float32 [16, 1024, 512], P('blk')
- w_up_grad: float32 [16, 1024, 512], P('blk')
- w_down_grad: float32 [16, 512, 1024], P('blk')
Inputs may be any that keep to these rules, and one draw needn't show every extreme that they name: `segments`: segment numbers never fall along a sequence and begin at 0; each sequence has six document boundaries, some of which may coincide. In one of the 2 sequences, which one varies, the boundaries lie within its first 256 and its last 256 positions; in the others they may lie anywhere. `routes`: each token names 8 different experts; among the 256 tokens of one device no expert is named more than 256 times, a bound that some block reaches.
All inputs are finite; a program needn't handle non-finite values.
Results may differ from a plain program's by a relative error of at most 0.019.
Values may be sent and summed in bfloat16 or wider, within the bound.
A program may use at most 256 MiB of HBM per device.

v0:
```python
import math

import jax
import jax.numpy as jnp
from jax import lax
from jax.sharding import PartitionSpec as P

D = 1024
H = 16
KV = 8
HD = 64
TOP = 8


EPS = 1e-06
NEG = -1e30
HIGH = lax.Precision.HIGHEST


def rope_tables(positions):
    half = HD // 2
    freq = jnp.exp(-math.log(10000.0) * jnp.arange(half, dtype=jnp.float32) * 2.0 / HD)
    angle = positions.astype(jnp.float32)[:, None] * freq[None, :]
    cosine = jnp.concatenate([jnp.cos(angle), jnp.cos(angle)], -1)
    sine = jnp.concatenate([jnp.sin(angle), jnp.sin(angle)], -1)
    return (cosine, sine)


def rotate_half(v):
    half = v.shape[-1] // 2
    return jnp.concatenate([-v[..., half:], v[..., :half]], -1)


def rotary(v, cosine, sine):
    return v * cosine[:, None, :] + rotate_half(v) * sine[:, None, :]


def unrotary(v, cosine, sine):
    return v * cosine[:, None, :] - rotate_half(v) * sine[:, None, :]


def rms_scale(v):
    return lax.rsqrt(jnp.mean(v * v, -1, keepdims=True) + EPS)


def rms_back(inputs, scale_rows, gain, grad):
    scaled = grad * gain
    d_inputs = scale_rows * scaled - inputs * scale_rows**3 * jnp.mean(
        scaled * inputs, -1, keepdims=True
    )
    return (d_inputs, jnp.sum(grad * inputs * scale_rows, 0))


def scores(queries, keys):
    return jnp.einsum("qkgd,skd->kgqs", queries, keys, preferred_element_type=jnp.float32) * HD ** (
        -0.5
    )


def per_device(
    tokens,
    segments,
    routes,
    route_weight,
    norm1_gain,
    w_query,
    w_key,
    w_value,
    w_out,
    norm2_gain,
    w_router,
    w_gate,
    w_up,
    w_down,
    cotangent,
):
    f32 = jnp.float32
    bf16 = jnp.bfloat16
    scale = HD ** (-0.5)
    group = H // KV
    xs = tokens[0].astype(f32)
    tok = xs.shape[0]
    blocks = lax.axis_size("blk")
    length = tok * blocks
    first = lax.axis_index("blk") * tok
    last = first + tok - 1
    positions = first + jnp.arange(tok, dtype=jnp.int32)
    cosine, sine = rope_tables(positions)
    scale1 = rms_scale(xs)
    xa = (xs * scale1 * norm1_gain).astype(bf16)
    query = jnp.dot(xa, w_query, preferred_element_type=f32)
    key = jnp.dot(xa, w_key, preferred_element_type=f32)
    value = jnp.dot(xa, w_value, preferred_element_type=f32).astype(bf16)
    q_rot = rotary(query.reshape(tok, H, HD), cosine, sine).astype(bf16).reshape(tok, KV, group, HD)
    k_rot = rotary(key.reshape(tok, KV, HD), cosine, sine).astype(bf16).reshape(tok, KV * HD)
    seg_float = segments[0].astype(bf16)
    k_all, v_all, seg_all = (
        lax.all_gather(k_rot, "blk", axis=0, tiled=True),
        lax.all_gather(value, "blk", axis=0, tiled=True),
        lax.all_gather(seg_float, "blk", axis=0, tiled=True),
    )
    kblk = min(512, length)
    nblk = length // kblk
    k_blocks = k_all.reshape(nblk, kblk, KV, HD)
    v_blocks = v_all.reshape(nblk, kblk, KV, HD)
    s_blocks = seg_all.reshape(nblk, kblk)
    starts = jnp.arange(nblk, dtype=jnp.int32) * kblk

    def visible(kseg, kstart):
        kpos = kstart + jnp.arange(kblk, dtype=jnp.int32)
        return ((seg_float[:, None] == kseg[None, :]) & (kpos[None, :] <= positions[:, None]))[
            None, None
        ]

    def forward_step(carry, block):
        kb, vb, sb, start = block

        def forward_compute(state):
            running, total, acc = state
            mask = visible(sb, start)
            score = jnp.where(mask, scores(q_rot, kb), NEG)
            newmax = jnp.maximum(running, jnp.max(score, -1))
            expo = jnp.where(mask, jnp.exp(score - newmax[..., None]), 0.0)
            factor = jnp.exp(running - newmax)
            total = total * factor + jnp.sum(expo, -1)
            acc = acc * factor[..., None] + jnp.einsum(
                "kgqs,skd->kgqd", expo.astype(bf16), vb, preferred_element_type=f32
            )
            return (newmax, total, acc)

        return (lax.cond(start <= last, forward_compute, lambda state: state, carry), None)

    init = (
        jnp.full((KV, group, tok), NEG, f32),
        jnp.zeros((KV, group, tok), f32),
        jnp.zeros((KV, group, tok, HD), f32),
    )
    (running, total, acc), unused = lax.scan(
        forward_step, init, (k_blocks, v_blocks, s_blocks, starts)
    )
    lse = running + jnp.log(total)
    o_rows = (acc / total[..., None]).transpose(2, 0, 1, 3)
    att_low = o_rows.reshape(tok, H * HD).astype(bf16)
    h1 = xs + jnp.dot(att_low, w_out, preferred_element_type=f32)
    scale2 = rms_scale(h1)
    xl = (h1 * scale2 * norm2_gain).astype(bf16)
    logits = jnp.dot(xl, w_router, preferred_element_type=f32)
    experts = logits.shape[1]
    route = routes[0]
    rweight = route_weight[0]
    chooser = (route[:, :, None] == jnp.arange(experts, dtype=jnp.int32)[None, None, :]).astype(f32)
    chosen = jnp.sum(chooser * logits[:, None, :], -1)
    gates = jax.nn.softmax(chosen, -1)
    combine = (rweight * gates).astype(bf16)
    cap = min(tok, 2 * tok * TOP // experts)
    flat_route = route.reshape(-1)
    onehot = (flat_route[:, None] == jnp.arange(experts, dtype=jnp.int32)[None, :]).astype(
        jnp.int32
    )
    rank = jnp.sum((jnp.cumsum(onehot, 0) - onehot) * onehot, -1)
    slots = (flat_route * cap + rank).reshape(tok, TOP)
    placed = jnp.any(
        slots[:, :, None] == jnp.arange(experts * cap, dtype=jnp.int32)[None, None, :], 1
    ).astype(bf16)
    outgoing = jnp.einsum("ts,td->sd", placed, xl, preferred_element_type=f32).astype(bf16)
    incoming = lax.all_to_all(
        outgoing.reshape(experts, cap, D), "blk", split_axis=0, concat_axis=0, tiled=True
    )
    local_exp = w_gate.shape[0]
    incoming = incoming.reshape(blocks, local_exp, cap, D)
    gate_pre = jnp.einsum("necd,edf->necf", incoming, w_gate, preferred_element_type=f32)
    up_pre = jnp.einsum("necd,edf->necf", incoming, w_up, preferred_element_type=f32)
    sigma = jax.nn.sigmoid(gate_pre)
    activated = gate_pre * sigma
    hidden = (activated * up_pre).astype(bf16)
    expert_out = jnp.einsum("necf,efd->necd", hidden, w_down, preferred_element_type=f32).astype(
        bf16
    )
    returned = lax.all_to_all(
        expert_out.reshape(experts, cap, D), "blk", split_axis=0, concat_axis=0, tiled=True
    )
    per_route = jnp.take(returned.reshape(experts * cap, D), slots.reshape(-1), axis=0).reshape(
        tok, TOP, D
    )
    mixture = jnp.einsum("tj,tjd->td", combine, per_route, preferred_element_type=f32)
    result = h1 + mixture
    grad_out = cotangent[0].astype(f32)
    grad_combine = jnp.einsum("td,tjd->tj", grad_out, per_route.astype(f32), precision=HIGH)
    route_grads = (combine.astype(f32)[:, :, None] * grad_out[:, None, :]).astype(bf16)
    grad_slots = (
        jnp.zeros((experts * cap, D), bf16)
        .at[slots.reshape(-1)]
        .set(route_grads.reshape(tok * TOP, D))
    )
    grad_incoming = lax.all_to_all(
        grad_slots.reshape(experts, cap, D), "blk", split_axis=0, concat_axis=0, tiled=True
    )
    grad_incoming = grad_incoming.reshape(blocks, local_exp, cap, D)
    grad_hidden = jnp.einsum("necd,efd->necf", grad_incoming, w_down, preferred_element_type=f32)
    grad_gate = (grad_hidden * up_pre * sigma * (1.0 + gate_pre * (1.0 - sigma))).astype(bf16)
    grad_up = (grad_hidden * activated).astype(bf16)
    d_down = jnp.einsum("necf,necd->efd", hidden, grad_incoming, preferred_element_type=f32)
    d_gate_w = jnp.einsum("necd,necf->edf", incoming, grad_gate, preferred_element_type=f32)
    d_up_w = jnp.einsum("necd,necf->edf", incoming, grad_up, preferred_element_type=f32)
    grad_in = (
        jnp.einsum("necf,edf->necd", grad_gate, w_gate, preferred_element_type=f32)
        + jnp.einsum("necf,edf->necd", grad_up, w_up, preferred_element_type=f32)
    ).astype(bf16)
    grad_back = lax.all_to_all(
        grad_in.reshape(experts, cap, D), "blk", split_axis=0, concat_axis=0, tiled=True
    )
    grad_xl = jnp.einsum(
        "ts,sd->td", placed, grad_back.reshape(experts * cap, D), preferred_element_type=f32
    )
    grad_gates = rweight * grad_combine
    grad_chosen = gates * (grad_gates - jnp.sum(gates * grad_gates, -1, keepdims=True))
    grad_logits = jnp.sum(chooser * grad_chosen[:, :, None], 1).astype(bf16)
    d_router = jnp.einsum("td,te->de", xl, grad_logits, preferred_element_type=f32)
    grad_xl = grad_xl + jnp.einsum("te,de->td", grad_logits, w_router, preferred_element_type=f32)
    grad_h1_norm, d_gain2 = rms_back(h1, scale2, norm2_gain, grad_xl)
    grad_h1 = grad_out + grad_h1_norm
    grad_att = grad_h1.astype(bf16)
    d_out_w = jnp.einsum("ti,td->id", att_low, grad_att, preferred_element_type=f32)
    grad_o = jnp.einsum("td,id->ti", grad_att, w_out, preferred_element_type=f32).astype(bf16)
    grad_o_rows = grad_o.reshape(tok, KV, group, HD)
    delta = jnp.einsum("qkgd,qkgd->kgq", grad_o_rows.astype(f32), o_rows)

    def query_terms(kb, vb, sb, start):
        mask = visible(sb, start)
        prob = jnp.where(mask, jnp.exp(scores(q_rot, kb) - lse[..., None]), 0.0)
        dprob = jnp.einsum("qkgd,skd->kgqs", grad_o_rows, vb, preferred_element_type=f32)
        dscore = (prob * (dprob - delta[..., None])).astype(bf16)
        dq_term = jnp.einsum("kgqs,skd->qkgd", dscore, kb, preferred_element_type=f32) * scale
        return (dq_term, dscore, prob)

    zero_q = jnp.zeros((tok, KV, group, HD), f32)

    def backward_step(grad_q, block):
        kb, vb, sb, start = block

        def backward_compute(acc_q):
            dq_term, dscore, prob = query_terms(kb, vb, sb, start)
            gk = jnp.einsum("kgqs,qkgd->skd", dscore, q_rot, preferred_element_type=f32) * scale
            gv = jnp.einsum(
                "kgqs,qkgd->skd", prob.astype(bf16), grad_o_rows, preferred_element_type=f32
            )
            return (acc_q + dq_term, (gk.reshape(kblk, KV * HD), gv.reshape(kblk, KV * HD)))

        def skip(acc_q):
            empty = jnp.zeros((kblk, KV * HD), f32)
            return (acc_q, (empty, empty))

        return lax.cond(start <= last, backward_compute, skip, grad_q)

    grad_q, (gk_blocks, gv_blocks) = lax.scan(
        backward_step, zero_q, (k_blocks, v_blocks, s_blocks, starts)
    )
    grad_k, grad_v = (
        lax.psum_scatter(
            gk_blocks.reshape(length, KV * HD).astype(jnp.bfloat16),
            "blk",
            scatter_dimension=0,
            tiled=True,
        ).astype(jnp.float32),
        lax.psum_scatter(
            gv_blocks.reshape(length, KV * HD).astype(jnp.bfloat16),
            "blk",
            scatter_dimension=0,
            tiled=True,
        ).astype(jnp.float32),
    )
    grad_qr = unrotary(grad_q.reshape(tok, H, HD), cosine, sine).reshape(tok, H * HD).astype(bf16)
    grad_kr = unrotary(grad_k.reshape(tok, KV, HD), cosine, sine).reshape(tok, KV * HD).astype(bf16)
    grad_vr = grad_v.astype(bf16)
    d_query = jnp.einsum("td,te->de", xa, grad_qr, preferred_element_type=f32)
    d_key = jnp.einsum("td,te->de", xa, grad_kr, preferred_element_type=f32)
    d_value = jnp.einsum("td,te->de", xa, grad_vr, preferred_element_type=f32)
    grad_xa = (
        jnp.einsum("te,de->td", grad_qr, w_query, preferred_element_type=f32)
        + jnp.einsum("te,de->td", grad_kr, w_key, preferred_element_type=f32)
        + jnp.einsum("te,de->td", grad_vr, w_value, preferred_element_type=f32)
    )
    grad_x_norm, d_gain1 = rms_back(xs, scale1, norm1_gain, grad_xa)
    grad_x = grad_h1 + grad_x_norm
    summed = lax.psum(
        (d_gain1, d_query, d_key, d_value, d_out_w, d_gain2, d_router), ("seq", "blk")
    )
    expert_summed = (
        lax.psum(d_gate_w.astype(jnp.bfloat16), "seq").astype(jnp.float32),
        lax.psum(d_up_w.astype(jnp.bfloat16), "seq").astype(jnp.float32),
        lax.psum(d_down.astype(jnp.bfloat16), "seq").astype(jnp.float32),
    )
    return (
        result.astype(bf16)[None],
        grad_x[None],
        summed[0],
        summed[1],
        summed[2],
        summed[3],
        summed[4],
        summed[5],
        summed[6],
        expert_summed[0],
        expert_summed[1],
        expert_summed[2],
    )


def solution(mesh):
    return jax.shard_map(
        per_device,
        mesh=mesh,
        in_specs=(
            P("seq", "blk", None),
            P("seq", "blk"),
            P("seq", "blk", None),
            P("seq", "blk", None),
            P(),
            P(),
            P(),
            P(),
            P(),
            P(),
            P(),
            P("blk", None, None),
            P("blk", None, None),
            P("blk", None, None),
            P("seq", "blk", None),
        ),
        out_specs=(
            P("seq", "blk", None),
            P("seq", "blk", None),
            P(),
            P(),
            P(),
            P(),
            P(),
            P(),
            P(),
            P("blk", None, None),
            P("blk", None, None),
            P("blk", None, None),
        ),
        check_vma=False,
    )
```

profile of v0, /device:TPU:0, one launch (start us, length us, event | category | flops | bytes accessed | tf_op | source)
XLA Modules:
  0.0 1820.1 jit_solution(16352567257517354006)
XLA Ops:
  9.3 2.3 copy.103
  14.7 2.6 convolution_convert_fusion.3
  17.6 3.9 copy.104
  21.6 42.6 %all-gather = bf16[1,4096]{1,0:T(2,128)(2,1)S(1)} all-gather(bf16[1,256]{1,0:T(2,128)(2,1)S(1)} %convert_element_type.204), channel_id=2, replica_groups=mesh['seq'=2,'blk'=16] {'blk'}, dimensions={1}, use_global_device_ids=true | all-gather | bytes 8704 | tf_op jit(solution)/shard_map/all_gather | solution.py:100
  64.3 4.5 reduce-window.6
  70.0 2.4 fusion.114
  72.8 19.5 %fusion.46 = pred[256,4096]{1,0:T(8,128)(4,1)} fusion(s32[256,8]{1,0:T(8,128)S(1)} %copy.112), kind=kLoop, calls=%fused_computation.61 | loop fusion | flops 15728640 | bytes 1056768 | tf_op jit(solution)/shard_map/reduce_or | solution.py:162
  92.3 12.5 all-gather.4.cloned.1.call-done
  104.7 4.4 copy.169
  109.2 3.5 copy.106
  112.6 69.8 %all-gather.6.cloned.1.call-done = bf16[4096,512]{1,0:T(8,128)(2,1)} async-done(((bf16[256,512]{1,0:T(8,128)(2,1)}), bf16[4096,512]{1,0:T(8,128)(2,1)}) %all-gather.6.cloned.1.call-update) | async-done | bytes 4194320 | tf_op jit(solution)/shard_map/all_gather | solution.py:99
  182.5 11.2 reshape.552
  193.7 9.7 copy.107
  204.5 20.2 %while.33 = (s32[]{:T(128)}, f32[8,2,256]{2,1,0:T(2,128)S(1)}, f32[8,2,256]{2,1,0:T(2,128)S(1)}, f32[8,2,256,64]{2,3,1,0:T(8,128)}, s32[8]{0:T(128)S(1)}, /*inde...) while((s32[]{:T(128)}, f32[8,2,256]{2,1,0:T(2,128)S(1)}, ...), condition=%wide.region_6.7_spmd.clone, body=%wide.region_1.6_spmd.clone.sunk | while | flops 565322496 | bytes 38024048 | solution.py:138
  206.0 9.8 conditional.6
  206.9 2.5 fusion.4
  211.5 3.3 fusion.10
  229.5 3.8 convolution_convert_fusion
  233.3 256.3 %all_to_all.20 = bf16[16,256,1024]{2,1,0:T(8,128)(2,1)S(1)} all-to-all(bf16[16,256,1024]{2,1,0:T(8,128)(2,1)S(1)} %bitcast.403), channel_id=1, replica_groups=mesh['seq'=2,'blk'=16] {'blk'}, dimensions={0} | all-to-all | bytes 16777216 | tf_op jit(solution)/shard_map/all_to_all | solution.py:166
  489.7 4.5 fusion.105
  494.2 4.5 fusion.108
  498.8 3.1 fusion.59
  504.0 6.7 convolution_convert_fusion.1
  510.7 5.2 all-to-all-start.1
  518.0 150.1 %all-to-all-done.1 = bf16[16,256,1024]{2,1,0:T(8,128)(2,1)} async-done(((bf16[16,256,1024]{2,1,0:T(8,128)(2,1)}), bf16[16,256,1024]{2,1,0:T(8,128)(2,1)}, u32[]{:S(2)}, u32[]{:S(2)}) %all-to-all-start.1) | async-done | bytes 8388640 | tf_op jit(solution)/shard_map/all_to_all | solution.py:179
  668.1 15.4 gather_fusion
  683.6 5.5 fusion.68
  689.5 15.4 scatter_custom_fusion
  704.9 220.1 %all_to_all.21 = bf16[16,256,1024]{2,1,0:T(8,128)(2,1)S(1)} all-to-all(bf16[16,256,1024]{2,1,0:T(8,128)(2,1)} %bitcast.399), channel_id=1, replica_groups=mesh['seq'=2,'blk'=16] {'blk'}, dimensions={0} | all-to-all | bytes 16777216 | tf_op jit(solution)/shard_map/all_to_all | solution.py:195
  925.0 15.8 fusion.60
  940.8 10.5 fusion.63
  951.3 11.5 add_convert_fusion
  962.8 4.9 all-to-all-start.3
  968.4 4.5 fusion.69
  972.9 145.8 %all-to-all-done.3 = bf16[16,256,1024]{2,1,0:T(8,128)(2,1)} async-done(((bf16[16,256,1024]{2,1,0:T(8,128)(2,1)}), bf16[16,256,1024]{2,1,0:T(8,128)(2,1)}, u32[]{:S(2)}, u32[]{:S(2)}) %all-to-all-start.3) | async-done | bytes 8388640 | tf_op jit(solution)/shard_map/all_to_all | solution.py:209
  1118.7 5.9 fusion.149
  1131.7 86.5 %while.34 = (s32[]{:T(128)}, f32[256,8,2,64]{0,3,2,1:T(8,128)S(1)}, bf16[8,512,512]{2,1,0:T(8,128)(2,1)}, bf16[8,512,512]{2,1,0:T(8,128)(2,1)}, s32[8]{0:T(128)S...) while((s32[]{:T(128)}, f32[256,8,2,64]{0,3,2,1:T(8,128)S(1)}, ...), condition=%wide.region_22.23_spmd.clone, body=%wide.region_19.22_spmd.clone.sunk | while | flops 1364853504 | bytes 53409648 | solution.py:255
  1132.9 14.1 conditional.7
  1132.9 2.6 fusion.36
  1136.4 4.0 fusion.24
  1144.5 2.5 fusion.28
  1151.1 2.3 constant_dynamic-update-slice_fusion.3
  1160.4 2.2 constant_dynamic-update-slice_fusion.3
  1178.9 2.2 constant_dynamic-update-slice_fusion.3
  1188.2 2.2 constant_dynamic-update-slice_fusion.3
  1206.6 2.2 constant_dynamic-update-slice_fusion.3
  1215.9 2.3 constant_dynamic-update-slice_fusion.3
  1219.0 10.3 fusion.78
  1229.3 8.2 fusion.74
  1237.5 5.5 fusion.77
  1249.7 2.9 fusion.118
  1252.6 2.7 fusion.120
  1255.3 176.8 %reduce-scatter.3.cloned.1.call-done = bf16[256,512]{1,0:T(8,128)(2,1)} async-done(((bf16[4096,512]{1,0:T(8,128)(2,1)}), bf16[256,512]{1,0:T(8,128)(2,1)}) %reduce-scatter.3.cloned.1.call-update) | async-done | bytes 262160 | tf_op jit(solution)/shard_map/reduce_scatter | solution.py:259
  1439.4 2.9 fusion.142
  1442.3 86.7 %reduce-scatter.5.cloned.1.call-done = bf16[256,512]{1,0:T(8,128)(2,1)} async-done(((bf16[4096,512]{1,0:T(8,128)(2,1)}), bf16[256,512]{1,0:T(8,128)(2,1)}) %reduce-scatter.5.cloned.1.call-update) | async-done | bytes 262160 | tf_op jit(solution)/shard_map/reduce_scatter | solution.py:265
  1529.1 3.0 fusion.140
  1532.1 22.9 %all-reduce.8.cloned.1.call-done = (bf16[1,1024,512]{2,1,0:T(8,128)(2,1)}, bf16[1,1024,512]{2,1,0:T(8,128)(2,1)}, bf16[1,512,1024]{2,1,0:T(8,128)(2,1)}) async-done(((bf16[1,1024,512]{2,1,0:T(8,128)(2,1)}, bf16[1,1024,512]{2,1,0:T(8,128)(2,1)}, bf16[1,512,1024]{2,1,0:T(8,128)(2,1)}), (bf16[1,1024,512]{2,1,0:T(8,128)(2,1)}, bf16[1,1024,512]{2,1,0:T(8,128)(2,1)}, ...) | async-done | bytes 3145744 | tf_op jit(solution)/shard_map/psum | solution.py:289
  1555.0 3.0 convert_element_type.245
  1558.0 3.0 convert_element_type.248
  1561.0 2.8 convert_element_type.251
  1566.0 42.3 %all-reduce = (f32[1024]{0:T(1024)}, f32[1024]{0:T(1024)}) all-reduce(f32[1024]{0:T(1024)S(1)} %get-tuple-element.553, f32[1024]{0:T(1024)S(1)} %get-tuple-element.551), channel_id=1, replica_groups=mesh['seq'=2,'blk'=16] {'seq','blk'}, use_global_device_ids=true, to_apply=%region_27.28 | all-reduce | flops 2048 | bytes 16384 | tf_op jit(solution)/shard_map/psum | solution.py:285
  1608.3 2.7 fusion.90
  1611.0 191.7 %all-reduce.6.cloned.1.call-done = (f32[1024,1024]{1,0:T(8,128)}, f32[1024,512]{1,0:T(8,128)}, f32[1024,512]{1,0:T(8,128)}, f32[1024,1024]{1,0:T(8,128)}, f32[1024,16]{0,1:T(8,128)}) async-done(((f32[1024,1024]{1,0:T(8,128)}, f32[1024,512]{1,0:T(8,128)}, f32[1024,512]{1,0:T(8,128)}, f32[1024,1024]{1,0:T(8,128)}, f32[1024,16]{0,1:T(8,128)}), (f32[1024,1024]{1,0:T(8,128)}, f32[1024,512]{1,0:T(8,128)}, ...) | async-done | bytes 12648464 | tf_op jit(solution)/shard_map/psum | solution.py:285
  1802.6 5.1 copy.229
  (311 shorter events, 126.0 us)
Async XLA Ops:
  7.2 219.1 %copy-start = (bf16[1024,1024]{1,0:T(8,128)(2,1)S(1)}, bf16[1024,1024]{1,0:T(8,128)(2,1)}, u32[]{:S(2)}) copy-start(bf16[1024,1024]{1,0:T(8,128)(2,1)} %param.31) | copy-start | bytes 6291460
  7.2 62.8 %copy-start.3 = (bf16[1,256,1024]{2,1,0:T(8,128)(2,1)S(1)}, bf16[1,256,1024]{2,1,0:T(8,128)(2,1)}, u32[]{:S(2)}) copy-start(bf16[1,256,1024]{2,1,0:T(8,128)(2,1)} %param.23) | copy-start | bytes 1572868
  7.2 62.8 %copy-start.41 = (f32[1024]{0:T(1024)S(1)}, f32[1024]{0:T(1024)}, u32[]{:S(2)}) copy-start(f32[1024]{0:T(1024)} %param.27) | copy-start | bytes 12292
  7.2 10.1 copy-start.39
  7.2 14.4 copy-start.49
  7.2 97.5 %all-gather.4.cloned.1.call-start = ((), (), s32[]{:S(2)}) async-start(), calls=%async_computation.6 | async-start | bytes 4456448 | tf_op jit(solution)/shard_map/all_gather | solution.py:98
  9.3 63.1 %copy-start.46 = (f32[256]{0:T(256)}, f32[256]{0:T(256)S(1)}, u32[]{:S(2)}) copy-start(f32[256]{0:T(256)S(1)} %get-tuple-element.648) | copy-start | bytes 3076
  13.8 59.0 %copy-start.26 = (f32[256,64]{0,1:T(8,128)}, f32[256,64]{0,1:T(8,128)S(1)}, u32[]{:S(2)}) copy-start(f32[256,64]{0,1:T(8,128)S(1)} %get-tuple-element.656) | copy-start | bytes 196612
  13.8 59.0 %copy-start.28 = (f32[256,64]{0,1:T(8,128)}, f32[256,64]{0,1:T(8,128)S(1)}, u32[]{:S(2)}) copy-start(f32[256,64]{0,1:T(8,128)S(1)} %get-tuple-element.655) | copy-start | bytes 196612
  14.6 167.8 %all-gather.6.cloned.1.call-start = ((), (), s32[]{:S(2)}) async-start(), calls=%async_computation.7 | async-start | bytes 4456448 | tf_op jit(solution)/shard_map/all_gather | solution.py:99
  204.5 24.8 %copy-start.45 = (f32[1024]{0:T(1024)S(1)}, f32[1024]{0:T(1024)}, u32[]{:S(2)}) copy-start(f32[1024]{0:T(1024)} %param.32) | copy-start | bytes 12292
  206.9 4.6 copy-start.10
  224.7 8.6 copy-start.1
  226.3 7.0 copy-start.17
  229.5 260.2 %copy-start.19 = (bf16[256,1024]{1,0:T(8,128)(2,1)}, bf16[256,1024]{1,0:T(8,128)(2,1)S(1)}, u32[]{:S(2)}) copy-start(bf16[256,1024]{1,0:T(8,128)(2,1)S(1)} %multiply_convert_fusion) | copy-start | bytes 1572868
  233.3 256.3 %copy-start.54 = (bf16[1,1024,512]{2,1,0:T(8,128)(2,1)S(1)}, bf16[1,1024,512]{2,1,0:T(8,128)(2,1)}, u32[]{:S(2)}) copy-start(bf16[1,1024,512]{2,1,0:T(8,128)(2,1)} %param.35) | copy-start | bytes 3145732
  489.6 4.6 copy-start.13
  489.6 4.6 copy-start.52
  494.2 4.6 copy-start.15
  498.8 3.3 copy-start.16
  498.8 5.2 copy-start.50
  510.7 5.6 copy-start.43
  510.7 5.9 copy-start.30
  510.7 7.0 copy-start.20
  510.7 7.0 copy-start.40
  510.7 157.5 %all-to-all-start.1 = ((bf16[16,256,1024]{2,1,0:T(8,128)(2,1)}), bf16[16,256,1024]{2,1,0:T(8,128)(2,1)}, u32[]{:S(2)}, u32[]{:S(2)}) async-start(bf16[16,256,1024]{2,1,0:T(8,128)(2,1)} %convolution_convert_fusion.1), calls=%async_computation.1 | async-start | bytes 16777216 | tf_op jit(solution)/shard_map/all_to_all | solution.py:179
  683.6 5.9 copy-start.25
  704.9 220.1 %copy-start.51 = (bf16[1,512,1024]{2,1,0:T(8,128)(2,1)S(1)}, bf16[1,512,1024]{2,1,0:T(8,128)(2,1)}, u32[]{:S(2)}) copy-start(bf16[1,512,1024]{2,1,0:T(8,128)(2,1)} %param.36) | copy-start | bytes 3145732
  924.9 15.8 copy-start.14
  924.9 15.8 copy-start.53
  940.8 10.5 copy-start.55
  962.8 155.9 %copy-start.36 = (pred[256,4096]{1,0:T(8,128)(4,1)S(1)}, pred[256,4096]{1,0:T(8,128)(4,1)}, u32[]{:S(2)}) copy-start(pred[256,4096]{1,0:T(8,128)(4,1)} %fusion.46) | copy-start | bytes 3145732
  962.8 155.9 %all-to-all-start.3 = ((bf16[16,256,1024]{2,1,0:T(8,128)(2,1)}), bf16[16,256,1024]{2,1,0:T(8,128)(2,1)}, u32[]{:S(2)}, u32[]{:S(2)}) async-start(bf16[16,256,1024]{2,1,0:T(8,128)(2,1)} %add_convert_fusion), calls=%async_computation.3 | async-start | bytes 16777216 | tf_op jit(solution)/shard_map/all_to_all | solution.py:209
  967.7 464.5 %reduce-scatter.3.cloned.1.call-start = ((), (), s32[]{:S(2)}) async-start(), calls=%async_computation.8 | async-start | bytes 4456448 | tf_op jit(solution)/shard_map/reduce_scatter | solution.py:259
  1118.7 5.9 copy-start.9
  1118.7 6.5 copy-start.31
  1118.7 6.5 copy-start.37
  1126.4 5.1 copy-start.6
  1132.9 3.5 copy-start.32
  1218.2 310.9 %reduce-scatter.5.cloned.1.call-start = ((), (), s32[]{:S(2)}) async-start(), calls=%async_computation.9 | async-start | bytes 4456448 | tf_op jit(solution)/shard_map/reduce_scatter | solution.py:265
  1218.8 336.3 %all-reduce.8.cloned.1.call-start = ((), (), s32[]{:S(2)}) async-start(), calls=%async_computation.11 | async-start | bytes 6291456 | tf_op jit(solution)/shard_map/psum | solution.py:289
  1219.0 10.3 copy-start.57
  1219.0 18.5 %slice-start = ((s8[8388608]{0:T(1024)(128)(4,1)}), s8[4194304]{0:T(1024)(128)(4,1)S(1)}, s32[]{:S(2)}) async-start(s8[8388608]{0:T(1024)(128)(4,1)} %bitcast.401), calls=%async_computation.12 | async-start | bytes 8388608
  1229.3 8.2 slice-start.1
  1229.3 8.2 copy-start.56
  1237.5 5.8 copy-start.29
  1237.5 10.8 copy-start.27
  1243.0 6.7 copy-start.42
  1243.0 6.7 copy-start.47
  1243.1 559.6 %all-reduce.6.cloned.1.call-start = ((), (), s32[]{:S(2)}) async-start(), calls=%async_computation.10 | async-start | bytes 25296896 | tf_op jit(solution)/shard_map/psum | solution.py:285
  1246.2 3.5 copy-start.4
  1246.2 6.4 copy-start.7
  1246.3 6.4 copy-start.18
  1555.0 8.8 copy-start.24
  1555.0 9.0 copy-start.12
  1555.0 9.7 copy-start.23
  1558.0 7.2 copy-start.5
  1558.0 7.2 copy-start.35
  1558.0 7.3 copy-start.38
  1561.0 47.3 %copy-start.48 = (f32[256]{0:T(256)S(1)}, f32[256]{0:T(256)}, u32[]{:S(2)}) copy-start(f32[256]{0:T(256)} %get-tuple-element.647) | copy-start | bytes 3076
  1802.6 5.1 copy-start.34
  1802.6 6.4 copy-start.33
  1802.6 7.7 copy-start.22
  1807.7 4.7 copy-start.44
  (4 other events, 5.8 us)
Sparse Core Ops, SparseCore 0:
  14.7 89.9 all-gather.3
  108.1 74.3 all-gather.5
  1218.3 213.8 reduce-scatter.2
  1434.3 94.7 reduce-scatter.4
  1532.0 22.9 all-reduce.7
  1563.0 239.5 all-reduce.5
where the time goes:
time: 1830 us; the launch traced here: 1820 us
  waiting for transfers between devices  857 us (47%)
  blocking collectives  561 us (31%)
  local copies, waits for them, and re-layouts  149 us (8%)
  matrix products  143 us (8%)
  other arithmetic  72.2 us (4%)
    all_to_all x1, blocking collectives, per_device(): lax.all_to_all(outgoing.reshape(experts, cap, D), 'blk', split_axis=0, co...  256 us
    all_to_all x1, blocking collectives, per_device(): lax.all_to_all(grad_slots.reshape(experts, cap, D), 'blk', split_axis=0,...  220 us
    psum x1, waiting for transfers between devices, per_device(): lax.psum((d_gain1, d_query, d_key, d_value, d_out_w, d_gain2, d_router),...  192 us
    reduce_scatter x1, waiting for transfers between devices, per_device(): lax.psum_scatter(gk_blocks.reshape(length, KV * HD).astype(jnp.bfloat16),...  177 us
    all_to_all x1, waiting for transfers between devices, per_device(): lax.all_to_all(expert_out.reshape(experts, cap, D), 'blk', split_axis=0,...  150 us
    all_to_all x1, waiting for transfers between devices, per_device(): lax.all_to_all(grad_in.reshape(experts, cap, D), 'blk', split_axis=0, con...  146 us
    reduce_scatter x1, waiting for transfers between devices, per_device(): lax.psum_scatter(gv_blocks.reshape(length, KV * HD).astype(jnp.bfloat16),...  86.7 us
    all_gather x1, waiting for transfers between devices, per_device(): lax.all_gather(value, 'blk', axis=0, tiled=True)  69.8 us
  transfers between devices with their start and end apart: 8, of which 8 were waited for; matrix products, arithmetic and copies ran while one was open for 6% of the time, Pallas kernels for 0%

commit v1 on v0

--- a/solution.py
+++ b/solution.py
@@ -1,19 +1,510 @@
+import functools
 import math
 
 import jax
 import jax.numpy as jnp
+import numpy as np
 from jax import lax
+from jax.experimental import pallas as pl
+from jax.experimental.pallas import tpu as pltpu
 from jax.sharding import PartitionSpec as P
 
-D = 1024
 H = 16
 KV = 8
 HD = 64
 TOP = 8
-
-
 EPS = 1e-06
 NEG = -1e30
+F32 = jnp.float32
+BF16 = jnp.bfloat16
+MESH = pl.DeviceIdType.MESH
+VMEM_LIMIT = 60 * 2**20
+NT = (((1,), (1,)), ((), ()))
+TN = (((0,), (0,)), ((), ()))
+
+
+def mm(a, b, dims=(((1,), (0,)), ((), ()))):
+    return lax.dot_general(a, b, dims, preferred_element_type=F32)
+
+
+def remote(src, dst, send, recv, seq, blk):
+    return pltpu.make_async_remote_copy(
+        src_ref=src,
+        dst_ref=dst,
+        send_sem=send,
+        recv_sem=recv,
+        device_id=(seq, blk),
+        device_id_type=MESH,
+    )
+
+
+def greet_all(seqs, blocks, me_s, me_b):
+    barrier = pltpu.get_barrier_semaphore()
+    total = seqs * blocks
+
+    def hello(n, carry):
+        other = lax.rem(me_s * blocks + me_b + n, total)
+        pl.semaphore_signal(
+            barrier,
+            inc=1,
+            device_id=(other // blocks, lax.rem(other, blocks)),
+            device_id_type=MESH,
+        )
+        return carry
+
+    lax.fori_loop(1, total, hello, 0)
+    pl.semaphore_wait(barrier, total - 1)
+
+
+def rotate_pairs(u):
+    lanes = u.shape[-1]
+    half = HD // 2
+    lane = lax.broadcasted_iota(jnp.int32, u.shape, u.ndim - 1)
+    ahead = pltpu.roll(u, lanes - half, u.ndim - 1)
+    behind = pltpu.roll(u, half, u.ndim - 1)
+    return jnp.where(lane % HD < half, -ahead, behind)
+
+
+def stacked_heads(wide):
+    return jnp.concatenate([wide[:HD], wide[HD:]], axis=1)
+
+
+def attention_forward_kernel(
+    blocks,
+    pay,
+    o_ref,
+    kv_ref,
+    kvt_ref,
+    q_ref,
+    ot_ref,
+    stat_ref,
+    in_ref,
+    other_ref,
+    obuf,
+    cnt,
+    send_sem,
+    recv_sem,
+    fsend_sem,
+    frecv_sem,
+    osend_sem,
+    orecv_sem,
+):
+    me_s = lax.axis_index("seq")
+    me_b = lax.axis_index("blk")
+    tok = q_ref.shape[1]
+    steps = blocks // 2
+    sigma = me_b // KV
+    kappa = lax.rem(me_b, KV)
+    greet_all(2, blocks, me_s, me_b)
+
+    dest_core = lax.rem(me_b, 2)
+    slot = me_b // 2
+
+    def payload(n):
+        k = lax.rem(me_b + n, KV)
+        chip = me_s * KV + k
+        mine = (dest_core == me_s) & (chip == me_b)
+        return k, chip, mine
+
+    def send_payload(n, carry):
+        k, chip, mine = payload(n)
+
+        @pl.when(mine)
+        def _():
+            pltpu.make_async_copy(pay.at[k], in_ref.at[slot], recv_sem.at[slot]).start()
+
+        @pl.when(jnp.logical_not(mine))
+        def _():
+            remote(
+                pay.at[k], in_ref.at[slot], send_sem.at[k], recv_sem.at[slot], dest_core, chip
+            ).start()
+
+        return carry
+
+    lax.fori_loop(0, KV, send_payload, 0)
+
+    def arrival(t):
+        return pltpu.make_async_copy(pay.at[0], in_ref.at[t], recv_sem.at[t])
+
+    def forward(t):
+        return remote(
+            in_ref.at[t, :, pl.ds(2 * HD, 2 * HD)],
+            other_ref.at[t],
+            fsend_sem.at[t],
+            frecv_sem.at[t],
+            1 - me_s,
+            me_b,
+        )
+
+    arrival(0).wait()
+    forward(0).start()
+    cnt[...] = jnp.zeros_like(cnt)
+    first_core = me_s == 0
+    lane = lax.broadcasted_iota(jnp.int32, (1, 2 * tok), 1)
+    qrow = jnp.where(lane < tok, lane, lane - tok)
+    wide = 2 * tok
+
+    def step(t, carry):
+        @pl.when(t < steps - 1)
+        def _():
+            arrival(t + 1).wait()
+            forward(t + 1).start()
+
+        forward(t).wait_recv()
+        mine = in_ref[t]
+        kv_mine, seg_mine = mine[:tok, 2 * HD :], mine[tok:, 2 * HD :].astype(F32)
+        other = other_ref[t]
+        kv_other, seg_other = other[:tok], other[tok:].astype(F32)
+        pair = jnp.where(
+            first_core,
+            jnp.concatenate([kv_mine, kv_other], 0).astype(F32),
+            jnp.concatenate([kv_other, kv_mine], 0).astype(F32),
+        )
+        kv_ref[t] = pair.astype(BF16)
+        kvt_ref[t] = jnp.transpose(pair).astype(BF16)
+        number = lax.broadcasted_iota(jnp.int32, (8, tok), 0).astype(F32)
+        seg_q = jnp.concatenate([seg_mine[0:1], seg_mine[1:2]], 1)
+        seg_o = jnp.concatenate([seg_other[0:1], seg_other[1:2]], 1)
+        below = (seg_q < number).astype(F32) + (seg_o < number).astype(F32)
+        cnt[...] += jnp.sum(below, 1, keepdims=True)
+        start_q = jnp.sum(jnp.where(seg_q == number, cnt[:, :1], 0.0), 0, keepdims=True)
+        start = jnp.concatenate([start_q, start_q], 1).astype(jnp.int32)
+        q_two = mine[:tok, : 2 * HD]
+        q_ref[t] = q_two
+        qt = stacked_heads(jnp.transpose(q_two.astype(F32)))
+        qm = jnp.concatenate([qt, jnp.zeros_like(qt)], 0).astype(BF16)
+        qpos = (2 * t + me_s) * tok + qrow
+
+        def piece(u, state, last):
+            running, total, acc = state
+            score = mm(kv_ref[u], qm)
+            kpos = u * wide + lax.broadcasted_iota(jnp.int32, score.shape, 0)
+            mask = kpos >= start
+            if last:
+                mask &= kpos <= qpos
+            score = jnp.where(mask, score, NEG)
+            newmax = jnp.maximum(running, jnp.max(score, 0, keepdims=True))
+            expo = jnp.exp(score - newmax)
+            factor = jnp.exp(running - newmax)
+            total = total * factor + jnp.sum(expo, 0, keepdims=True)
+            acc = acc * factor + mm(kvt_ref[u, HD:, :], expo.astype(BF16))
+            return newmax, total, acc
+
+        state = (
+            jnp.full((1, wide), NEG, F32),
+            jnp.zeros((1, wide), F32),
+            jnp.zeros((HD, wide), F32),
+        )
+        state = lax.fori_loop(0, t, lambda u, s: piece(u, s, False), state)
+        running, total, acc = piece(t, state, True)
+        out_t = acc / total
+        ot_ref[t] = out_t
+        rows = lax.broadcasted_iota(jnp.int32, (8, wide), 0)
+        lse = running + jnp.log(total)
+        stat_ref[t] = jnp.where(rows == 0, lse, start.astype(F32))
+        upright = jnp.concatenate([out_t[:, :tok], out_t[:, tok:]], 0)
+        obuf[t] = jnp.transpose(upright).astype(BF16)
+        owner = 2 * t + me_s
+        home = (sigma == me_s) & (owner == me_b)
+        place = o_ref.at[:, pl.ds(pl.multiple_of(kappa * 2 * HD, 2 * HD), 2 * HD)]
+
+        @pl.when(home)
+        def _():
+            pltpu.make_async_copy(obuf.at[t], place, orecv_sem.at[kappa]).start()
+
+        @pl.when(jnp.logical_not(home))
+        def _():
+            remote(obuf.at[t], place, osend_sem.at[t], orecv_sem.at[kappa], sigma, owner).start()
+
+        return carry
+
+    lax.fori_loop(0, steps, step, 0)
+
+    def finish(t, carry):
+        k, chip, mine = payload(t)
+
+        @pl.when(jnp.logical_not(mine))
+        def _():
+            remote(
+                pay.at[k], in_ref.at[slot], send_sem.at[k], recv_sem.at[slot], dest_core, chip
+            ).wait_send()
+
+        return carry
+
+    lax.fori_loop(0, KV, finish, 0)
+
+    def finish_steps(t, carry):
+        forward(t).wait_send()
+        owner = 2 * t + me_s
+        home = (sigma == me_s) & (owner == me_b)
+
+        @pl.when(jnp.logical_not(home))
+        def _():
+            remote(
+                obuf.at[t],
+                o_ref.at[:, pl.ds(0, 2 * HD)],
+                osend_sem.at[t],
+                orecv_sem.at[0],
+                sigma,
+                owner,
+            ).wait_send()
+
+        return carry
+
+    lax.fori_loop(0, steps, finish_steps, 0)
+
+    def gather(k, carry):
+        pltpu.make_async_copy(
+            obuf.at[0],
+            o_ref.at[:, pl.ds(pl.multiple_of(k * 2 * HD, 2 * HD), 2 * HD)],
+            orecv_sem.at[k],
+        ).wait()
+        return carry
+
+    lax.fori_loop(0, KV, gather, 0)
+
+
+def attention_forward(blocks, pay):
+    tok = pay.shape[2]
+    steps = blocks // 2
+    vm = pl.BlockSpec(memory_space=pltpu.VMEM)
+    dma = pltpu.SemaphoreType.DMA
+    return pl.pallas_call(
+        functools.partial(attention_forward_kernel, blocks),
+        out_shape=(
+            jax.ShapeDtypeStruct((tok, H * HD), BF16),
+            jax.ShapeDtypeStruct((steps, 2 * tok, 2 * HD), BF16),
+            jax.ShapeDtypeStruct((steps, 2 * HD, 2 * tok), BF16),
+            jax.ShapeDtypeStruct((steps, tok, 2 * HD), BF16),
+            jax.ShapeDtypeStruct((steps, HD, 2 * tok), F32),
+            jax.ShapeDtypeStruct((steps, 8, 2 * tok), F32),
+        ),
+        in_specs=[vm],
+        out_specs=(vm,) * 6,
+        scratch_shapes=[
+            pltpu.VMEM((steps, tok + 16, 4 * HD), BF16),
+            pltpu.VMEM((steps, tok + 16, 2 * HD), BF16),
+            pltpu.VMEM((steps, tok, 2 * HD), BF16),
+            pltpu.VMEM((8, 128), F32),
+            dma((KV,)),
+            dma((steps,)),
+            dma((steps,)),
+            dma((steps,)),
+            dma((steps,)),
+            dma((KV,)),
+        ],
+        compiler_params=pltpu.CompilerParams(
+            collective_id=0, has_side_effects=True, vmem_limit_bytes=VMEM_LIMIT
+        ),
+        name="attention_forward",
+    )(pay)
+
+
+def attention_backward_kernel(
+    blocks,
+    do_ref,
+    kv_ref,
+    kvt_ref,
+    q_ref,
+    ot_ref,
+    stat_ref,
+    cos_ref,
+    sin_ref,
+    out_ref,
+    in_ref,
+    dkv,
+    part,
+    xch,
+    done,
+    send_sem,
+    recv_sem,
+    xsend_sem,
+    xrecv_sem,
+    osend_sem,
+    orecv_sem,
+):
+    me_s = lax.axis_index("seq")
+    me_b = lax.axis_index("blk")
+    tok = q_ref.shape[1]
+    steps = blocks // 2
+    sigma = me_b // KV
+    kappa = lax.rem(me_b, KV)
+    greet_all(2, blocks, me_s, me_b)
+
+    dest_core = lax.rem(me_b, 2)
+    slot = me_b // 2
+
+    def outgoing(n):
+        k = lax.rem(me_b + n, KV)
+        chip = me_s * KV + k
+        mine = (dest_core == me_s) & (chip == me_b)
+        src = do_ref.at[:, pl.ds(pl.multiple_of(k * 2 * HD, 2 * HD), 2 * HD)]
+        return k, chip, mine, src
+
+    def send_grad(n, carry):
+        k, chip, mine, src = outgoing(n)
+
+        @pl.when(mine)
+        def _():
+            pltpu.make_async_copy(src, in_ref.at[slot], recv_sem.at[slot]).start()
+
+        @pl.when(jnp.logical_not(mine))
+        def _():
+            remote(src, in_ref.at[slot], send_sem.at[k], recv_sem.at[slot], dest_core, chip).start()
+
+        return carry
+
+    lax.fori_loop(0, KV, send_grad, 0)
+    dkv[...] = jnp.zeros_like(dkv)
+    wide = 2 * tok
+    lane = lax.broadcasted_iota(jnp.int32, (1, wide), 1)
+    qrow = jnp.where(lane < tok, lane, lane - tok)
+    low = lax.broadcasted_iota(jnp.int32, (tok, 2 * HD), 1) < HD
+
+    def swap(t):
+        return remote(part.at[t], xch.at[t], xsend_sem.at[t], xrecv_sem.at[t], 1 - me_s, me_b)
+
+    def deliver(t, act):
+        owner = 2 * t + me_s
+        home = (sigma == me_s) & (owner == me_b)
+        src, dst = done.at[t], out_ref.at[kappa]
+
+        @pl.when(home)
+        def _():
+            if act == "start":
+                pltpu.make_async_copy(src, dst, orecv_sem.at[kappa]).start()
+
+        @pl.when(jnp.logical_not(home))
+        def _():
+            copy = remote(src, dst, osend_sem.at[t], orecv_sem.at[kappa], sigma, owner)
+            copy.start() if act == "start" else copy.wait_send()
+
+    def finalize(t):
+        swap(t).wait_recv()
+        place = pl.ds(pl.multiple_of(me_s * tok, tok), tok)
+        total = dkv[t, place, :] + xch[t]
+        owner = 2 * t + me_s
+        cosine = jnp.where(low, cos_ref[owner], 1.0)
+        sine = jnp.where(low, sin_ref[owner], 0.0)
+        back = total * cosine - rotate_pairs(total) * sine
+        done[t, :, pl.ds(2 * HD, 2 * HD)] = back.astype(BF16)
+        deliver(t, "start")
+
+    def step(n, carry):
+        t = steps - 1 - n
+        pltpu.make_async_copy(do_ref.at[:, pl.ds(0, 2 * HD)], in_ref.at[t], recv_sem.at[t]).wait()
+        d_two = in_ref[t].astype(F32)
+        q_two = q_ref[t].astype(F32)
+        dt = stacked_heads(jnp.transpose(d_two))
+        qt = stacked_heads(jnp.transpose(q_two))
+        zero = jnp.zeros_like(dt)
+        dm = jnp.concatenate([zero, dt], 0).astype(BF16)
+        qm = jnp.concatenate([qt, zero], 0).astype(BF16)
+        delta = jnp.sum(ot_ref[t] * dt, 0, keepdims=True)
+        right = jnp.concatenate(
+            [
+                jnp.where(low, q_two, 0.0),
+                jnp.where(low, pltpu.roll(q_two, HD, 1), 0.0),
+                jnp.where(low, 0.0, pltpu.roll(d_two, HD, 1)),
+                jnp.where(low, 0.0, d_two),
+            ],
+            0,
+        ).astype(BF16)
+        stat = stat_ref[t]
+        lse, start = stat[0:1], stat[1:2].astype(jnp.int32)
+        qpos = (2 * t + me_s) * tok + qrow
+
+        def piece(u, dq, last):
+            keys = kv_ref[u]
+            score = mm(keys, qm)
+            kpos = u * wide + lax.broadcasted_iota(jnp.int32, score.shape, 0)
+            mask = kpos >= start
+            if last:
+                mask &= kpos <= qpos
+            prob = jnp.where(mask, jnp.exp(score - lse), 0.0)
+            dprob = mm(keys, dm)
+            dscore = (prob * (dprob - delta)).astype(BF16)
+            both = jnp.concatenate([dscore, prob.astype(BF16)], 1)
+            dkv[u] += mm(both, right)
+            return dq + mm(kvt_ref[u, :HD, :], dscore)
+
+        dq = jnp.zeros((HD, wide), F32)
+        dq = lax.fori_loop(0, t, lambda u, s: piece(u, s, False), dq)
+        dq = piece(t, dq, True) * HD ** (-0.5)
+        upright = jnp.transpose(jnp.concatenate([dq[:, :tok], dq[:, tok:]], 0))
+        owner = 2 * t + me_s
+        back = upright * cos_ref[owner] - rotate_pairs(upright) * sin_ref[owner]
+        done[t, :, pl.ds(0, 2 * HD)] = back.astype(BF16)
+        part[t] = dkv[t, pl.ds(pl.multiple_of((1 - me_s) * tok, tok), tok), :]
+        swap(t).start()
+
+        @pl.when(n > 0)
+        def _():
+            finalize(t + 1)
+
+        return carry
+
+    lax.fori_loop(0, steps, step, 0)
+    finalize(0)
+
+    def finish(n, carry):
+        k, chip, mine, src = outgoing(n)
+
+        @pl.when(jnp.logical_not(mine))
+        def _():
+            remote(
+                src, in_ref.at[slot], send_sem.at[k], recv_sem.at[slot], dest_core, chip
+            ).wait_send()
+
+        return carry
+
+    lax.fori_loop(0, KV, finish, 0)
+
+    def finish_steps(t, carry):
+        swap(t).wait_send()
+        deliver(t, "wait")
+        return carry
+
+    lax.fori_loop(0, steps, finish_steps, 0)
+
+    def gather(k, carry):
+        pltpu.make_async_copy(done.at[0], out_ref.at[k], orecv_sem.at[k]).wait()
+        return carry
+
+    lax.fori_loop(0, KV, gather, 0)
+
+
+def attention_backward(blocks, d_o, kv, kvt, q_two, out_t, stat, cos_all, sin_all):
+    tok = q_two.shape[1]
+    steps = blocks // 2
+    vm = pl.BlockSpec(memory_space=pltpu.VMEM)
+    dma = pltpu.SemaphoreType.DMA
+    return pl.pallas_call(
+        functools.partial(attention_backward_kernel, blocks),
+        out_shape=jax.ShapeDtypeStruct((KV, tok, 4 * HD), BF16),
+        in_specs=[vm] * 8,
+        out_specs=vm,
+        scratch_shapes=[
+            pltpu.VMEM((steps, tok, 2 * HD), BF16),
+            pltpu.VMEM((steps, 2 * tok, 2 * HD), F32),
+            pltpu.VMEM((steps, tok, 2 * HD), F32),
+            pltpu.VMEM((steps, tok, 2 * HD), F32),
+            pltpu.VMEM((steps, tok, 4 * HD), BF16),
+            dma((KV,)),
+            dma((steps,)),
+            dma((steps,)),
+            dma((steps,)),
+            dma((steps,)),
+            dma((KV,)),
+        ],
+        compiler_params=pltpu.CompilerParams(
+            collective_id=1, has_side_effects=True, vmem_limit_bytes=VMEM_LIMIT
+        ),
+        name="attention_backward",
+    )(d_o, kv, kvt, q_two, out_t, stat, cos_all, sin_all)
+
+
+D = 1024
 HIGH = lax.Precision.HIGHEST
 
 
@@ -57,7 +548,7 @@
     )
 
 
-def per_device(
+def per_device_plain(
     tokens,
     segments,
     routes,
@@ -153,12 +644,11 @@
     gates = jax.nn.softmax(chosen, -1)
     combine = (rweight * gates).astype(bf16)
     cap = min(tok, 2 * tok * TOP // experts)
-    flat_route = route.reshape(-1)
-    onehot = (flat_route[:, None] == jnp.arange(experts, dtype=jnp.int32)[None, :]).astype(
-        jnp.int32
-    )
-    rank = jnp.sum((jnp.cumsum(onehot, 0) - onehot) * onehot, -1)
-    slots = (flat_route * cap + rank).reshape(tok, TOP)
+    member = jnp.sum(chooser, 1)
+    before = jnp.asarray(np.tril(np.ones((tok, tok), np.float32), -1))
+    order = jnp.dot(before, member, precision=HIGH)
+    rank = jnp.sum(chooser * order[:, None, :], -1).astype(jnp.int32)
+    slots = route * cap + rank
     placed = jnp.any(
         slots[:, :, None] == jnp.arange(experts * cap, dtype=jnp.int32)[None, None, :], 1
     ).astype(bf16)
@@ -306,9 +796,190 @@
     )
 
 
+def by_head(w_query, w_key, w_value):
+    d = w_query.shape[0]
+    return jnp.concatenate(
+        [w_query.reshape(d, KV, 2 * HD), w_key.reshape(d, KV, HD), w_value.reshape(d, KV, HD)], -1
+    ).reshape(d, KV * 4 * HD)
+
+
+def tables(length):
+    half = HD // 2
+    freq = np.exp(-math.log(10000.0) * np.arange(half, dtype=np.float32) * 2.0 / HD).astype(np.float32)
+    angle = np.arange(length, dtype=np.float32)[:, None] * freq[None, :]
+    return np.tile(np.cos(angle), (1, 4)), np.tile(np.sin(angle), (1, 4))
+
+
+def per_device(
+    tokens,
+    segments,
+    routes,
+    route_weight,
+    norm1_gain,
+    w_query,
+    w_key,
+    w_value,
+    w_out,
+    norm2_gain,
+    w_router,
+    w_gate,
+    w_up,
+    w_down,
+    cotangent,
+):
+    f32 = jnp.float32
+    bf16 = jnp.bfloat16
+    scale = HD ** (-0.5)
+    xs = tokens[0].astype(f32)
+    tok = xs.shape[0]
+    blocks = lax.axis_size("blk")
+    length = tok * blocks
+    cos_np, sin_np = tables(length)
+    cos_all = jnp.asarray(cos_np.reshape(blocks, tok, 2 * HD))
+    sin_all = jnp.asarray(sin_np.reshape(blocks, tok, 2 * HD))
+    me = lax.axis_index("blk")
+    cosine = lax.dynamic_index_in_dim(cos_all, me, 0, keepdims=False)[:, None, :]
+    sine = lax.dynamic_index_in_dim(sin_all, me, 0, keepdims=False)[:, None, :]
+    scale1 = rms_scale(xs)
+    xa = (xs * scale1 * norm1_gain).astype(bf16)
+    w_all = by_head(w_query, w_key, w_value)
+    qkv = jnp.dot(xa, w_all, preferred_element_type=f32).reshape(tok, KV, 4 * HD)
+
+    def turned(u):
+        parts = u.reshape(tok, KV, -1, HD)
+        return (
+            parts * cosine[:, :, None, :HD] + rotate_half(parts) * sine[:, :, None, :HD]
+        ).reshape(u.shape)
+
+    pay = jnp.concatenate(
+        [turned(qkv[..., : 2 * HD]) * scale, turned(qkv[..., 2 * HD : 3 * HD]), qkv[..., 3 * HD :]], -1
+    ).astype(bf16)
+    seg = jnp.zeros((16, 4 * HD), bf16).at[:2, 2 * HD :].set(
+        segments[0].astype(bf16).reshape(2, tok // 2)
+    )
+    pay = jnp.concatenate(
+        [pay.transpose(1, 0, 2), jnp.broadcast_to(seg[None], (KV, 16, 4 * HD))], 1
+    )
+    att_low, *kept = attention_forward(blocks, pay)
+    h1 = xs + jnp.dot(att_low, w_out, preferred_element_type=f32)
+    scale2 = rms_scale(h1)
+    xl = (h1 * scale2 * norm2_gain).astype(bf16)
+    logits = jnp.dot(xl, w_router, preferred_element_type=f32)
+    experts = logits.shape[1]
+    route = routes[0]
+    rweight = route_weight[0]
+    chooser = (route[:, :, None] == jnp.arange(experts, dtype=jnp.int32)[None, None, :]).astype(f32)
+    chosen = jnp.sum(chooser * logits[:, None, :], -1)
+    gates = jax.nn.softmax(chosen, -1)
+    combine = (rweight * gates).astype(bf16)
+    cap = min(tok, 2 * tok * TOP // experts)
+    member = jnp.sum(chooser, 1)
+    before = jnp.asarray(np.tril(np.ones((tok, tok), np.float32), -1))
+    order = jnp.dot(before, member, precision=HIGH)
+    rank = jnp.sum(chooser * order[:, None, :], -1).astype(jnp.int32)
+    slots = route * cap + rank
+    placed = jnp.any(
+        slots[:, :, None] == jnp.arange(experts * cap, dtype=jnp.int32)[None, None, :], 1
+    ).astype(bf16)
+    outgoing = jnp.einsum("ts,td->sd", placed, xl, preferred_element_type=f32).astype(bf16)
+    incoming = lax.all_to_all(
+        outgoing.reshape(experts, cap, D), "blk", split_axis=0, concat_axis=0, tiled=True
+    )
+    local_exp = w_gate.shape[0]
+    incoming = incoming.reshape(blocks, local_exp, cap, D)
+    gate_pre = jnp.einsum("necd,edf->necf", incoming, w_gate, preferred_element_type=f32)
+    up_pre = jnp.einsum("necd,edf->necf", incoming, w_up, preferred_element_type=f32)
+    sigma = jax.nn.sigmoid(gate_pre)
+    activated = gate_pre * sigma
+    hidden = (activated * up_pre).astype(bf16)
+    expert_out = jnp.einsum("necf,efd->necd", hidden, w_down, preferred_element_type=f32).astype(
+        bf16
+    )
+    returned = lax.all_to_all(
+        expert_out.reshape(experts, cap, D), "blk", split_axis=0, concat_axis=0, tiled=True
+    )
+    per_route = jnp.take(returned.reshape(experts * cap, D), slots.reshape(-1), axis=0).reshape(
+        tok, TOP, D
+    )
+    mixture = jnp.einsum("tj,tjd->td", combine, per_route, preferred_element_type=f32)
+    result = h1 + mixture
+    grad_out = cotangent[0].astype(f32)
+    grad_combine = jnp.einsum("td,tjd->tj", grad_out, per_route.astype(f32), precision=HIGH)
+    route_grads = (combine.astype(f32)[:, :, None] * grad_out[:, None, :]).astype(bf16)
+    grad_slots = (
+        jnp.zeros((experts * cap, D), bf16)
+        .at[slots.reshape(-1)]
+        .set(route_grads.reshape(tok * TOP, D))
+    )
+    grad_incoming = lax.all_to_all(
+        grad_slots.reshape(experts, cap, D), "blk", split_axis=0, concat_axis=0, tiled=True
+    )
+    grad_incoming = grad_incoming.reshape(blocks, local_exp, cap, D)
+    grad_hidden = jnp.einsum("necd,efd->necf", grad_incoming, w_down, preferred_element_type=f32)
+    grad_gate = (grad_hidden * up_pre * sigma * (1.0 + gate_pre * (1.0 - sigma))).astype(bf16)
+    grad_up = (grad_hidden * activated).astype(bf16)
+    d_down = jnp.einsum("necf,necd->efd", hidden, grad_incoming, preferred_element_type=f32)
+    d_gate_w = jnp.einsum("necd,necf->edf", incoming, grad_gate, preferred_element_type=f32)
+    d_up_w = jnp.einsum("necd,necf->edf", incoming, grad_up, preferred_element_type=f32)
+    grad_in = (
+        jnp.einsum("necf,edf->necd", grad_gate, w_gate, preferred_element_type=f32)
+        + jnp.einsum("necf,edf->necd", grad_up, w_up, preferred_element_type=f32)
+    ).astype(bf16)
+    grad_back = lax.all_to_all(
+        grad_in.reshape(experts, cap, D), "blk", split_axis=0, concat_axis=0, tiled=True
+    )
+    grad_xl = jnp.einsum(
+        "ts,sd->td", placed, grad_back.reshape(experts * cap, D), preferred_element_type=f32
+    )
+    grad_gates = rweight * grad_combine
+    grad_chosen = gates * (grad_gates - jnp.sum(gates * grad_gates, -1, keepdims=True))
+    grad_logits = jnp.sum(chooser * grad_chosen[:, :, None], 1).astype(bf16)
+    d_router = jnp.einsum("td,te->de", xl, grad_logits, preferred_element_type=f32)
+    grad_xl = grad_xl + jnp.einsum("te,de->td", grad_logits, w_router, preferred_element_type=f32)
+    grad_h1_norm, d_gain2 = rms_back(h1, scale2, norm2_gain, grad_xl)
+    grad_h1 = grad_out + grad_h1_norm
+    grad_att = grad_h1.astype(bf16)
+    d_out_w = jnp.einsum("ti,td->id", att_low, grad_att, preferred_element_type=f32)
+    grad_o = jnp.einsum("td,id->ti", grad_att, w_out, preferred_element_type=f32).astype(bf16)
+    got = attention_backward(blocks, grad_o, *kept, cos_all, sin_all)
+    grad_all = got.transpose(1, 0, 2).reshape(tok, KV * 4 * HD)
+    d_all = jnp.einsum("td,te->de", xa, grad_all, preferred_element_type=f32)
+    grad_xa = jnp.einsum("te,de->td", grad_all, w_all, preferred_element_type=f32)
+    d_model = d_all.shape[0]
+    d_heads = d_all.reshape(d_model, KV, 4 * HD)
+    d_query = d_heads[..., : 2 * HD].reshape(d_model, H * HD)
+    d_key = d_heads[..., 2 * HD : 3 * HD].reshape(d_model, KV * HD)
+    d_value = d_heads[..., 3 * HD :].reshape(d_model, KV * HD)
+    grad_x_norm, d_gain1 = rms_back(xs, scale1, norm1_gain, grad_xa)
+    grad_x = grad_h1 + grad_x_norm
+    summed = lax.psum(
+        (d_gain1, d_query, d_key, d_value, d_out_w, d_gain2, d_router), ("seq", "blk")
+    )
+    expert_summed = (
+        lax.psum(d_gate_w.astype(jnp.bfloat16), "seq").astype(jnp.float32),
+        lax.psum(d_up_w.astype(jnp.bfloat16), "seq").astype(jnp.float32),
+        lax.psum(d_down.astype(jnp.bfloat16), "seq").astype(jnp.float32),
+    )
+    return (
+        result.astype(bf16)[None],
+        grad_x[None],
+        summed[0],
+        summed[1],
+        summed[2],
+        summed[3],
+        summed[4],
+        summed[5],
+        summed[6],
+        expert_summed[0],
+        expert_summed[1],
+        expert_summed[2],
+    )
+
+
 def solution(mesh):
+    fused = dict(mesh.shape) == {"seq": 2, "blk": 2 * KV}
     return jax.shard_map(
-        per_device,
+        per_device if fused else per_device_plain,
         mesh=mesh,
         in_specs=(
             P("seq", "blk", None),

time: 1830 us -> 1380 us (0.75)
  waiting for transfers between devices: 857 us -> 458 us
  Pallas kernels: 0 us -> 162 us
  blocking collectives: 561 us -> 451 us
  local copies, waits for them, and re-layouts: 149 us -> 86.9 us
  matrix products: 143 us -> 112 us
    reduce_scatter x2 -> x0, waiting for transfers between devices: 264 us -> none  [the longest x1 177 us: per_device(): lax.psum_scatter(gk_blocks.reshape(length, KV * HD).astype(jnp.bfloat16),...]
    pallas_call x0 -> x2, Pallas kernels: none -> 162 us  [the longest x1 99 us: attention_backward(): pl.pallas_call(functools.partial(attention_backward_kernel, blocks), out_...]
    all_gather x2 -> x0, waiting for transfers between devices: 82.3 us -> none  [the longest x1 69.8 us: per_device(): lax.all_gather(value, 'blk', axis=0, tiled=True)]
    all_to_all x1, blocking collectives: 256 us -> 192 us  [per_device(): lax.all_to_all(outgoing.reshape(experts, cap, D), 'blk', split_axis=0, co...]
    dynamic_update_slice x24 -> x0, local copies, waits for them, and re-layouts: 50.7 us -> none  [per_device(): lax.scan(backward_step, zero_q, (k_blocks, v_blocks, s_blocks, starts))]
    all_gather x1 -> x0, blocking collectives: 42.6 us -> none  [per_device(): lax.all_gather(seg_float, 'blk', axis=0, tiled=True)]
    dot_general x16 -> x4, matrix products: 36.6 us -> 8.85 us  [the longest x1 3.52 us: per_device(): jnp.dot(xa, w_all, preferred_element_type=f32).reshape(tok, KV, 4 * HD)]
    psum x1, waiting for transfers between devices: 22.9 us -> 0.02 us  [per_device(): lax.psum(d_gate_w.astype(jnp.bfloat16), 'seq').astype(jnp.float32)]
  transfers between devices with their start and end apart: 8 -> 4, of which waited for: 8 -> 3; matrix products, arithmetic and copies ran while one was open for 6% -> 6% of each run, Pallas kernels for 0% -> 7%
where the time goes in v1:
time: 1380 us; the launch traced here: 1370 us
  waiting for transfers between devices  458 us (33%)
  blocking collectives  451 us (33%)
  Pallas kernels  162 us (12%)
  matrix products  112 us (8%)
  local copies, waits for them, and re-layouts  86.9 us (6%)
  other arithmetic  66.9 us (5%)
  starting transfers between devices  18.9 us (1%)
  between operations  15 us (1%)
    all_to_all x1, blocking collectives, per_device(): lax.all_to_all(grad_slots.reshape(experts, cap, D), 'blk', split_axis=0,...  220 us
    all_to_all x1, blocking collectives, per_device(): lax.all_to_all(outgoing.reshape(experts, cap, D), 'blk', split_axis=0, co...  192 us
    psum x1, waiting for transfers between devices, per_device(): lax.psum((d_gain1, d_query, d_key, d_value, d_out_w, d_gain2, d_router),...  184 us
    all_to_all x1, waiting for transfers between devices, per_device(): lax.all_to_all(expert_out.reshape(experts, cap, D), 'blk', split_axis=0,...  149 us
    all_to_all x1, waiting for transfers between devices, per_device(): lax.all_to_all(grad_in.reshape(experts, cap, D), 'blk', split_axis=0, con...  125 us
    pallas_call x1, Pallas kernels, attention_backward(): pl.pallas_call(functools.partial(attention_backward_kernel, blocks), out_...  99 us
    pallas_call x1, Pallas kernels, attention_forward(): pl.pallas_call(functools.partial(attention_forward_kernel, blocks), out_s...  62.8 us
    psum x1, blocking collectives, per_device(): lax.psum((d_gain1, d_query, d_key, d_value, d_out_w, d_gain2, d_router),...  38.3 us
  transfers between devices with their start and end apart: 4, of which 3 were waited for; matrix products, arithmetic and copies ran while one was open for 6% of the time, Pallas kernels for 7%

profile of v1, /device:TPU:0, one launch (start us, length us, event | category | flops | bytes accessed | tf_op | source)
XLA Modules:
  0.0 1370.1 jit_solution(9161620005326849678)
XLA Ops:
  7.2 1.4 fusion.39
  9.1 1.5 copy.79
  10.6 1.8 copy.82
  12.4 1.5 copy.80
  13.9 1.8 copy.83
  15.6 3.9 copy.78
  19.6 3.9 copy.81
  23.5 5.2 pad_maximum_fusion
  28.6 6.5 copy.84
  35.1 3.5 fusion.15
  43.1 1.6 dynamic-slice_bitcast_fusion
  46.5 1.5 mul.293
  48.1 1.7 copy.87
  49.7 2.5 copy.88
  54.6 2.5 copy.91
  59.7 1.6 scatter.12
  62.5 62.8 %attention_forward.1 = (bf16[256,1024]{1,0:T(8,128)(2,1)}, bf16[8,512,128]{2,1,0:T(8,128)(2,1)}, bf16[8,128,512]{2,1,0:T(8,128)(2,1)}, bf16[8,256,128]{2,1,0:T(8...) custom-call(bf16[8,272,256]{2,1,0:T(8,128)(2,1)} %pad_maximum_fusion.1.pay), custom_call_target="tpu_custom_call" | custom-call | tf_op jit(solution)/shard_map/attention_forward/pallas_call | solution.py:272
  125.3 2.0 multiply_reduce_fusion.2
  129.1 18.8 %fusion = pred[256,4096]{1,0:T(8,128)(4,1)S(1)} fusion(s32[256,8]{1,0:T(8,128)S(1)} %copy.95), kind=kLoop, calls=%fused_computation.3 | loop fusion | flops 15728640 | bytes 1056768 | tf_op jit(solution)/shard_map/reduce_or | solution.py:881
  147.9 3.8 convolution_convert_fusion
  151.7 192.3 %all_to_all.20 = bf16[16,256,1024]{2,1,0:T(8,128)(2,1)S(1)} all-to-all(bf16[16,256,1024]{2,1,0:T(8,128)(2,1)S(1)} %bitcast.272), channel_id=1, replica_groups=mesh['seq'=2,'blk'=16] {'blk'}, dimensions={0} | all-to-all | bytes 16777216 | tf_op jit(solution)/shard_map/all_to_all | solution.py:885
  344.1 4.5 fusion.59
  348.6 4.5 fusion.62
  353.2 3.0 fusion.13
  356.4 1.9 copy-done.12
  358.4 6.7 convolution_convert_fusion.1
  365.1 13.5 all-to-all-start.1
  379.6 2.1 bitcast_convert_fusion.3
  381.8 148.9 %all-to-all-done.1 = bf16[16,256,1024]{2,1,0:T(8,128)(2,1)} async-done(((bf16[16,256,1024]{2,1,0:T(8,128)(2,1)}), bf16[16,256,1024]{2,1,0:T(8,128)(2,1)}, u32[]{:S(2)}, u32[]{:S(2)}) %all-to-all-start.1) | async-done | bytes 8388640 | tf_op jit(solution)/shard_map/all_to_all | solution.py:898
  530.7 15.4 %gather_fusion = bf16[2048,1024]{1,0:T(8,128)(2,1)} fusion(bf16[4096,1024]{1,0:T(8,128)(2,1)} %bitcast.42, s32[2048]{0:T(1024)S(1)} %broadcast_clamp_fusion), kind=kCustom, calls=%fused_computation | custom fusion | bytes 8396800 | tf_op jit(solution)/shard_map/jit(_take)/gather | solution.py:901
  546.1 5.4 fusion.24
  551.9 15.6 %scatter_custom_fusion = bf16[4096,1024]{1,0:T(8,128)(2,1)} fusion(s32[2048]{0:T(1024)S(1)} %bitcast.288, f32[256,1024]{1,0:T(8,128)} %bitcast_convert_fusion.3, f32[2048]{0:T(1024)S(1)} %fusion.75, bf16[]{:T(256)} %constant.76.clone.1), kind=kCustom, calls=%fused_computation.24 | custom fusion | flops 4194304 | bytes 9445378 | tf_op jit(solution)/shard_map/scatter | solution.py:912
  567.5 220.1 %all_to_all.21 = bf16[16,256,1024]{2,1,0:T(8,128)(2,1)S(1)} all-to-all(bf16[16,256,1024]{2,1,0:T(8,128)(2,1)} %bitcast.268), channel_id=1, replica_groups=mesh['seq'=2,'blk'=16] {'blk'}, dimensions={0} | all-to-all | bytes 16777216 | tf_op jit(solution)/shard_map/all_to_all | solution.py:914
  787.6 15.9 %fusion.14 = (bf16[16,256,512]{2,1,0:T(8,128)(2,1)}, bf16[16,1,256,512]{3,2,0,1:T(8,128)(2,1)}) fusion(f32[16,256,512]{2,1,0:T(8,128)} %copy-done.9, f32[16,256,512]{2,1,0:T(8,128)} %copy-done.8, bf16[16,256,1024]{2,1,0:T(8,128)(2,1)S(1)} %all_to_all.21, bf16[1,512,1024]{2,1,0:T(8,128)(2,1)S(1)} %copy-done.39), kind=kOutput, calls=%fused_computation.26 | convolution fusion | flops 4322230272 | bytes 34603008 | tf_op jit(solution)/shard_map/necd,efd->necf/dot_general | solution.py:918
  803.5 10.5 fusion.19
  813.9 11.5 add_convert_fusion
  825.4 4.8 all-to-all-start.3
  830.8 2.0 fusion.92
  832.8 4.7 fusion.25
  837.5 8.2 fusion.34
  845.8 5.5 fusion.33
  851.3 5.5 fusion.30
  857.0 125.2 %all-to-all-done.3 = bf16[16,256,1024]{2,1,0:T(8,128)(2,1)} async-done(((bf16[16,256,1024]{2,1,0:T(8,128)(2,1)}), bf16[16,256,1024]{2,1,0:T(8,128)(2,1)}, u32[]{:S(2)}, u32[]{:S(2)}) %all-to-all-start.3) | async-done | bytes 8388640 | tf_op jit(solution)/shard_map/all_to_all | solution.py:928
  982.3 6.1 fusion.91
  989.0 2.5 subtract_add_fusion
  991.5 1.5 convolution_convert_fusion.2.do_ref
  993.0 99.0 %attention_backward.1 = bf16[8,256,256]{2,1,0:T(8,128)(2,1)} custom-call(bf16[256,1024]{1,0:T(8,128)(2,1)} %convolution_convert_fusion.2.do_ref, bf16[8,512,128]{2,1,0:T(8,128)(2,1)} %get-tuple-element.31.kv_ref, bf16[8,128,512]{2,1,0:T(8,128)(2,1)} %get-tuple-element.32.kvt_ref, bf16[8,256,128]{2,1,0:T(8,128)(2,1)} %get-tuple-element.33.q_ref, ...), custom_call_target="tpu_custom_call" | custom-call | tf_op jit(solution)/shard_map/attention_backward/pallas_call | solution.py:482
  1092.0 2.3 copy.100
  1094.3 2.7 fusion.52
  1097.0 2.3 slice.90
  1099.3 2.3 fusion.85
  1101.7 2.9 copy.103
  1104.5 2.9 copy.102
  1107.4 5.3 copy.101
  1112.8 3.8 fusion.67
  1116.7 3.0 convert_element_type.173
  1119.6 3.3 convert_element_type.176
  1123.0 1.6 convert_element_type.179
  1124.5 2.3 fusion.46
  1126.8 38.3 %all-reduce = (f32[1024]{0:T(1024)}, f32[1024]{0:T(1024)}) all-reduce(f32[1024]{0:T(1024)S(1)} %get-tuple-element.38, f32[1024]{0:T(1024)S(1)} %get-tuple-element.36), channel_id=1, replica_groups=mesh['seq'=2,'blk'=16] {'seq','blk'}, use_global_device_ids=true, to_apply=%region_15.16 | all-reduce | flops 2048 | bytes 16384 | tf_op jit(solution)/shard_map/psum | solution.py:955
  1165.1 2.7 fusion.43
  1167.8 184.0 %all-reduce.6.cloned.1.call-done = (f32[1024,1024]{1,0:T(8,128)}, f32[1024,512]{1,0:T(8,128)}, f32[1024,512]{1,0:T(8,128)}, f32[1024,1024]{1,0:T(8,128)}, f32[1024,16]{0,1:T(8,128)}) async-done(((f32[1024,1024]{1,0:T(8,128)}, f32[1024,512]{1,0:T(8,128)}, f32[1024,512]{1,0:T(8,128)}, f32[1024,1024]{1,0:T(8,128)}, f32[1024,16]{0,1:T(8,128)}), (f32[1024,1024]{1,0:T(8,128)}, f32[1024,512]{1,0:T(8,128)}, ...) | async-done | bytes 12648464 | tf_op jit(solution)/shard_map/psum | solution.py:955
  1351.8 4.9 copy.129
  1360.4 2.0 copy.132
  (161 shorter events, 21.8 us)
Async XLA Ops:
  7.2 118.1 %copy-start = (bf16[1024,1024]{1,0:T(8,128)(2,1)S(1)}, bf16[1024,1024]{1,0:T(8,128)(2,1)}, u32[]{:S(2)}) copy-start(bf16[1024,1024]{1,0:T(8,128)(2,1)} %param.28) | copy-start | bytes 6291460
  9.1 26.0 %copy-start.34 = (f32[256]{0:T(256)}, f32[256]{0:T(256)S(1)}, u32[]{:S(2)}) copy-start(f32[256]{0:T(256)S(1)} %get-tuple-element.69) | copy-start | bytes 3076
  28.6 6.5 copy-start.5
  28.6 6.5 copy-start.32
  38.7 1.5 copy-start.3
  38.7 2.5 copy-start.44
  38.7 3.7 copy-start.26
  53.5 4.0 copy-start.37
  57.1 1.6 copy-start.4
  57.1 2.0 copy-start.16
  57.1 2.0 copy-start.24
  57.5 1.8 copy-start.18
  59.7 67.6 %copy-start.25 = (f32[256,256]{1,0:T(8,128)S(1)}, f32[256,256]{1,0:T(8,128)}, u32[]{:S(2)}) copy-start(f32[256,256]{1,0:T(8,128)} %constant.89.clone) | copy-start | bytes 786436
  59.7 67.6 %copy-start.29 = (f32[256,16]{0,1:T(8,128)S(1)}, f32[256,16]{0,1:T(8,128)}, u32[]{:S(2)}) copy-start(f32[256,16]{0,1:T(8,128)} %convert_reduce_fusion) | copy-start | bytes 49156
  59.7 68.0 %copy-start.31 = (f32[1024]{0:T(1024)S(1)}, f32[1024]{0:T(1024)}, u32[]{:S(2)}) copy-start(f32[1024]{0:T(1024)} %param.29) | copy-start | bytes 12292
  61.4 67.3 %copy-start.27 = (bf16[1024,16]{0,1:T(8,128)(2,1)S(1)}, bf16[1024,16]{0,1:T(8,128)(2,1)}, u32[]{:S(2)}) copy-start(bf16[1024,16]{0,1:T(8,128)(2,1)} %param.30) | copy-start | bytes 98308
  127.3 861.1 %copy-start.2 = (f32[256,1024]{1,0:T(8,128)}, f32[256,1024]{1,0:T(8,128)S(1)}, u32[]{:S(2)}) copy-start(f32[256,1024]{1,0:T(8,128)S(1)} %get-tuple-element.75) | copy-start | bytes 3145732
  127.8 0.8 copy-start.11
  147.9 3.8 copy-start.22
  151.7 192.3 %copy-start.42 = (bf16[1,1024,512]{2,1,0:T(8,128)(2,1)S(1)}, bf16[1,1024,512]{2,1,0:T(8,128)(2,1)}, u32[]{:S(2)}) copy-start(bf16[1,1024,512]{2,1,0:T(8,128)(2,1)} %param.32) | copy-start | bytes 3145732
  344.1 4.6 copy-start.7
  344.1 4.6 copy-start.40
  348.6 4.5 copy-start.8
  353.2 3.2 copy-start.9
  353.2 5.2 copy-start.38
  356.4 1.9 copy-start.12
  365.1 13.8 %copy-start.28 = (f32[1,256,8]{1,2,0:T(8,128)S(1)}, f32[1,256,8]{1,2,0:T(8,128)}, u32[]{:S(2)}) copy-start(f32[1,256,8]{1,2,0:T(8,128)} %param.23) | copy-start | bytes 24580
  365.1 165.6 %all-to-all-start.1 = ((bf16[16,256,1024]{2,1,0:T(8,128)(2,1)}), bf16[16,256,1024]{2,1,0:T(8,128)(2,1)}, u32[]{:S(2)}, u32[]{:S(2)}) async-start(bf16[16,256,1024]{2,1,0:T(8,128)(2,1)} %convolution_convert_fusion.1), calls=%async_computation.1 | async-start | bytes 16777216 | tf_op jit(solution)/shard_map/all_to_all | solution.py:898
  567.5 220.1 %copy-start.39 = (bf16[1,512,1024]{2,1,0:T(8,128)(2,1)S(1)}, bf16[1,512,1024]{2,1,0:T(8,128)(2,1)}, u32[]{:S(2)}) copy-start(bf16[1,512,1024]{2,1,0:T(8,128)(2,1)} %param.33) | copy-start | bytes 3145732
  787.6 15.9 %copy-start.10 = (bf16[16,256,1024]{2,1,0:T(8,128)(2,1)}, bf16[16,256,1024]{2,1,0:T(8,128)(2,1)S(1)}, u32[]{:S(2)}) copy-start(bf16[16,256,1024]{2,1,0:T(8,128)(2,1)S(1)} %all_to_all.21) | copy-start | bytes 25165828
  787.6 15.9 %copy-start.41 = (bf16[1,1024,512]{2,1,0:T(8,128)(2,1)S(1)}, bf16[1,1024,512]{2,1,0:T(8,128)(2,1)}, u32[]{:S(2)}) copy-start(bf16[1,1024,512]{2,1,0:T(8,128)(2,1)} %param.31) | copy-start | bytes 3145732
  803.4 10.5 copy-start.43
  825.4 156.9 %all-to-all-start.3 = ((bf16[16,256,1024]{2,1,0:T(8,128)(2,1)}), bf16[16,256,1024]{2,1,0:T(8,128)(2,1)}, u32[]{:S(2)}, u32[]{:S(2)}) async-start(bf16[16,256,1024]{2,1,0:T(8,128)(2,1)} %add_convert_fusion), calls=%async_computation.3 | async-start | bytes 16777216 | tf_op jit(solution)/shard_map/all_to_all | solution.py:928
  830.2 286.4 %all-reduce.8.cloned.1.call-start = ((), (), s32[]{:S(2)}) async-start(), calls=%async_computation.5 | async-start | bytes 6291456 | tf_op jit(solution)/shard_map/psum | solution.py:959
  830.8 6.7 copy-start.13
  832.8 12.9 slice-start
  837.5 8.2 slice-start.1
  837.5 8.2 copy-start.45
  845.8 5.5 copy-start.46
  856.8 494.9 %all-reduce.6.cloned.1.call-start = ((), (), s32[]{:S(2)}) async-start(), calls=%async_computation.4 | async-start | bytes 25296896 | tf_op jit(solution)/shard_map/psum | solution.py:955
  982.3 6.7 copy-start.17
  982.3 6.7 copy-start.23
  993.0 101.2 %copy-start.33 = (f32[1024]{0:T(1024)S(1)}, f32[1024]{0:T(1024)}, u32[]{:S(2)}) copy-start(f32[1024]{0:T(1024)} %param.24) | copy-start | bytes 12292
  993.0 101.2 %copy-start.35 = (f32[256]{0:T(256)S(1)}, f32[256]{0:T(256)}, u32[]{:S(2)}) copy-start(f32[256]{0:T(256)} %copy-done.34) | copy-start | bytes 3076
  1116.6 6.3 copy-start.21
  1116.6 7.9 copy-start.1
  1116.6 7.9 copy-start.6
  1116.6 7.9 copy-start.14
  1124.5 40.6 %copy-start.36 = (f32[256]{0:T(256)S(1)}, f32[256]{0:T(256)}, u32[]{:S(2)}) copy-start(f32[256]{0:T(256)} %get-tuple-element.68) | copy-start | bytes 3076
  1351.8 4.9 copy-start.20
  1351.8 6.3 copy-start.19
  1356.7 3.7 copy-start.15
  1360.4 2.0 copy-start.30
Sparse Core Ops, SparseCore 0:
  856.9 24.5 all-reduce.7
  1116.7 235.0 all-reduce.5

commit v2 on v1

--- a/solution.py
+++ b/solution.py
@@ -56,6 +56,14 @@
     pl.semaphore_wait(barrier, total - 1)
 
 
+def flip(place, n):
+    if n == 1:
+        return place + 1 - 2 * lax.rem(place, 2)
+    if n == 2:
+        return place + 2 - 4 * (place // 2)
+    return 3 - place
+
+
 def rotate_pairs(u):
     lanes = u.shape[-1]
     half = HD // 2
@@ -72,12 +80,20 @@
 def attention_forward_kernel(
     blocks,
     pay,
+    g_ref,
+    wg_ref,
+    wu_ref,
+    wd_ref,
     o_ref,
     kv_ref,
     kvt_ref,
     q_ref,
     ot_ref,
     stat_ref,
+    g_all,
+    wg_all,
+    wu_all,
+    wd_all,
     in_ref,
     other_ref,
     obuf,
@@ -88,6 +104,12 @@
     frecv_sem,
     osend_sem,
     orecv_sem,
+    gsend_sem,
+    grecv_sem,
+    wsend_sem,
+    wrecv_sem,
+    hsend_sem,
+    hrecv_sem,
 ):
     me_s = lax.axis_index("seq")
     me_b = lax.axis_index("blk")
@@ -99,6 +121,39 @@
 
     dest_core = lax.rem(me_b, 2)
     slot = me_b // 2
+    line, plane = me_b // 4, lax.rem(me_b, 4)
+    weights = ((wg_ref, wg_all), (wu_ref, wu_all), (wd_ref, wd_all))
+
+    def share_grad(n):
+        return remote(
+            g_ref,
+            g_all.at[line],
+            gsend_sem.at[n - 1],
+            grecv_sem.at[n - 1],
+            me_s,
+            flip(line, n) * 4 + plane,
+        )
+
+    def half(ref):
+        rows = ref.shape[0] // 2
+        return ref.at[pl.ds(pl.multiple_of(me_s * rows, rows), rows)]
+
+    def share_weight(n, i):
+        own, everyone = weights[i]
+        return remote(
+            half(own),
+            half(everyone.at[plane]),
+            wsend_sem.at[n - 1, i],
+            wrecv_sem.at[n - 1, i],
+            me_s,
+            line * 4 + flip(plane, n),
+        )
+
+    def pass_weight(n, i):
+        arrived = half(weights[i][1].at[flip(plane, n)])
+        return remote(
+            arrived, arrived, hsend_sem.at[n - 1, i], hrecv_sem.at[n - 1, i], 1 - me_s, me_b
+        )
 
     def payload(n):
         k = lax.rem(me_b + n, KV)
@@ -122,6 +177,10 @@
         return carry
 
     lax.fori_loop(0, KV, send_payload, 0)
+    for n in (1, 2, 3):
+        share_grad(n).start()
+        for i in range(3):
+            share_weight(n, i).start()
 
     def arrival(t):
         return pltpu.make_async_copy(pay.at[0], in_ref.at[t], recv_sem.at[t])
@@ -219,6 +278,10 @@
         return carry
 
     lax.fori_loop(0, steps, step, 0)
+    for n in (1, 2, 3):
+        for i in range(3):
+            share_weight(n, i).wait_recv()
+            pass_weight(n, i).start()
 
     def finish(t, carry):
         k, chip, mine = payload(t)
@@ -262,12 +325,18 @@
         return carry
 
     lax.fori_loop(0, KV, gather, 0)
-
-
-def attention_forward(blocks, pay):
+    for n in (1, 2, 3):
+        share_grad(n).wait()
+        for i in range(3):
+            share_weight(n, i).wait_send()
+            pass_weight(n, i).wait()
+
+
+def attention_forward(blocks, pay, g, w_gate, w_up, w_down):
     tok = pay.shape[2]
     steps = blocks // 2
     vm = pl.BlockSpec(memory_space=pltpu.VMEM)
+    hbm = pl.BlockSpec(memory_space=pl.ANY)
     dma = pltpu.SemaphoreType.DMA
     return pl.pallas_call(
         functools.partial(attention_forward_kernel, blocks),
@@ -278,9 +347,13 @@
             jax.ShapeDtypeStruct((steps, tok, 2 * HD), BF16),
             jax.ShapeDtypeStruct((steps, HD, 2 * tok), F32),
             jax.ShapeDtypeStruct((steps, 8, 2 * tok), F32),
+            jax.ShapeDtypeStruct((4, *g.shape), BF16),
+            jax.ShapeDtypeStruct((4, *w_gate.shape), BF16),
+            jax.ShapeDtypeStruct((4, *w_up.shape), BF16),
+            jax.ShapeDtypeStruct((4, *w_down.shape), BF16),
         ),
-        in_specs=[vm],
-        out_specs=(vm,) * 6,
+        in_specs=[vm] + [hbm] * 4,
+        out_specs=(vm,) * 6 + (hbm,) * 4,
         scratch_shapes=[
             pltpu.VMEM((steps, tok + 16, 4 * HD), BF16),
             pltpu.VMEM((steps, tok + 16, 2 * HD), BF16),
@@ -292,12 +365,18 @@
             dma((steps,)),
             dma((steps,)),
             dma((KV,)),
+            dma((3,)),
+            dma((3,)),
+            dma((3, 3)),
+            dma((3, 3)),
+            dma((3, 3)),
+            dma((3, 3)),
         ],
         compiler_params=pltpu.CompilerParams(
             collective_id=0, has_side_effects=True, vmem_limit_bytes=VMEM_LIMIT
         ),
         name="attention_forward",
-    )(pay)
+    )(pay, g, w_gate, w_up, w_down)
 
 
 def attention_backward_kernel(
@@ -310,7 +389,15 @@
     stat_ref,
     cos_ref,
     sin_ref,
+    mix_ref,
+    dwg_ref,
+    dwu_ref,
+    dwd_ref,
     out_ref,
+    mix_in,
+    dwg_in,
+    dwu_in,
+    dwd_in,
     in_ref,
     dkv,
     part,
@@ -322,6 +409,10 @@
     xrecv_sem,
     osend_sem,
     orecv_sem,
+    msend_sem,
+    mrecv_sem,
+    wsend_sem,
+    wrecv_sem,
 ):
     me_s = lax.axis_index("seq")
     me_b = lax.axis_index("blk")
@@ -333,6 +424,29 @@
 
     dest_core = lax.rem(me_b, 2)
     slot = me_b // 2
+    line, plane = me_b // 4, lax.rem(me_b, 4)
+    weights = ((dwg_ref, dwg_in), (dwu_ref, dwu_in), (dwd_ref, dwd_in))
+
+    def give_mix(n):
+        return remote(
+            mix_ref.at[n - 1],
+            mix_in.at[n - 1],
+            msend_sem.at[n - 1],
+            mrecv_sem.at[n - 1],
+            me_s,
+            flip(line, n) * 4 + plane,
+        )
+
+    def give_weight(n, i):
+        src, dst = weights[i]
+        return remote(
+            src.at[flip(plane, n)],
+            dst.at[n - 1],
+            wsend_sem.at[n - 1, i],
+            wrecv_sem.at[n - 1, i],
+            me_s,
+            line * 4 + flip(plane, n),
+        )
 
     def outgoing(n):
         k = lax.rem(me_b + n, KV)
@@ -355,6 +469,10 @@
         return carry
 
     lax.fori_loop(0, KV, send_grad, 0)
+    for n in (1, 2, 3):
+        give_mix(n).start()
+        for i in range(3):
+            give_weight(n, i).start()
     dkv[...] = jnp.zeros_like(dkv)
     wide = 2 * tok
     lane = lax.broadcasted_iota(jnp.int32, (1, wide), 1)
@@ -472,18 +590,31 @@
         return carry
 
     lax.fori_loop(0, KV, gather, 0)
-
-
-def attention_backward(blocks, d_o, kv, kvt, q_two, out_t, stat, cos_all, sin_all):
+    for n in (1, 2, 3):
+        give_mix(n).wait()
+        for i in range(3):
+            give_weight(n, i).wait()
+
+
+def attention_backward(
+    blocks, d_o, kv, kvt, q_two, out_t, stat, cos_all, sin_all, mix, dwg, dwu, dwd
+):
     tok = q_two.shape[1]
     steps = blocks // 2
     vm = pl.BlockSpec(memory_space=pltpu.VMEM)
+    hbm = pl.BlockSpec(memory_space=pl.ANY)
     dma = pltpu.SemaphoreType.DMA
     return pl.pallas_call(
         functools.partial(attention_backward_kernel, blocks),
-        out_shape=jax.ShapeDtypeStruct((KV, tok, 4 * HD), BF16),
-        in_specs=[vm] * 8,
-        out_specs=vm,
+        out_shape=(
+            jax.ShapeDtypeStruct((KV, tok, 4 * HD), BF16),
+            jax.ShapeDtypeStruct(mix.shape, BF16),
+            jax.ShapeDtypeStruct((3, *dwg.shape[1:]), BF16),
+            jax.ShapeDtypeStruct((3, *dwu.shape[1:]), BF16),
+            jax.ShapeDtypeStruct((3, *dwd.shape[1:]), BF16),
+        ),
+        in_specs=[vm] * 8 + [hbm] * 4,
+        out_specs=(vm,) + (hbm,) * 4,
         scratch_shapes=[
             pltpu.VMEM((steps, tok, 2 * HD), BF16),
             pltpu.VMEM((steps, 2 * tok, 2 * HD), F32),
@@ -496,12 +627,299 @@
             dma((steps,)),
             dma((steps,)),
             dma((KV,)),
+            dma((3,)),
+            dma((3,)),
+            dma((3, 3)),
+            dma((3, 3)),
         ],
         compiler_params=pltpu.CompilerParams(
             collective_id=1, has_side_effects=True, vmem_limit_bytes=VMEM_LIMIT
         ),
         name="attention_backward",
-    )(d_o, kv, kvt, q_two, out_t, stat, cos_all, sin_all)
+    )(d_o, kv, kvt, q_two, out_t, stat, cos_all, sin_all, mix, dwg, dwu, dwd)
+
+
+def mixture_kernel(
+    x_ref,
+    g_ref,
+    wg_ref,
+    wu_ref,
+    wd_ref,
+    g_all,
+    wg_all,
+    wu_all,
+    wd_all,
+    mix_own,
+    mix_peer,
+    d_in,
+    dwg_out,
+    dwu_out,
+    dwd_out,
+    x_in,
+    x_t,
+    g_in,
+    wg,
+    wu,
+    wd,
+    hc,
+    dg,
+    du,
+    acc_o,
+    acc_d,
+    acc_c,
+    d_send,
+    d_recv,
+    xg,
+    xu,
+    xd,
+    load_sem,
+    gload_sem,
+    send_sem,
+    recv_sem,
+    bsend_sem,
+    brecv_sem,
+    psend_sem,
+    precv_sem,
+    store_sem,
+):
+    me_s = lax.axis_index("seq")
+    me_b = lax.axis_index("blk")
+    line, plane = me_b // 4, lax.rem(me_b, 4)
+    tok, d = g_in.shape[1:]
+    ff = wg.shape[2]
+    barrier = pltpu.get_barrier_semaphore()
+    places = [(me_s, flip(line, n) * 4 + plane) for n in (1, 2, 3)] + [(1 - me_s, me_b)]
+    for place in places:
+        pl.semaphore_signal(barrier, inc=1, device_id=place, device_id_type=MESH)
+
+    owns = ((wg_ref, wg_all, wg), (wu_ref, wu_all, wu), (wd_ref, wd_all, wd))
+
+    def load_own(i):
+        return pltpu.make_async_copy(owns[i][0], owns[i][2].at[plane], load_sem.at[i, plane])
+
+    def load_other(i, e):
+        return pltpu.make_async_copy(owns[i][1].at[e], owns[i][2].at[e], load_sem.at[i, e])
+
+    for i in range(3):
+        load_own(i).start()
+        for n in (1, 2, 3):
+            load_other(i, flip(plane, n)).start()
+
+    def load_grad(n):
+        src = g_ref if n == 0 else g_all.at[flip(line, n)]
+        return pltpu.make_async_copy(src, g_in.at[n], gload_sem.at[n])
+
+    for n in range(4):
+        load_grad(n).start()
+    pl.semaphore_wait(barrier, 4)
+
+    def spread(n):
+        return remote(
+            x_ref, x_in.at[n], send_sem.at[n - 1], recv_sem.at[n - 1], *places[n - 1]
+        )
+
+    for n in (1, 2, 3):
+        spread(n).start()
+    x_in[0] = x_ref[...]
+    for n in range(4):
+        load_grad(n).wait()
+
+    def load_wait(e, carry):
+        for i in range(3):
+            load_other(i, e).wait()
+        return carry
+
+    lane = lax.broadcasted_iota(jnp.int32, (tok, 128), 1)
+
+    def block(n, carry):
+        @pl.when(n > 0)
+        def _():
+            pltpu.make_async_copy(x_ref, x_in.at[n], recv_sem.at[jnp.maximum(n - 1, 0)]).wait()
+
+        acc_o[...] = jnp.zeros_like(acc_o)
+        acc_d[...] = jnp.zeros_like(acc_d)
+        acc_c[...] = jnp.zeros_like(acc_c)
+        rows = pl.ds(pl.multiple_of(n * tok, tok), tok)
+
+        def expert(e, carry):
+            @pl.when(n == 0)
+            def _():
+                load_wait(e, 0)
+
+            x = x_in[n, :, :d]
+            here = lane == line * 4 + e
+            share = jnp.sum(
+                jnp.where(here, x_in[n, :, d:].astype(F32), 0.0), 1, keepdims=True
+            )
+            gate = mm(x, wg[e])
+            up = mm(x, wu[e])
+            dh = mm(g_in[n], wd[e], NT)
+            sg = jax.nn.sigmoid(gate)
+            act = gate * sg
+            hidden = act * up
+            acc_c[...] += jnp.where(here, jnp.sum(dh * hidden, 1, keepdims=True), 0.0)
+            dh = dh * share
+            hcb = (hidden * share).astype(BF16)
+            dgb = (dh * up * sg * (1.0 + gate * (1.0 - sg))).astype(BF16)
+            dub = (dh * act).astype(BF16)
+            hc[e, rows, :] = hcb
+            dg[e, rows, :] = dgb
+            du[e, rows, :] = dub
+            acc_o[...] += mm(hcb, wd[e])
+            acc_d[...] += mm(dgb, wg[e], NT) + mm(dub, wu[e], NT)
+            return carry
+
+        lax.fori_loop(0, 4, expert, 0)
+
+        @pl.when(n == 0)
+        def _():
+            mix_own[...] = acc_o[...]
+            d_in[:, :d] = acc_d[...]
+            d_in[:, d:] = acc_c[...]
+
+        for m in (1, 2, 3):
+
+            @pl.when(n == m)
+            def _():
+                mix_peer[m - 1] = acc_o[...].astype(BF16)
+                d_send[m - 1, :, :d] = acc_d[...].astype(BF16)
+                high = acc_c[...].astype(BF16).astype(F32)
+                rest = acc_c[...] - high
+                d_send[m - 1, :, d:] = (high + pltpu.roll(rest, 32, 1)).astype(BF16)
+                give_back(m).start()
+
+        x_t[:, rows] = jnp.transpose(x_in[n, :, :d].astype(F32)).astype(BF16)
+        return carry
+
+    def give_back(n):
+        return remote(
+            d_send.at[n - 1],
+            d_recv.at[n - 1],
+            bsend_sem.at[n - 1],
+            brecv_sem.at[n - 1],
+            *places[n - 1],
+        )
+
+    lax.fori_loop(0, 4, block, 0)
+
+    half, dhalf = d // 2, ff // 2
+    theirs = pl.multiple_of((1 - me_s) * half, half)
+    dtheirs = pl.multiple_of((1 - me_s) * dhalf, dhalf)
+    mine = pl.multiple_of(me_s * half, half)
+    dmine = pl.multiple_of(me_s * dhalf, dhalf)
+    g_rows = g_in.reshape(4 * tok, d)
+
+    def swap(i, e):
+        src = (wg.at[e, pl.ds(0, half)], wu.at[e, pl.ds(0, half)], wd.at[e, pl.ds(0, dhalf)])[i]
+        dst = (xg, xu, xd)[i].at[e]
+        return remote(src, dst, psend_sem.at[i, e], precv_sem.at[i, e], *places[3])
+
+    def store(i, e):
+        return pltpu.make_async_copy(
+            (xg, xu, xd)[i].at[e], (dwg_out, dwu_out, dwd_out)[i].at[e], store_sem.at[i, e]
+        )
+
+    def give(e, carry):
+        left = x_t[pl.ds(theirs, half), :]
+        wg[e, :half, :] = mm(left, dg[e]).astype(BF16)
+        swap(0, e).start()
+        wu[e, :half, :] = mm(left, du[e]).astype(BF16)
+        swap(1, e).start()
+        wd[e, :dhalf, :] = mm(hc[e, :, pl.ds(dtheirs, dhalf)], g_rows[...], TN).astype(BF16)
+        swap(2, e).start()
+        return carry
+
+    lax.fori_loop(0, 4, give, 0)
+
+    def keep(e, carry):
+        left = x_t[pl.ds(mine, half), :]
+        own = mm(left, dg[e])
+        swap(0, e).wait_recv()
+        xg[e] = (own + xg[e].astype(F32)).astype(BF16)
+        store(0, e).start()
+        own = mm(left, du[e])
+        swap(1, e).wait_recv()
+        xu[e] = (own + xu[e].astype(F32)).astype(BF16)
+        store(1, e).start()
+        own = mm(hc[e, :, pl.ds(dmine, dhalf)], g_rows[...], TN)
+        swap(2, e).wait_recv()
+        xd[e] = (own + xd[e].astype(F32)).astype(BF16)
+        store(2, e).start()
+        return carry
+
+    lax.fori_loop(0, 4, keep, 0)
+
+    for n in (1, 2, 3):
+        give_back(n).wait_recv()
+        d_in[:, :d] += d_recv[n - 1, :, :d].astype(F32)
+        tail = d_recv[n - 1, :, d:].astype(F32)
+        both = tail + pltpu.roll(tail, 96, 1)
+        d_in[:, d:] += jnp.where(lane < 32, both, 0.0)
+    for n in (1, 2, 3):
+        spread(n).wait_send()
+        give_back(n).wait_send()
+
+    def finish(e, carry):
+        for i in range(3):
+            swap(i, e).wait_send()
+            store(i, e).wait()
+        return carry
+
+    lax.fori_loop(0, 4, finish, 0)
+
+
+def mixture(x, g, w_gate, w_up, w_down, g_all, wg_all, wu_all, wd_all):
+    tok, d = g.shape
+    ff = w_gate.shape[1]
+    vm = pl.BlockSpec(memory_space=pltpu.VMEM)
+    hbm = pl.BlockSpec(memory_space=pl.ANY)
+    dma = pltpu.SemaphoreType.DMA
+    vmem = pltpu.VMEM
+    return pl.pallas_call(
+        mixture_kernel,
+        out_shape=(
+            jax.ShapeDtypeStruct((tok, d), F32),
+            jax.ShapeDtypeStruct((3, tok, d), BF16),
+            jax.ShapeDtypeStruct((tok, d + 128), F32),
+            jax.ShapeDtypeStruct((4, d // 2, ff), BF16),
+            jax.ShapeDtypeStruct((4, d // 2, ff), BF16),
+            jax.ShapeDtypeStruct((4, ff // 2, d), BF16),
+        ),
+        in_specs=[vm] + [hbm] * 8,
+        out_specs=(vm, vm, vm, hbm, hbm, hbm),
+        scratch_shapes=[
+            vmem((4, tok, d + 128), BF16),
+            vmem((d, 4 * tok), BF16),
+            vmem((4, tok, d), BF16),
+            vmem((4, d, ff), BF16),
+            vmem((4, d, ff), BF16),
+            vmem((4, ff, d), BF16),
+            vmem((4, 4 * tok, ff), BF16),
+            vmem((4, 4 * tok, ff), BF16),
+            vmem((4, 4 * tok, ff), BF16),
+            vmem((tok, d), F32),
+            vmem((tok, d), F32),
+            vmem((tok, 128), F32),
+            vmem((3, tok, d + 128), BF16),
+            vmem((3, tok, d + 128), BF16),
+            vmem((4, d // 2, ff), BF16),
+            vmem((4, d // 2, ff), BF16),
+            vmem((4, ff // 2, d), BF16),
+            dma((3, 4)),
+            dma((4,)),
+            dma((3,)),
+            dma((3,)),
+            dma((3,)),
+            dma((3,)),
+            dma((3, 4)),
+            dma((3, 4)),
+            dma((3, 4)),
+        ],
+        compiler_params=pltpu.CompilerParams(
+            collective_id=2, has_side_effects=True, vmem_limit_bytes=VMEM_LIMIT
+        ),
+        name="mixture",
+    )(x, g, w_gate, w_up, w_down, g_all, wg_all, wu_all, wd_all)
 
 
 D = 1024
@@ -827,23 +1245,22 @@
     w_down,
     cotangent,
 ):
-    f32 = jnp.float32
-    bf16 = jnp.bfloat16
     scale = HD ** (-0.5)
-    xs = tokens[0].astype(f32)
-    tok = xs.shape[0]
+    xs = tokens[0].astype(F32)
+    tok, d = xs.shape
     blocks = lax.axis_size("blk")
-    length = tok * blocks
-    cos_np, sin_np = tables(length)
+    experts = w_router.shape[1]
+    cos_np, sin_np = tables(tok * blocks)
     cos_all = jnp.asarray(cos_np.reshape(blocks, tok, 2 * HD))
     sin_all = jnp.asarray(sin_np.reshape(blocks, tok, 2 * HD))
     me = lax.axis_index("blk")
+    me_s = lax.axis_index("seq")
     cosine = lax.dynamic_index_in_dim(cos_all, me, 0, keepdims=False)[:, None, :]
     sine = lax.dynamic_index_in_dim(sin_all, me, 0, keepdims=False)[:, None, :]
     scale1 = rms_scale(xs)
-    xa = (xs * scale1 * norm1_gain).astype(bf16)
+    xa = (xs * scale1 * norm1_gain).astype(BF16)
     w_all = by_head(w_query, w_key, w_value)
-    qkv = jnp.dot(xa, w_all, preferred_element_type=f32).reshape(tok, KV, 4 * HD)
+    qkv = mm(xa, w_all).reshape(tok, KV, 4 * HD)
 
     def turned(u):
         parts = u.reshape(tok, KV, -1, HD)
@@ -852,128 +1269,80 @@
         ).reshape(u.shape)
 
     pay = jnp.concatenate(
-        [turned(qkv[..., : 2 * HD]) * scale, turned(qkv[..., 2 * HD : 3 * HD]), qkv[..., 3 * HD :]], -1
-    ).astype(bf16)
-    seg = jnp.zeros((16, 4 * HD), bf16).at[:2, 2 * HD :].set(
-        segments[0].astype(bf16).reshape(2, tok // 2)
+        [
+            turned(qkv[..., : 2 * HD]) * scale,
+            turned(qkv[..., 2 * HD : 3 * HD]),
+            qkv[..., 3 * HD :],
+        ],
+        -1,
+    ).astype(BF16)
+    seg = (
+        jnp.zeros((16, 4 * HD), BF16)
+        .at[:2, 2 * HD :]
+        .set(segments[0].astype(BF16).reshape(2, tok // 2))
     )
     pay = jnp.concatenate(
         [pay.transpose(1, 0, 2), jnp.broadcast_to(seg[None], (KV, 16, 4 * HD))], 1
     )
-    att_low, *kept = attention_forward(blocks, pay)
-    h1 = xs + jnp.dot(att_low, w_out, preferred_element_type=f32)
+    g_low = cotangent[0]
+    att_low, *kept = attention_forward(blocks, pay, g_low, w_gate[0], w_up[0], w_down[0])
+    kept, shared = kept[:5], kept[5:]
+
+    h1 = xs + mm(att_low, w_out)
     scale2 = rms_scale(h1)
-    xl = (h1 * scale2 * norm2_gain).astype(bf16)
-    logits = jnp.dot(xl, w_router, preferred_element_type=f32)
-    experts = logits.shape[1]
-    route = routes[0]
-    rweight = route_weight[0]
-    chooser = (route[:, :, None] == jnp.arange(experts, dtype=jnp.int32)[None, None, :]).astype(f32)
-    chosen = jnp.sum(chooser * logits[:, None, :], -1)
-    gates = jax.nn.softmax(chosen, -1)
-    combine = (rweight * gates).astype(bf16)
-    cap = min(tok, 2 * tok * TOP // experts)
-    member = jnp.sum(chooser, 1)
-    before = jnp.asarray(np.tril(np.ones((tok, tok), np.float32), -1))
-    order = jnp.dot(before, member, precision=HIGH)
-    rank = jnp.sum(chooser * order[:, None, :], -1).astype(jnp.int32)
-    slots = route * cap + rank
-    placed = jnp.any(
-        slots[:, :, None] == jnp.arange(experts * cap, dtype=jnp.int32)[None, None, :], 1
-    ).astype(bf16)
-    outgoing = jnp.einsum("ts,td->sd", placed, xl, preferred_element_type=f32).astype(bf16)
-    incoming = lax.all_to_all(
-        outgoing.reshape(experts, cap, D), "blk", split_axis=0, concat_axis=0, tiled=True
-    )
-    local_exp = w_gate.shape[0]
-    incoming = incoming.reshape(blocks, local_exp, cap, D)
-    gate_pre = jnp.einsum("necd,edf->necf", incoming, w_gate, preferred_element_type=f32)
-    up_pre = jnp.einsum("necd,edf->necf", incoming, w_up, preferred_element_type=f32)
-    sigma = jax.nn.sigmoid(gate_pre)
-    activated = gate_pre * sigma
-    hidden = (activated * up_pre).astype(bf16)
-    expert_out = jnp.einsum("necf,efd->necd", hidden, w_down, preferred_element_type=f32).astype(
-        bf16
-    )
-    returned = lax.all_to_all(
-        expert_out.reshape(experts, cap, D), "blk", split_axis=0, concat_axis=0, tiled=True
-    )
-    per_route = jnp.take(returned.reshape(experts * cap, D), slots.reshape(-1), axis=0).reshape(
-        tok, TOP, D
-    )
-    mixture = jnp.einsum("tj,tjd->td", combine, per_route, preferred_element_type=f32)
-    result = h1 + mixture
-    grad_out = cotangent[0].astype(f32)
-    grad_combine = jnp.einsum("td,tjd->tj", grad_out, per_route.astype(f32), precision=HIGH)
-    route_grads = (combine.astype(f32)[:, :, None] * grad_out[:, None, :]).astype(bf16)
-    grad_slots = (
-        jnp.zeros((experts * cap, D), bf16)
-        .at[slots.reshape(-1)]
-        .set(route_grads.reshape(tok * TOP, D))
-    )
-    grad_incoming = lax.all_to_all(
-        grad_slots.reshape(experts, cap, D), "blk", split_axis=0, concat_axis=0, tiled=True
-    )
-    grad_incoming = grad_incoming.reshape(blocks, local_exp, cap, D)
-    grad_hidden = jnp.einsum("necd,efd->necf", grad_incoming, w_down, preferred_element_type=f32)
-    grad_gate = (grad_hidden * up_pre * sigma * (1.0 + gate_pre * (1.0 - sigma))).astype(bf16)
-    grad_up = (grad_hidden * activated).astype(bf16)
-    d_down = jnp.einsum("necf,necd->efd", hidden, grad_incoming, preferred_element_type=f32)
-    d_gate_w = jnp.einsum("necd,necf->edf", incoming, grad_gate, preferred_element_type=f32)
-    d_up_w = jnp.einsum("necd,necf->edf", incoming, grad_up, preferred_element_type=f32)
-    grad_in = (
-        jnp.einsum("necf,edf->necd", grad_gate, w_gate, preferred_element_type=f32)
-        + jnp.einsum("necf,edf->necd", grad_up, w_up, preferred_element_type=f32)
-    ).astype(bf16)
-    grad_back = lax.all_to_all(
-        grad_in.reshape(experts, cap, D), "blk", split_axis=0, concat_axis=0, tiled=True
-    )
-    grad_xl = jnp.einsum(
-        "ts,sd->td", placed, grad_back.reshape(experts * cap, D), preferred_element_type=f32
-    )
-    grad_gates = rweight * grad_combine
-    grad_chosen = gates * (grad_gates - jnp.sum(gates * grad_gates, -1, keepdims=True))
-    grad_logits = jnp.sum(chooser * grad_chosen[:, :, None], 1).astype(bf16)
-    d_router = jnp.einsum("td,te->de", xl, grad_logits, preferred_element_type=f32)
-    grad_xl = grad_xl + jnp.einsum("te,de->td", grad_logits, w_router, preferred_element_type=f32)
+    xl = (h1 * scale2 * norm2_gain).astype(BF16)
+    logits = mm(xl, w_router)
+    chooser = routes[0][:, :, None] == jnp.arange(experts, dtype=jnp.int32)[None, None, :]
+    routed = jnp.any(chooser, 1)
+    rweight = jnp.sum(jnp.where(chooser, route_weight[0][:, :, None], 0.0), 1)
+    top = jnp.max(jnp.where(routed, logits, NEG), -1, keepdims=True)
+    expo = jnp.where(routed, jnp.exp(logits - top), 0.0)
+    gates = expo / jnp.sum(expo, -1, keepdims=True)
+    combine = (rweight * gates).astype(BF16)
+    sent = jnp.concatenate([xl, jnp.pad(combine, ((0, 0), (0, 128 - experts)))], 1)
+    mix_own, mix_peer, d_in, dwg, dwu, dwd = mixture(
+        sent, g_low, w_gate[0], w_up[0], w_down[0], *shared
+    )
+
+    grad_out = g_low.astype(F32)
+    grad_gates = rweight * d_in[:, d : d + experts]
+    grad_logits = (
+        gates * (grad_gates - jnp.sum(gates * grad_gates, -1, keepdims=True))
+    ).astype(BF16)
+    d_router = mm(xl, grad_logits, TN)
+    grad_xl = d_in[:, :d] + mm(grad_logits, w_router, NT)
     grad_h1_norm, d_gain2 = rms_back(h1, scale2, norm2_gain, grad_xl)
     grad_h1 = grad_out + grad_h1_norm
-    grad_att = grad_h1.astype(bf16)
-    d_out_w = jnp.einsum("ti,td->id", att_low, grad_att, preferred_element_type=f32)
-    grad_o = jnp.einsum("td,id->ti", grad_att, w_out, preferred_element_type=f32).astype(bf16)
-    got = attention_backward(blocks, grad_o, *kept, cos_all, sin_all)
+    grad_att = grad_h1.astype(BF16)
+    d_out_w = mm(att_low, grad_att, TN)
+    grad_o = mm(grad_att, w_out, NT).astype(BF16)
+    got, mix_in, dwg_in, dwu_in, dwd_in = attention_backward(
+        blocks, grad_o, *kept, cos_all, sin_all, mix_peer, dwg, dwu, dwd
+    )
+    result = h1 + mix_own + jnp.sum(mix_in.astype(F32), 0)
+    plane = lax.rem(me, 4)
+
+    def collect(own, arrived, axis):
+        own = lax.dynamic_index_in_dim(own, plane, 0, keepdims=False).astype(F32)
+        total = own + jnp.sum(arrived.astype(F32), 0)
+        return lax.all_gather(total.astype(BF16), "seq", axis=axis, tiled=True).astype(F32)
+
+    d_gate_w = collect(dwg, dwg_in, 0)[None]
+    d_up_w = collect(dwu, dwu_in, 0)[None]
+    d_down = collect(dwd, dwd_in, 0)[None]
     grad_all = got.transpose(1, 0, 2).reshape(tok, KV * 4 * HD)
-    d_all = jnp.einsum("td,te->de", xa, grad_all, preferred_element_type=f32)
-    grad_xa = jnp.einsum("te,de->td", grad_all, w_all, preferred_element_type=f32)
-    d_model = d_all.shape[0]
-    d_heads = d_all.reshape(d_model, KV, 4 * HD)
-    d_query = d_heads[..., : 2 * HD].reshape(d_model, H * HD)
-    d_key = d_heads[..., 2 * HD : 3 * HD].reshape(d_model, KV * HD)
-    d_value = d_heads[..., 3 * HD :].reshape(d_model, KV * HD)
+    d_all = mm(xa, grad_all, TN)
+    grad_xa = mm(grad_all, w_all, NT)
+    d_heads = d_all.reshape(d, KV, 4 * HD)
+    d_query = d_heads[..., : 2 * HD].reshape(d, H * HD)
+    d_key = d_heads[..., 2 * HD : 3 * HD].reshape(d, KV * HD)
+    d_value = d_heads[..., 3 * HD :].reshape(d, KV * HD)
     grad_x_norm, d_gain1 = rms_back(xs, scale1, norm1_gain, grad_xa)
     grad_x = grad_h1 + grad_x_norm
     summed = lax.psum(
         (d_gain1, d_query, d_key, d_value, d_out_w, d_gain2, d_router), ("seq", "blk")
     )
-    expert_summed = (
-        lax.psum(d_gate_w.astype(jnp.bfloat16), "seq").astype(jnp.float32),
-        lax.psum(d_up_w.astype(jnp.bfloat16), "seq").astype(jnp.float32),
-        lax.psum(d_down.astype(jnp.bfloat16), "seq").astype(jnp.float32),
-    )
-    return (
-        result.astype(bf16)[None],
-        grad_x[None],
-        summed[0],
-        summed[1],
-        summed[2],
-        summed[3],
-        summed[4],
-        summed[5],
-        summed[6],
-        expert_summed[0],
-        expert_summed[1],
-        expert_summed[2],
-    )
+    return (result.astype(BF16)[None], grad_x[None], *summed, d_gate_w, d_up_w, d_down)
 
 
 def solution(mesh):

time: 1380 us -> 684 us (0.50)
  blocking collectives: 451 us -> 39.3 us
  waiting for transfers between devices: 458 us -> 176 us
  Pallas kernels: 162 us -> 314 us
  matrix products: 112 us -> 20.1 us
  other arithmetic: 66.9 us -> 43.1 us
  starting transfers between devices: 18.9 us -> 0.39 us
    all_to_all x2 -> x0, blocking collectives: 412 us -> none  [the longest x1 220 us: per_device(): lax.all_to_all(grad_slots.reshape(experts, cap, D), 'blk', split_axis=0,...]
    all_to_all x2 -> x0, waiting for transfers between devices: 274 us -> none  [the longest x1 149 us: per_device(): lax.all_to_all(expert_out.reshape(experts, cap, D), 'blk', split_axis=0,...]
    pallas_call x0 -> x1, Pallas kernels: none -> 97 us  [mixture(): pl.pallas_call(mixture_kernel, out_shape=(jax.ShapeDtypeStruct((tok, d),...]
    dot_general x23 -> x9, matrix products: 112 us -> 20.1 us  [mm(): return lax.dot_general(a, b, dims, preferred_element_type=F32)]
    pallas_call x1, Pallas kernels: 62.8 us -> 103 us  [attention_forward(): pl.pallas_call(functools.partial(attention_forward_kernel, blocks), out_s...]
    reduce_or x1, other arithmetic: 18.8 us -> 0.02 us  [per_device(): routed = jnp.any(chooser, 1)]
    all_to_all x2 -> x0, starting transfers between devices: 18.3 us -> none  [the longest x1 13.5 us: per_device(): lax.all_to_all(expert_out.reshape(experts, cap, D), 'blk', split_axis=0,...]
    scatter x1 -> x0, other arithmetic: 15.6 us -> none  [per_device(): grad_slots = jnp.zeros((experts * cap, D), bf16).at[slots.reshape(-1)].se...]
  transfers between devices with their start and end apart: 4 -> 4, of which waited for: 3 -> 1; matrix products, arithmetic and copies ran while one was open for 6% -> 7% of each run, Pallas kernels for 7% -> 0%
where the time goes in v2:
time: 684 us; the launch traced here: 683 us
  Pallas kernels  314 us (46%)
  waiting for transfers between devices  176 us (26%)
  local copies, waits for them, and re-layouts  73.7 us (11%)
  other arithmetic  43.1 us (6%)
  blocking collectives  39.3 us (6%)
  matrix products  20.1 us (3%)
  between operations  15.7 us (2%)
    psum x1, waiting for transfers between devices, per_device(): lax.psum((d_gain1, d_query, d_key, d_value, d_out_w, d_gain2, d_router),...  176 us
    pallas_call x1, Pallas kernels, attention_backward(): pl.pallas_call(functools.partial(attention_backward_kernel, blocks), out_...  114 us
    pallas_call x1, Pallas kernels, attention_forward(): pl.pallas_call(functools.partial(attention_forward_kernel, blocks), out_s...  103 us
    pallas_call x1, Pallas kernels, mixture(): pl.pallas_call(mixture_kernel, out_shape=(jax.ShapeDtypeStruct((tok, d),...  97 us
    psum x1, blocking collectives, per_device(): lax.psum((d_gain1, d_query, d_key, d_value, d_out_w, d_gain2, d_router),...  39.3 us
    unnamed x82, local copies, waits for them, and re-layouts  24.4 us
    dot_general x9, matrix products, mm(): return lax.dot_general(a, b, dims, preferred_element_type=F32)  20.1 us
  transfers between devices with their start and end apart: 4, of which 1 were waited for; matrix products, arithmetic and copies ran while one was open for 7% of the time, Pallas kernels for 0%

profile of v2, /device:TPU:0, one launch (start us, length us, event | category | flops | bytes accessed | tf_op | source)
XLA Modules:
  0.0 682.8 jit_solution(5901011581796104634)
XLA Ops:
  8.1 1.4 fusion.7
  10.0 1.5 copy.88
  11.5 1.8 copy.91
  13.3 1.5 copy.89
  14.7 1.8 copy.92
  16.5 3.9 copy.87
  20.4 3.9 copy.90
  24.3 5.2 pad_maximum_fusion
  29.5 6.5 copy.93
  36.0 3.5 fusion
  39.6 1.2 slice.116
  40.7 1.0 slice_bitcast_fusion.1
  43.9 1.6 dynamic-slice_bitcast_fusion
  46.3 0.8 mul.203
  47.9 0.9 slice_bitcast_fusion.3
  49.5 1.5 mul.198
  51.0 1.7 copy.96
  52.7 1.3 copy.97
  54.0 1.3 slice_negate_fusion.1
  55.3 1.1 pad_maximum_fusion.2
  56.3 2.5 copy.100
  61.2 0.9 copy-done.15
  62.4 1.6 scatter.4
  63.9 1.1 pad_maximum_fusion.1.pay
  65.0 102.8 %attention_forward.1 = (bf16[256,1024]{1,0:T(8,128)(2,1)}, bf16[8,512,128]{2,1,0:T(8,128)(2,1)}, bf16[8,128,512]{2,1,0:T(8,128)(2,1)}, bf16[8,256,128]{2,1,0:T(8...) custom-call(bf16[8,272,256]{2,1,0:T(8,128)(2,1)} %pad_maximum_fusion, ...), custom_call_target="tpu_custom_call" | custom-call | tf_op jit(solution)/shard_map/attention_forward/pallas_call | solution.py:341
  167.8 1.9 multiply_reduce_fusion.2
  172.5 1.9 fusion.25.x_ref
  174.4 97.0 %mixture.1 = (f32[256,1024]{1,0:T(8,128)}, bf16[3,256,1024]{2,1,0:T(8,128)(2,1)}, f32[256,1152]{1,0:T(8,128)}, bf16[4,512,512]{2,1,0:T(8,128)(2,1)}, bf16[4,512,...) custom-call(bf16[256,1152]{1,0:T(8,128)(2,1)} %fusion.25.x_ref, bf16[256,1024]{1,0:T(8,128)(2,1)} %bitcast.128, ...), custom_call_target="tpu_custom_call" | custom-call | tf_op jit(solution)/shard_map/mixture/pallas_call | solution.py:878
  271.4 1.2 multiply_reduce_fusion.3
  272.6 1.1 multiply_convert_fusion.2
  273.7 1.7 multiply_reduce_fusion
  275.8 1.0 copy-done.2
  276.7 1.6 convolution_convert_fusion.do_ref
  278.3 114.3 %attention_backward.1 = (bf16[8,256,256]{2,1,0:T(8,128)(2,1)}, bf16[3,256,1024]{2,1,0:T(8,128)(2,1)}, bf16[3,512,512]{2,1,0:T(8,128)(2,1)}, bf16[3,512,512]{2,1,0:T(8,128)(2,1)}, bf16[3,256,1024]{2,1,0:T(8,128)(2,1)}) custom-call(bf16[256,1024]{1,0:T(8,128)(2,1)} %convolution_convert_fusion.do_ref, bf16[8,512,128]{2,1,0:T(8,128)(2,1)} %get-tuple-element.52.kv_ref, ...), custom_call_target="tpu_custom_call" | custom-call | tf_op jit(solution)/shard_map/attention_backward/pallas_call | solution.py:607
  392.7 1.8 convert_reduce_fusion.2
  394.4 2.0 fusion.22
  396.5 1.8 convert_reduce_fusion.1
  398.3 2.0 fusion.21
  400.6 1.9 convert_reduce_fusion
  402.5 2.1 fusion.20
  404.7 1.5 copy.108
  406.2 1.4 fusion.23
  407.6 2.3 slice.96
  409.9 2.3 fusion.38
  412.2 3.1 copy.111
  415.3 2.9 copy.110
  418.1 5.5 copy.109
  423.6 0.8 fusion.40
  424.5 3.8 fusion.28
  428.3 5.2 fusion.14
  433.5 39.3 %all-reduce.1 = (f32[1024]{0:T(1024)}, f32[1024]{0:T(1024)}) all-reduce(f32[1024]{0:T(1024)S(1)} %get-tuple-element.68, f32[1024]{0:T(1024)S(1)} %get-tuple-element.66), channel_id=1, replica_groups=mesh['seq'=2,'blk'=16] {'seq','blk'}, use_global_device_ids=true, to_apply=%region_12.13 | all-reduce | flops 2048 | bytes 16384 | tf_op jit(solution)/shard_map/psum | solution.py:1342
  472.8 1.9 convert_reduce_fusion.3
  474.8 1.0 fusion.26
  476.0 1.3 fusion.11
  477.3 2.9 bitcast_convert_fusion.2
  480.2 2.8 bitcast_convert_fusion.1
  483.0 2.8 bitcast_convert_fusion
  485.8 176.4 %all-reduce.5.cloned.1.call-done = (f32[1024,1024]{1,0:T(8,128)}, f32[1024,512]{1,0:T(8,128)}, f32[1024,512]{1,0:T(8,128)}, f32[1024,1024]{1,0:T(8,128)}, f32[1024,16]{0,1:T(8,128)}) async-done(((f32[1024,1024]{1,0:T(8,128)}, f32[1024,512]{1,0:T(8,128)}, f32[1024,512]{1,0:T(8,128)}, f32[1024,1024]{1,0:T(8,128)}, f32[1024,16]{0,1:T(8,128)}), (f32[1024,1024]{1,0:T(8,128)}, f32[1024,512]{1,0:T(8,128)}, ...) | async-done | bytes 12648464 | tf_op jit(solution)/shard_map/psum | solution.py:1342
  662.2 4.9 copy.119
  667.2 1.3 copy.120
  668.5 1.0 copy-done.16
  669.5 1.3 copy.121
  670.8 1.6 copy-done.13
  672.5 2.1 copy.122
  (112 shorter events, 12.3 us)
Async XLA Ops:
  8.0 159.8 %copy-start = (bf16[1024,1024]{1,0:T(8,128)(2,1)S(1)}, bf16[1024,1024]{1,0:T(8,128)(2,1)}, u32[]{:S(2)}) copy-start(bf16[1024,1024]{1,0:T(8,128)(2,1)} %param.27) | copy-start | bytes 6291460
  8.0 469.3 %all-gather.4.cloned.1.call-start = ((), (), s32[]{:S(2)}) async-start(), calls=%async_computation | async-start | bytes 1572864 | tf_op jit(solution)/shard_map/all_gather | solution.py:1328
  10.0 26.0 %copy-start.30 = (f32[256]{0:T(256)}, f32[256]{0:T(256)S(1)}, u32[]{:S(2)}) copy-start(f32[256]{0:T(256)S(1)} %get-tuple-element.84) | copy-start | bytes 3076
  29.5 6.5 copy-start.7
  29.5 6.5 copy-start.27
  39.5 2.2 copy-start.4
  40.7 1.1 copy-start.36
  40.7 2.3 copy-start.26
  40.7 2.3 copy-start.32
  41.8 10.9 %slice-start = ((f32[256,8,256]{2,0,1:T(8,128)}), f32[256,8,128]{2,0,1:T(8,128)S(1)}, s32[]{:S(2)}) async-start(f32[256,8,256]{2,0,1:T(8,128)} %copy-done.4), calls=%async_computation.4 | async-start | bytes 2097152 | tf_op jit(solution)/shard_map/slice | solution.py:1273
  55.3 3.6 copy-start.6
  58.9 0.7 copy-start.35
  58.9 1.6 copy-start.5
  59.6 1.4 copy-start.14
  59.6 1.4 copy-start.21
  59.6 1.4 copy-start.22
  61.0 1.0 copy-start.15
  65.0 102.8 %copy-start.8 = (bf16[1,256,1024]{2,1,0:T(8,128)(2,1)S(1)}, bf16[1,256,1024]{2,1,0:T(8,128)(2,1)}, u32[]{:S(2)}) copy-start(bf16[1,256,1024]{2,1,0:T(8,128)(2,1)} %param.19) | copy-start | bytes 1572868
  167.8 3.0 copy-start.25
  167.8 4.0 copy-start.23
  169.7 2.5 copy-start.20
  170.3 0.6 copy-start.28
  171.0 0.8 copy-start.10
  174.4 99.3 %copy-start.29 = (f32[256]{0:T(256)S(1)}, f32[256]{0:T(256)}, u32[]{:S(2)}) copy-start(f32[256]{0:T(256)} %copy-done.28) | copy-start | bytes 3076
  271.4 4.0 copy-start.12
  271.4 4.0 copy-start.34
  275.8 1.0 copy-start.2
  396.4 83.7 %all-gather.6.cloned.1.call-start = ((), (), s32[]{:S(2)}) async-start(), calls=%async_computation.1 | async-start | bytes 1572864 | tf_op jit(solution)/shard_map/all_gather | solution.py:1328
  400.3 82.7 %all-gather.8.cloned.1.call-start = ((), (), s32[]{:S(2)}) async-start(), calls=%async_computation.2 | async-start | bytes 1572864 | tf_op jit(solution)/shard_map/all_gather | solution.py:1328
  402.5 3.7 copy-start.9
  402.5 3.7 copy-start.31
  404.6 257.6 %all-reduce.5.cloned.1.call-start = ((), (), s32[]{:S(2)}) async-start(), calls=%async_computation.3 | async-start | bytes 25296896 | tf_op jit(solution)/shard_map/psum | solution.py:1342
  418.1 5.5 copy-start.11
  418.1 6.4 copy-start.3
  472.8 2.0 copy-start.18
  474.7 1.3 copy-start.19
  474.7 1.3 copy-start.33
  662.2 4.9 copy-start.17
  667.2 2.3 copy-start.16
  669.5 2.9 copy-start.13
  672.5 2.1 copy-start.24
  672.5 3.2 copy-start.1
Sparse Core Ops, SparseCore 0:
  396.6 5.7 all-gather.3
  403.9 10.1 all-gather.5
  415.7 10.1 all-gather.7
Sparse Core Ops, SparseCore 1:
  428.4 233.8 all-reduce.4

commit v3 on v2

--- a/solution.py
+++ b/solution.py
@@ -79,12 +79,20 @@
 
 def attention_forward_kernel(
     blocks,
-    pay,
+    x_ref,
+    gain_ref,
+    wq_ref,
+    wk_ref,
+    wv_ref,
+    seg_ref,
+    cos_ref,
+    sin_ref,
     g_ref,
     wg_ref,
     wu_ref,
     wd_ref,
     o_ref,
+    xa_ref,
     kv_ref,
     kvt_ref,
     q_ref,
@@ -94,10 +102,13 @@
     wg_all,
     wu_all,
     wd_all,
+    pay,
+    turn,
     in_ref,
     other_ref,
     obuf,
     cnt,
+    turn_sem,
     send_sem,
     recv_sem,
     fsend_sem,
@@ -117,6 +128,34 @@
     steps = blocks // 2
     sigma = me_b // KV
     kappa = lax.rem(me_b, KV)
+    tables_in = [
+        pltpu.make_async_copy(src.at[me_b], turn.at[i], turn_sem.at[i])
+        for i, src in enumerate((cos_ref, sin_ref))
+    ]
+    for copy in tables_in:
+        copy.start()
+    xs = x_ref[...].astype(F32)
+    xa = (xs * rms_scale(xs) * gain_ref[...]).astype(BF16)
+    xa_ref[...] = xa
+    for copy in tables_in:
+        copy.wait()
+    cosine, sine = turn[0], turn[1]
+    low = lax.broadcasted_iota(jnp.int32, (tok, 2 * HD), 1) < HD
+    pay[:, tok:, : 2 * HD] = jnp.zeros((KV, 16, 2 * HD), BF16)
+    for m in range(KV // 2):
+        pair = slice(m * 2 * HD, (m + 1) * 2 * HD)
+        keys = mm(xa, wk_ref[:, pair])
+        keys = keys * cosine + rotate_pairs(keys) * sine
+        values = mm(xa, wv_ref[:, pair])
+        first = jnp.where(low, keys, pltpu.roll(values, HD, 1))
+        second = jnp.where(low, pltpu.roll(keys, HD, 1), values)
+        pay[2 * m, :tok, 2 * HD :] = first.astype(BF16)
+        pay[2 * m + 1, :tok, 2 * HD :] = second.astype(BF16)
+        for k in (2 * m, 2 * m + 1):
+            query = mm(xa, wq_ref[:, k * 2 * HD : (k + 1) * 2 * HD])
+            query = (query * cosine + rotate_pairs(query) * sine) * HD ** (-0.5)
+            pay[k, :tok, : 2 * HD] = query.astype(BF16)
+            pay[k, tok:, 2 * HD :] = seg_ref[...]
     greet_all(2, blocks, me_s, me_b)
 
     dest_core = lax.rem(me_b, 2)
@@ -332,8 +371,10 @@
             pass_weight(n, i).wait()
 
 
-def attention_forward(blocks, pay, g, w_gate, w_up, w_down):
-    tok = pay.shape[2]
+def attention_forward(
+    blocks, x, gain, w_query, w_key, w_value, seg, cos_all, sin_all, g, w_gate, w_up, w_down
+):
+    tok, d = x.shape
     steps = blocks // 2
     vm = pl.BlockSpec(memory_space=pltpu.VMEM)
     hbm = pl.BlockSpec(memory_space=pl.ANY)
@@ -342,6 +383,7 @@
         functools.partial(attention_forward_kernel, blocks),
         out_shape=(
             jax.ShapeDtypeStruct((tok, H * HD), BF16),
+            jax.ShapeDtypeStruct((tok, d), BF16),
             jax.ShapeDtypeStruct((steps, 2 * tok, 2 * HD), BF16),
             jax.ShapeDtypeStruct((steps, 2 * HD, 2 * tok), BF16),
             jax.ShapeDtypeStruct((steps, tok, 2 * HD), BF16),
@@ -352,13 +394,16 @@
             jax.ShapeDtypeStruct((4, *w_up.shape), BF16),
             jax.ShapeDtypeStruct((4, *w_down.shape), BF16),
         ),
-        in_specs=[vm] + [hbm] * 4,
-        out_specs=(vm,) * 6 + (hbm,) * 4,
+        in_specs=[vm] * 6 + [hbm] * 6,
+        out_specs=(vm,) * 7 + (hbm,) * 4,
         scratch_shapes=[
+            pltpu.VMEM((KV, tok + 16, 4 * HD), BF16),
+            pltpu.VMEM((2, tok, 2 * HD), F32),
             pltpu.VMEM((steps, tok + 16, 4 * HD), BF16),
             pltpu.VMEM((steps, tok + 16, 2 * HD), BF16),
             pltpu.VMEM((steps, tok, 2 * HD), BF16),
             pltpu.VMEM((8, 128), F32),
+            dma((2,)),
             dma((KV,)),
             dma((steps,)),
             dma((steps,)),
@@ -376,7 +421,7 @@
             collective_id=0, has_side_effects=True, vmem_limit_bytes=VMEM_LIMIT
         ),
         name="attention_forward",
-    )(pay, g, w_gate, w_up, w_down)
+    )(x, gain, w_query, w_key, w_value, seg, cos_all, sin_all, g, w_gate, w_up, w_down)
 
 
 def attention_backward_kernel(
@@ -922,6 +967,314 @@
     )(x, g, w_gate, w_up, w_down, g_all, wg_all, wu_all, wd_all)
 
 
+STAGES = 6
+
+
+class Summed:
+    def __init__(self, refs, send_sem, recv_sem, fin):
+        self.out, self.arrived, self.acc, self.part, self.plane_in, self.line_in = refs
+        self.send_sem, self.recv_sem, self.fin = send_sem, recv_sem, fin
+        self.me_s = lax.axis_index("seq")
+        me_b = lax.axis_index("blk")
+        self.line, self.plane = me_b // 4, lax.rem(me_b, 4)
+        self.sibling = [(1 - self.me_s, me_b)]
+        self.planes = [(self.me_s, self.line * 4 + flip(self.plane, n)) for n in (1, 2, 3)]
+        self.lines = [(self.me_s, flip(self.line, n) * 4 + self.plane) for n in (1, 2, 3)]
+        rows = fin.shape[0]
+        self.half, self.quarter, self.piece = rows // 2, rows // 8, rows // 32
+
+    def rows(self, start, size):
+        return pl.ds(pl.multiple_of(start, size), size)
+
+    def halves(self):
+        theirs = self.rows((1 - self.me_s) * self.half, self.half)
+        return theirs, self.rows(self.me_s * self.half, self.half)
+
+    def copy(self, stage, n):
+        sems = self.send_sem.at[stage, n], self.recv_sem.at[stage, n]
+        base = self.me_s * self.half
+        if stage == 0:
+            return remote(self.out, self.arrived, *sems, *self.sibling[n])
+        if stage == 1:
+            src = self.part.at[self.rows(flip(self.plane, n + 1) * self.quarter, self.quarter)]
+            return remote(src, self.plane_in.at[n], *sems, *self.planes[n])
+        if stage == 2:
+            at = self.plane * self.quarter + flip(self.line, n + 1) * self.piece
+            src = self.part.at[self.rows(at, self.piece)]
+            return remote(src, self.line_in.at[n], *sems, *self.lines[n])
+        if stage == 3:
+            at = base + self.plane * self.quarter + self.line * self.piece
+            part = self.fin.at[self.rows(at, self.piece)]
+            return remote(part, part, *sems, *self.lines[n])
+        if stage == 4:
+            part = self.fin.at[self.rows(base + self.plane * self.quarter, self.quarter)]
+            return remote(part, part, *sems, *self.planes[n])
+        part = self.fin.at[self.rows(base, self.half)]
+        return remote(part, part, *sems, *self.sibling[n])
+
+    def start(self, stage):
+        for n in range(1) if stage in (0, 5) else (2, 0, 1):
+            self.copy(stage, n).start()
+
+    def arrive(self, stage):
+        for n in range(1 if stage in (0, 5) else 3):
+            self.copy(stage, n).wait_recv()
+
+    def pair(self):
+        self.arrive(0)
+        self.part[...] = (self.acc[...] + self.arrived[...].astype(F32)).astype(BF16)
+        self.start(1)
+
+    def over_plane(self):
+        self.arrive(1)
+        here = self.rows(self.plane * self.quarter, self.quarter)
+        total = self.part[here, :].astype(F32)
+        for n in range(3):
+            total = total + self.plane_in[n].astype(F32)
+        self.part[here, :] = total.astype(BF16)
+        self.start(2)
+
+    def over_line(self):
+        self.arrive(2)
+        at = self.plane * self.quarter + self.line * self.piece
+        total = self.part[self.rows(at, self.piece), :].astype(F32)
+        for n in range(3):
+            total = total + self.line_in[n].astype(F32)
+        self.fin[self.rows(self.me_s * self.half + at, self.piece), :] = total.astype(BF16)
+        self.start(3)
+
+    def back(self, stage):
+        self.arrive(stage)
+        self.start(stage + 1)
+
+    def finish(self):
+        self.arrive(5)
+        for stage in range(STAGES):
+            for n in range(1 if stage in (0, 5) else 3):
+                self.copy(stage, n).wait_send()
+
+
+def summed_scratch(rows, width):
+    vmem, dma = pltpu.VMEM, pltpu.SemaphoreType.DMA
+    return [
+        vmem((rows // 2, width), BF16),
+        vmem((rows // 2, width), BF16),
+        vmem((rows // 2, width), F32),
+        vmem((rows // 2, width), BF16),
+        vmem((3, rows // 8, width), BF16),
+        vmem((3, rows // 32, width), BF16),
+        dma((STAGES, 3)),
+        dma((STAGES, 3)),
+    ]
+
+
+def tail_kernel(
+    got,
+    xa_ref,
+    x_ref,
+    gain_ref,
+    dh_ref,
+    wq_ref,
+    wk_ref,
+    wv_ref,
+    ao_ref,
+    datt_ref,
+    xl_ref,
+    dlog_ref,
+    dgain2_ref,
+    eg_ref,
+    eu_ref,
+    ed_ref,
+    eg_in,
+    eu_in,
+    ed_in,
+    dx_ref,
+    gsum_ref,
+    fin_o,
+    fin_q,
+    fin_kv,
+    eg_out,
+    eu_out,
+    ed_out,
+    d_all,
+    ev,
+    edv,
+    gbuf,
+    grv,
+    load_sem,
+    esend,
+    erecv,
+    gsend,
+    grecv,
+    *summing,
+):
+    me_s = lax.axis_index("seq")
+    me_b = lax.axis_index("blk")
+    plane = lax.rem(me_b, 4)
+    tok, d = xa_ref.shape
+    sums = [
+        Summed(summing[8 * i : 8 * i + 6], *summing[8 * i + 6 : 8 * i + 8], fin)
+        for i, fin in enumerate((fin_o, fin_q, fin_kv))
+    ]
+    for_out, for_q, for_kv = sums
+    [sibling], planes, lines = for_q.sibling, for_q.planes, for_q.lines
+    barrier = pltpu.get_barrier_semaphore()
+    for place in [sibling, *planes, *lines]:
+        pl.semaphore_signal(barrier, inc=1, device_id=place, device_id_type=MESH)
+
+    experts = ((eg_ref, eg_in, ev.at[0]), (eu_ref, eu_in, ev.at[1]), (ed_ref, ed_in, edv))
+
+    def loads(i):
+        own, arrived, dst = experts[i]
+        return (
+            pltpu.make_async_copy(own.at[plane], dst.at[0], load_sem.at[i, 0]),
+            pltpu.make_async_copy(arrived, dst.at[pl.ds(1, 3)], load_sem.at[i, 1]),
+        )
+
+    for i in range(3):
+        for copy in loads(i):
+            copy.start()
+    pl.semaphore_wait(barrier, 7)
+    theirs, mine = for_q.halves()
+    for_out.out[:, :d] = mm(ao_ref[:, theirs], datt_ref[...], TN).astype(BF16)
+    for_out.out[:, d:] = mm(xl_ref[:, theirs], dlog_ref[...], TN).astype(BF16)
+    for_out.start(0)
+
+    low = lax.broadcasted_iota(jnp.int32, (tok, 2 * HD), 1) < HD
+    for m in range(KV // 2):
+        a, b = got[2 * m], got[2 * m + 1]
+        d_all[:, 2 * m * 2 * HD : (2 * m + 1) * 2 * HD] = a[:, : 2 * HD]
+        d_all[:, (2 * m + 1) * 2 * HD : (2 * m + 2) * 2 * HD] = b[:, : 2 * HD]
+        ka, kb = a[:, 2 * HD :].astype(F32), b[:, 2 * HD :].astype(F32)
+        at = H * HD + m * 2 * HD
+        d_all[:, at : at + 2 * HD] = jnp.where(low, ka, pltpu.roll(kb, HD, 1)).astype(BF16)
+        at += KV * HD
+        d_all[:, at : at + 2 * HD] = jnp.where(low, pltpu.roll(ka, HD, 1), kb).astype(BF16)
+    parts = ((for_q, slice(0, H * HD)), (for_kv, slice(H * HD, (H + 2 * KV) * HD)))
+    for item, cols in parts:
+        item.out[...] = mm(xa_ref[:, theirs], d_all[:, cols], TN).astype(BF16)
+        item.start(0)
+    for_out.acc[:, :d] = mm(ao_ref[:, mine], datt_ref[...], TN)
+    for_out.acc[:, d:] = mm(xl_ref[:, mine], dlog_ref[...], TN)
+    for_out.pair()
+    for item, cols in parts:
+        item.acc[...] = mm(xa_ref[:, mine], d_all[:, cols], TN)
+        item.pair()
+
+    grad = (
+        mm(d_all[:, : H * HD], wq_ref[...], NT)
+        + mm(d_all[:, H * HD : (H + KV) * HD], wk_ref[...], NT)
+        + mm(d_all[:, (H + KV) * HD :], wv_ref[...], NT)
+    )
+    xs = x_ref[...].astype(F32)
+    scale = rms_scale(xs)
+    scaled = grad * gain_ref[...]
+    inner = jnp.mean(scaled * xs, -1, keepdims=True)
+    dx_ref[...] = dh_ref[...] + scale * scaled - xs * scale**3 * inner
+    gbuf[0, :8, :] = jnp.sum((grad * xs * scale).reshape(tok // 8, 8, d), 0)
+    gbuf[0, 8:, :] = dgain2_ref[...]
+
+    stages = [[sibling], planes, lines]
+
+    def gain_copy(s, n):
+        at = (0, 1, 4)[s] + n
+        return remote(gbuf.at[s], grv.at[at], gsend.at[at], grecv.at[at], *stages[s][n])
+
+    def gain_stage(s):
+        for n in range(len(stages[s])):
+            gain_copy(s, n).start()
+
+    def gain_total(s):
+        total = gbuf[s]
+        for n in range(len(stages[s])):
+            gain_copy(s, n).wait_recv()
+            total = total + grv[(0, 1, 4)[s] + n]
+        return total
+
+    gain_stage(0)
+    for_out.over_plane()
+
+    outs = (eg_out, eu_out, ed_out)
+
+    def expert_swap(i):
+        rows = outs[i].shape[0] // 2
+        part = outs[i].at[pl.ds(pl.multiple_of(me_s * rows, rows), rows)]
+        return remote(part, part, esend.at[i], erecv.at[i], *sibling)
+
+    for i in range(3):
+        for copy in loads(i):
+            copy.wait()
+        terms = experts[i][2]
+        rows = outs[i].shape[0] // 2
+        total = terms[0].astype(F32)
+        for n in (1, 2, 3):
+            total = total + terms[n].astype(F32)
+        outs[i][pl.ds(pl.multiple_of(me_s * rows, rows), rows), :] = total.astype(BF16)
+        expert_swap(i).start()
+    gbuf[1] = gain_total(0)
+    gain_stage(1)
+    for_q.over_plane()
+    for_out.over_line()
+    for_kv.over_plane()
+    gbuf[2] = gain_total(1)
+    gain_stage(2)
+    for_q.over_line()
+    for_out.back(3)
+    for_kv.over_line()
+    for_q.back(3)
+    for_kv.back(3)
+    gsum_ref[...] = gain_total(2)
+    for item in sums:
+        item.back(4)
+    for item in sums:
+        item.finish()
+    for i in range(3):
+        expert_swap(i).wait()
+    for s in range(3):
+        for n in range(len(stages[s])):
+            gain_copy(s, n).wait_send()
+
+
+def tail(blocks_in, own, arrived):
+    tok, d = blocks_in[1].shape
+    ff = own[0].shape[2]
+    widths = (d + 128, H * HD, 2 * KV * HD)
+    vm = pl.BlockSpec(memory_space=pltpu.VMEM)
+    hbm = pl.BlockSpec(memory_space=pl.ANY)
+    dma = pltpu.SemaphoreType.DMA
+    vmem = pltpu.VMEM
+    return pl.pallas_call(
+        tail_kernel,
+        out_shape=(
+            jax.ShapeDtypeStruct((tok, d), F32),
+            jax.ShapeDtypeStruct((16, d), F32),
+            *(jax.ShapeDtypeStruct((d, width), BF16) for width in widths),
+            jax.ShapeDtypeStruct((d, ff), BF16),
+            jax.ShapeDtypeStruct((d, ff), BF16),
+            jax.ShapeDtypeStruct((ff, d), BF16),
+        ),
+        in_specs=[vm] * len(blocks_in) + [hbm] * 6,
+        out_specs=(vm,) * 8,
+        scratch_shapes=[
+            vmem((tok, (H + 2 * KV) * HD), BF16),
+            vmem((2, 4, d // 2, ff), BF16),
+            vmem((4, ff // 2, d), BF16),
+            vmem((3, 16, d), F32),
+            vmem((7, 16, d), F32),
+            dma((3, 2)),
+            dma((3,)),
+            dma((3,)),
+            dma((7,)),
+            dma((7,)),
+            *(ref for width in widths for ref in summed_scratch(d, width)),
+        ],
+        compiler_params=pltpu.CompilerParams(
+            collective_id=3, has_side_effects=True, vmem_limit_bytes=VMEM_LIMIT
+        ),
+        name="tail",
+    )(*blocks_in, *own, *arrived)
+
+
 D = 1024
 HIGH = lax.Precision.HIGHEST
 
@@ -1214,13 +1567,6 @@
     )
 
 
-def by_head(w_query, w_key, w_value):
-    d = w_query.shape[0]
-    return jnp.concatenate(
-        [w_query.reshape(d, KV, 2 * HD), w_key.reshape(d, KV, HD), w_value.reshape(d, KV, HD)], -1
-    ).reshape(d, KV * 4 * HD)
-
-
 def tables(length):
     half = HD // 2
     freq = np.exp(-math.log(10000.0) * np.arange(half, dtype=np.float32) * 2.0 / HD).astype(np.float32)
@@ -1245,7 +1591,6 @@
     w_down,
     cotangent,
 ):
-    scale = HD ** (-0.5)
     xs = tokens[0].astype(F32)
     tok, d = xs.shape
     blocks = lax.axis_size("blk")
@@ -1253,39 +1598,24 @@
     cos_np, sin_np = tables(tok * blocks)
     cos_all = jnp.asarray(cos_np.reshape(blocks, tok, 2 * HD))
     sin_all = jnp.asarray(sin_np.reshape(blocks, tok, 2 * HD))
-    me = lax.axis_index("blk")
-    me_s = lax.axis_index("seq")
-    cosine = lax.dynamic_index_in_dim(cos_all, me, 0, keepdims=False)[:, None, :]
-    sine = lax.dynamic_index_in_dim(sin_all, me, 0, keepdims=False)[:, None, :]
-    scale1 = rms_scale(xs)
-    xa = (xs * scale1 * norm1_gain).astype(BF16)
-    w_all = by_head(w_query, w_key, w_value)
-    qkv = mm(xa, w_all).reshape(tok, KV, 4 * HD)
-
-    def turned(u):
-        parts = u.reshape(tok, KV, -1, HD)
-        return (
-            parts * cosine[:, :, None, :HD] + rotate_half(parts) * sine[:, :, None, :HD]
-        ).reshape(u.shape)
-
-    pay = jnp.concatenate(
-        [
-            turned(qkv[..., : 2 * HD]) * scale,
-            turned(qkv[..., 2 * HD : 3 * HD]),
-            qkv[..., 3 * HD :],
-        ],
-        -1,
-    ).astype(BF16)
-    seg = (
-        jnp.zeros((16, 4 * HD), BF16)
-        .at[:2, 2 * HD :]
-        .set(segments[0].astype(BF16).reshape(2, tok // 2))
-    )
-    pay = jnp.concatenate(
-        [pay.transpose(1, 0, 2), jnp.broadcast_to(seg[None], (KV, 16, 4 * HD))], 1
-    )
+    seg = jnp.pad(segments[0].astype(BF16).reshape(2, tok // 2), ((0, 14), (0, 0)))
+    gain1 = norm1_gain[None]
     g_low = cotangent[0]
-    att_low, *kept = attention_forward(blocks, pay, g_low, w_gate[0], w_up[0], w_down[0])
+    att_low, xa, *kept = attention_forward(
+        blocks,
+        tokens[0],
+        gain1,
+        w_query,
+        w_key,
+        w_value,
+        seg,
+        cos_all,
+        sin_all,
+        g_low,
+        w_gate[0],
+        w_up[0],
+        w_down[0],
+    )
     kept, shared = kept[:5], kept[5:]
 
     h1 = xs + mm(att_low, w_out)
@@ -1309,40 +1639,48 @@
     grad_logits = (
         gates * (grad_gates - jnp.sum(gates * grad_gates, -1, keepdims=True))
     ).astype(BF16)
-    d_router = mm(xl, grad_logits, TN)
     grad_xl = d_in[:, :d] + mm(grad_logits, w_router, NT)
-    grad_h1_norm, d_gain2 = rms_back(h1, scale2, norm2_gain, grad_xl)
+    grad_h1_norm, unused = rms_back(h1, scale2, norm2_gain, grad_xl)
+    gain2_terms = jnp.sum((grad_xl * h1 * scale2).reshape(tok // 8, 8, d), 0)
     grad_h1 = grad_out + grad_h1_norm
     grad_att = grad_h1.astype(BF16)
-    d_out_w = mm(att_low, grad_att, TN)
     grad_o = mm(grad_att, w_out, NT).astype(BF16)
-    got, mix_in, dwg_in, dwu_in, dwd_in = attention_backward(
+    got, mix_in, *arrived = attention_backward(
         blocks, grad_o, *kept, cos_all, sin_all, mix_peer, dwg, dwu, dwd
     )
     result = h1 + mix_own + jnp.sum(mix_in.astype(F32), 0)
-    plane = lax.rem(me, 4)
-
-    def collect(own, arrived, axis):
-        own = lax.dynamic_index_in_dim(own, plane, 0, keepdims=False).astype(F32)
-        total = own + jnp.sum(arrived.astype(F32), 0)
-        return lax.all_gather(total.astype(BF16), "seq", axis=axis, tiled=True).astype(F32)
-
-    d_gate_w = collect(dwg, dwg_in, 0)[None]
-    d_up_w = collect(dwu, dwu_in, 0)[None]
-    d_down = collect(dwd, dwd_in, 0)[None]
-    grad_all = got.transpose(1, 0, 2).reshape(tok, KV * 4 * HD)
-    d_all = mm(xa, grad_all, TN)
-    grad_xa = mm(grad_all, w_all, NT)
-    d_heads = d_all.reshape(d, KV, 4 * HD)
-    d_query = d_heads[..., : 2 * HD].reshape(d, H * HD)
-    d_key = d_heads[..., 2 * HD : 3 * HD].reshape(d, KV * HD)
-    d_value = d_heads[..., 3 * HD :].reshape(d, KV * HD)
-    grad_x_norm, d_gain1 = rms_back(xs, scale1, norm1_gain, grad_xa)
-    grad_x = grad_h1 + grad_x_norm
-    summed = lax.psum(
-        (d_gain1, d_query, d_key, d_value, d_out_w, d_gain2, d_router), ("seq", "blk")
-    )
-    return (result.astype(BF16)[None], grad_x[None], *summed, d_gate_w, d_up_w, d_down)
+    blocks_in = (
+        got,
+        xa,
+        tokens[0],
+        gain1,
+        grad_h1,
+        w_query,
+        w_key,
+        w_value,
+        att_low,
+        grad_att,
+        xl,
+        jnp.pad(grad_logits, ((0, 0), (0, 128 - experts))),
+        gain2_terms,
+    )
+    grad_x, gains, d_out, d_query, d_kv, d_gate_w, d_up_w, d_down = tail(
+        blocks_in, (dwg, dwu, dwd), arrived
+    )
+    return (
+        result.astype(BF16)[None],
+        grad_x[None],
+        jnp.sum(gains[:8], 0),
+        d_query.astype(F32),
+        d_kv[:, : KV * HD].astype(F32),
+        d_kv[:, KV * HD :].astype(F32),
+        d_out[:, :d].astype(F32),
+        jnp.sum(gains[8:], 0),
+        d_out[:, d : d + experts].astype(F32),
+        d_gate_w[None].astype(F32),
+        d_up_w[None].astype(F32),
+        d_down[None].astype(F32),
+    )
 
 
 def solution(mesh):

time: 684 us -> 460 us (0.67)
  waiting for transfers between devices: 176 us -> 0 us
  Pallas kernels: 314 us -> 421 us
  local copies, waits for them, and re-layouts: 73.7 us -> 4.98 us
  blocking collectives: 39.3 us -> 0 us
  other arithmetic: 43.1 us -> 27.8 us
  between operations: 15.7 us -> 0.84 us
  matrix products: 20.1 us -> 5.3 us
    psum x1 -> x0, waiting for transfers between devices: 176 us -> none  [per_device(): lax.psum((d_gain1, d_query, d_key, d_value, d_out_w, d_gain2, d_router),...]
    pallas_call x0 -> x1, Pallas kernels: none -> 101 us  [tail(): pl.pallas_call(tail_kernel, out_shape=(jax.ShapeDtypeStruct((tok, d), F32...]
    psum x1 -> x0, blocking collectives: 39.3 us -> none  [per_device(): lax.psum((d_gain1, d_query, d_key, d_value, d_out_w, d_gain2, d_router),...]
    unnamed x82 -> x32, local copies, waits for them, and re-layouts: 24.4 us -> 3.41 us
    reshape x7 -> x0, local copies, waits for them, and re-layouts: 19.9 us -> none  [the longest x1 5.49 us: per_device(): d_query = d_heads[..., :2 * HD].reshape(d, H * HD)]
    dot_general x9 -> x4, matrix products: 20.1 us -> 5.3 us  [mm(): return lax.dot_general(a, b, dims, preferred_element_type=F32)]
    broadcast_in_dim x5 -> x0, other arithmetic: 10.6 us -> none  [the longest x1 2.88 us: per_device(): d_gate_w = collect(dwg, dwg_in, 0)[None]]
    convert_element_type x3 -> x8, other arithmetic: 6.11 us -> 16.6 us  [the longest x1 4.16 us: per_device(): d_out[:, :d].astype(F32)]
  transfers between devices with their start and end apart: 4 -> 0, of which waited for: 1 -> 0; matrix products, arithmetic and copies ran while one was open for 7% -> 0% of each run, Pallas kernels for 0% -> 0%
where the time goes in v3:
time: 460 us
  Pallas kernels  421 us (92%)
  other arithmetic  27.8 us (6%)
  matrix products  5.3 us (1%)
  local copies, waits for them, and re-layouts  4.98 us (1%)
    pallas_call x1, Pallas kernels, attention_backward(): pl.pallas_call(functools.partial(attention_backward_kernel, blocks), out_...  114 us
    pallas_call x1, Pallas kernels, attention_forward(): pl.pallas_call(functools.partial(attention_forward_kernel, blocks), out_s...  108 us
    pallas_call x1, Pallas kernels, tail(): pl.pallas_call(tail_kernel, out_shape=(jax.ShapeDtypeStruct((tok, d), F32...  101 us
    pallas_call x1, Pallas kernels, mixture(): pl.pallas_call(mixture_kernel, out_shape=(jax.ShapeDtypeStruct((tok, d),...  97.1 us

profile of v3, /device:TPU:0, one launch (start us, length us, event | category | flops | bytes accessed | tf_op | source)
XLA Modules:
  0.0 459.6 jit_solution(13420623536762140120)
XLA Ops:
  0.6 0.0 copy-start
  0.7 0.8 convert_reduce_fusion.1
  1.5 0.6 pad.11.seg_ref
  2.1 0.7 fusion.3
  2.8 0.7 select_reduce_fusion
  3.6 0.1 copy.40
  3.7 0.1 copy.42
  3.8 0.0 copy-start.4
  3.8 108.2 %attention_forward.1 = (bf16[256,1024]{1,0:T(8,128)(2,1)}, bf16[256,1024]{1,0:T(8,128)(2,1)}, bf16[8,512,128]{2,1,0:T(8,128)(2,1)}, bf16[8,128,512]{2,1,0:T(8,12...) custom-call(bf16[256,1024]{1,0:T(8,128)(2,1)} %bitcast.36, ...), custom_call_target="tpu_custom_call" | custom-call | tf_op jit(solution)/shard_map/attention_forward/pallas_call | solution.py:382
  112.0 0.0 copy-done
  112.0 0.0 copy-done.4
  112.1 0.0 copy-start.14
  112.1 0.0 copy-start.13
  112.1 1.9 multiply_reduce_fusion.1
  114.0 0.0 copy-done.14
  114.0 0.2 multiply_convert_fusion.xl_ref
  114.1 0.0 copy-start.2
  114.1 0.8 copy-done.2
  114.9 0.0 copy-done.13
  114.9 0.3 select_reduce_fusion.1
  115.2 0.1 copy.39
  115.3 0.2 fusion.5
  115.5 0.2 multiply_convert_fusion.2
  115.6 1.9 fusion.1.x_ref
  117.5 97.1 %mixture.1 = (f32[256,1024]{1,0:T(8,128)}, bf16[3,256,1024]{2,1,0:T(8,128)(2,1)}, f32[256,1152]{1,0:T(8,128)}, bf16[4,512,512]{2,1,0:T(8,128)(2,1)}, bf16[4,512,...) custom-call(bf16[256,1152]{1,0:T(8,128)(2,1)} %fusion.1.x_ref, bf16[256,1024]{1,0:T(8,128)(2,1)} %bitcast.35, ...), custom_call_target="tpu_custom_call" | custom-call | tf_op jit(solution)/shard_map/mixture/pallas_call | solution.py:923
  214.7 1.1 multiply_reduce_fusion.2
  215.8 1.1 multiply_convert_fusion.1
  216.9 0.0 copy-start.3
  216.9 1.6 multiply_reduce_fusion
  218.5 0.7 pad.13.dlog_ref
  219.2 0.8 bitcast_reduce_fusion.dgain2_ref
  220.0 0.0 copy-done.3
  220.0 1.3 fusion.6
  221.4 0.0 copy-start.7
  221.4 1.5 convolution_convert_fusion.do_ref
  222.9 114.5 %attention_backward.1 = (bf16[8,256,256]{2,1,0:T(8,128)(2,1)}, bf16[3,256,1024]{2,1,0:T(8,128)(2,1)}, bf16[3,512,512]{2,1,0:T(8,128)(2,1)}, bf16[3,512,512]{2,1,0:T(8,128)(2,1)}, bf16[3,256,1024]{2,1,0:T(8,128)(2,1)}) custom-call(bf16[256,1024]{1,0:T(8,128)(2,1)} %convolution_convert_fusion.do_ref, bf16[8,512,128]{2,1,0:T(8,128)(2,1)} %get-tuple-element.49.kv_ref, ...), custom_call_target="tpu_custom_call" | custom-call | tf_op jit(solution)/shard_map/attention_backward/pallas_call | solution.py:652
  337.4 0.0 copy-done.7
  337.4 0.0 copy-start.8
  337.4 1.9 convert_reduce_fusion
  339.3 0.0 copy-done.8
  339.3 1.0 fusion.2
  340.3 100.9 %tail.1 = (f32[256,1024]{1,0:T(8,128)}, f32[16,1024]{1,0:T(8,128)}, bf16[1024,1152]{1,0:T(8,128)(2,1)}, bf16[1024,1024]{1,0:T(8,128)(2,1)}, bf16[1024,1024]{1,0:...) custom-call(bf16[8,256,256]{2,1,0:T(8,128)(2,1)} %get-tuple-element.59.got, ...), custom_call_target="tpu_custom_call" | custom-call | tf_op jit(solution)/shard_map/tail/pallas_call | solution.py:1246
  441.2 1.4 slice_reduce_fusion
  442.6 1.0 slice_convert_fusion.3
  443.6 0.8 copy.44
  444.4 0.0 copy-start.9
  444.4 4.2 slice_convert_fusion
  448.6 0.0 copy-done.9
  448.6 0.0 copy-start.6
  448.6 1.6 bitcast_convert_fusion
  450.2 0.8 copy-done.6
  450.9 0.0 copy-start.5
  450.9 2.5 convert_element_type.83
  453.4 0.0 copy-done.5
  453.4 0.0 copy-start.11
  453.4 0.0 copy-start.12
  453.4 2.6 slice_convert_fusion.1
  456.0 0.0 copy-done.11
  456.0 0.0 copy-done.12
  456.0 0.0 copy-start.10
  456.1 2.6 bitcast_convert_fusion.1
  458.7 0.0 copy-done.10
  458.7 1.0 copy.46
  459.6 0.0 copy-done.1
  (3 shorter events, 0.0 us)
Async XLA Ops:
  0.6 111.4 %copy-start = (bf16[1024,1024]{1,0:T(8,128)(2,1)S(1)}, bf16[1024,1024]{1,0:T(8,128)(2,1)}, u32[]{:S(2)}) copy-start(bf16[1024,1024]{1,0:T(8,128)(2,1)} %param.25) | copy-start | bytes 6291460
  3.8 108.3 %copy-start.4 = (bf16[1,256,1024]{2,1,0:T(8,128)(2,1)S(1)}, bf16[1,256,1024]{2,1,0:T(8,128)(2,1)}, u32[]{:S(2)}) copy-start(bf16[1,256,1024]{2,1,0:T(8,128)(2,1)} %param.17) | copy-start | bytes 1572868
  112.1 1.9 copy-start.14
  112.1 2.9 copy-start.13
  114.1 0.8 copy-start.2
  216.9 3.2 copy-start.3
  221.4 116.0 %copy-start.7 = (bf16[256,1024]{1,0:T(8,128)(2,1)}, bf16[256,1024]{1,0:T(8,128)(2,1)S(1)}, u32[]{:S(2)}) copy-start(bf16[256,1024]{1,0:T(8,128)(2,1)S(1)} %get-tuple-element.110.datt_ref) | copy-start | bytes 1572868
  337.4 1.9 copy-start.8
  444.4 4.2 copy-start.9
  448.6 2.3 copy-start.6
  450.9 2.5 copy-start.5
  453.4 2.6 copy-start.11
  453.4 2.6 copy-start.12
  456.0 2.6 copy-start.10
  456.0 3.6 copy-start.1

commit v4 on v3

--- a/solution.py
+++ b/solution.py
@@ -19,6 +19,8 @@
 BF16 = jnp.bfloat16
 MESH = pl.DeviceIdType.MESH
 VMEM_LIMIT = 60 * 2**20
+GRAD_STEPS = (1, 4, 6)
+HOP_STEP = 4
 NT = (((1,), (1,)), ((), ()))
 TN = (((0,), (0,)), ((), ()))
 
@@ -75,6 +77,107 @@
 
 def stacked_heads(wide):
     return jnp.concatenate([wide[:HD], wide[HD:]], axis=1)
+
+
+STAGES = 6
+
+
+class Summed:
+    def __init__(self, refs, send_sem, recv_sem, fin):
+        self.out, self.arrived, self.acc, self.part, self.plane_in, self.line_in = refs
+        self.send_sem, self.recv_sem, self.fin = send_sem, recv_sem, fin
+        self.me_s = lax.axis_index("seq")
+        me_b = lax.axis_index("blk")
+        self.line, self.plane = me_b // 4, lax.rem(me_b, 4)
+        self.sibling = [(1 - self.me_s, me_b)]
+        self.planes = [(self.me_s, self.line * 4 + flip(self.plane, n)) for n in (1, 2, 3)]
+        self.lines = [(self.me_s, flip(self.line, n) * 4 + self.plane) for n in (1, 2, 3)]
+        rows = fin.shape[0]
+        self.half, self.quarter, self.piece = rows // 2, rows // 8, rows // 32
+
+    def rows(self, start, size):
+        return pl.ds(pl.multiple_of(start, size), size)
+
+    def halves(self):
+        theirs = self.rows((1 - self.me_s) * self.half, self.half)
+        return theirs, self.rows(self.me_s * self.half, self.half)
+
+    def copy(self, stage, n):
+        sems = self.send_sem.at[stage, n], self.recv_sem.at[stage, n]
+        base = self.me_s * self.half
+        if stage == 0:
+            return remote(self.out, self.arrived, *sems, *self.sibling[n])
+        if stage == 1:
+            src = self.part.at[self.rows(flip(self.plane, n + 1) * self.quarter, self.quarter)]
+            return remote(src, self.plane_in.at[n], *sems, *self.planes[n])
+        if stage == 2:
+            at = self.plane * self.quarter + flip(self.line, n + 1) * self.piece
+            src = self.part.at[self.rows(at, self.piece)]
+            return remote(src, self.line_in.at[n], *sems, *self.lines[n])
+        if stage == 3:
+            at = base + self.plane * self.quarter + self.line * self.piece
+            part = self.fin.at[self.rows(at, self.piece)]
+            return remote(part, part, *sems, *self.lines[n])
+        if stage == 4:
+            part = self.fin.at[self.rows(base + self.plane * self.quarter, self.quarter)]
+            return remote(part, part, *sems, *self.planes[n])
+        part = self.fin.at[self.rows(base, self.half)]
+        return remote(part, part, *sems, *self.sibling[n])
+
+    def start(self, stage):
+        for n in range(1) if stage in (0, 5) else (2, 0, 1):
+            self.copy(stage, n).start()
+
+    def arrive(self, stage):
+        for n in range(1 if stage in (0, 5) else 3):
+            self.copy(stage, n).wait_recv()
+
+    def pair(self):
+        self.arrive(0)
+        self.part[...] = (self.acc[...] + self.arrived[...].astype(F32)).astype(BF16)
+        self.start(1)
+
+    def over_plane(self):
+        self.arrive(1)
+        here = self.rows(self.plane * self.quarter, self.quarter)
+        total = self.part[here, :].astype(F32)
+        for n in range(3):
+            total = total + self.plane_in[n].astype(F32)
+        self.part[here, :] = total.astype(BF16)
+        self.start(2)
+
+    def over_line(self):
+        self.arrive(2)
+        at = self.plane * self.quarter + self.line * self.piece
+        total = self.part[self.rows(at, self.piece), :].astype(F32)
+        for n in range(3):
+            total = total + self.line_in[n].astype(F32)
+        self.fin[self.rows(self.me_s * self.half + at, self.piece), :] = total.astype(BF16)
+        self.start(3)
+
+    def back(self, stage):
+        self.arrive(stage)
+        self.start(stage + 1)
+
+    def finish(self):
+        self.arrive(5)
+        for stage in range(STAGES):
+            for n in range(1 if stage in (0, 5) else 3):
+                self.copy(stage, n).wait_send()
+
+
+def summed_scratch(rows, width):
+    vmem, dma = pltpu.VMEM, pltpu.SemaphoreType.DMA
+    return [
+        vmem((rows // 2, width), BF16),
+        vmem((rows // 2, width), BF16),
+        vmem((rows // 2, width), F32),
+        vmem((rows // 2, width), BF16),
+        vmem((3, rows // 8, width), BF16),
+        vmem((3, rows // 32, width), BF16),
+        dma((STAGES, 3)),
+        dma((STAGES, 3)),
+    ]
 
 
 def attention_forward_kernel(
@@ -121,6 +224,8 @@
     wrecv_sem,
     hsend_sem,
     hrecv_sem,
+    dsend_sem,
+    drecv_sem,
 ):
     me_s = lax.axis_index("seq")
     me_b = lax.axis_index("blk")
@@ -128,6 +233,85 @@
     steps = blocks // 2
     sigma = me_b // KV
     kappa = lax.rem(me_b, KV)
+    greet_all(2, blocks, me_s, me_b)
+    dest_core = lax.rem(me_b, 2)
+    slot = me_b // 2
+    line, plane = me_b // 4, lax.rem(me_b, 4)
+    weights = ((wg_ref, wg_all), (wu_ref, wu_all), (wd_ref, wd_all))
+
+    def along(k, step, own):
+        at = 0 if step < 0 else 1
+        return remote(
+            g_ref if own else g_all.at[k],
+            g_all.at[k],
+            gsend_sem.at[at, k],
+            grecv_sem.at[k],
+            me_s,
+            (line + step) * 4 + plane,
+        )
+
+    def pass_on(k, step, own=False):
+        @pl.when((line + step >= 0) & (line + step < 4))
+        def _():
+            along(k, step, own).start()
+
+    def pass_distance(j):
+        for step in (-1, 1):
+            k = line - step * j
+
+            @pl.when((k >= 0) & (k < 4))
+            def _():
+                pltpu.make_async_copy(g_ref, g_all.at[k], grecv_sem.at[k]).wait()
+                pass_on(k, step)
+
+    def half(ref):
+        rows = ref.shape[0] // 2
+        return ref.at[pl.ds(pl.multiple_of(me_s * rows, rows), rows)]
+
+    def share_weight(n, i):
+        own, everyone = weights[i]
+        return remote(
+            half(own),
+            half(everyone.at[plane]),
+            wsend_sem.at[n - 1, i],
+            wrecv_sem.at[n - 1, i],
+            me_s,
+            line * 4 + flip(plane, n),
+        )
+
+    def diagonal(n, i):
+        place = weights[i][1].at[flip(plane, n)]
+        rows = place.shape[0] // 2
+        start, size = me_s * rows, rows
+        if i == 2:
+            size = rows // 2
+            start = start + (n - 1) * size
+        part = place.at[pl.ds(pl.multiple_of(start, size), size)]
+        return remote(
+            part,
+            part,
+            dsend_sem.at[n - 1, i],
+            drecv_sem.at[n - 1, i],
+            me_s,
+            line * 4 + flip(plane, 3 - n),
+        )
+
+    def diagonal_in(n, i):
+        place = weights[i][1].at[flip(plane, 3)]
+        rows = place.shape[0] // 2
+        start, size = me_s * rows, rows
+        if i == 2:
+            size = rows // 2
+            start = start + (2 - n) * size
+        part = place.at[pl.ds(pl.multiple_of(start, size), size)]
+        return pltpu.make_async_copy(part, part, drecv_sem.at[2 - n, i])
+
+    def pass_weight(n, i):
+        arrived = half(weights[i][1].at[flip(plane, n)])
+        return remote(
+            arrived, arrived, hsend_sem.at[n - 1, i], hrecv_sem.at[n - 1, i], 1 - me_s, me_b
+        )
+
     tables_in = [
         pltpu.make_async_copy(src.at[me_b], turn.at[i], turn_sem.at[i])
         for i, src in enumerate((cos_ref, sin_ref))
@@ -156,44 +340,6 @@
             query = (query * cosine + rotate_pairs(query) * sine) * HD ** (-0.5)
             pay[k, :tok, : 2 * HD] = query.astype(BF16)
             pay[k, tok:, 2 * HD :] = seg_ref[...]
-    greet_all(2, blocks, me_s, me_b)
-
-    dest_core = lax.rem(me_b, 2)
-    slot = me_b // 2
-    line, plane = me_b // 4, lax.rem(me_b, 4)
-    weights = ((wg_ref, wg_all), (wu_ref, wu_all), (wd_ref, wd_all))
-
-    def share_grad(n):
-        return remote(
-            g_ref,
-            g_all.at[line],
-            gsend_sem.at[n - 1],
-            grecv_sem.at[n - 1],
-            me_s,
-            flip(line, n) * 4 + plane,
-        )
-
-    def half(ref):
-        rows = ref.shape[0] // 2
-        return ref.at[pl.ds(pl.multiple_of(me_s * rows, rows), rows)]
-
-    def share_weight(n, i):
-        own, everyone = weights[i]
-        return remote(
-            half(own),
-            half(everyone.at[plane]),
-            wsend_sem.at[n - 1, i],
-            wrecv_sem.at[n - 1, i],
-            me_s,
-            line * 4 + flip(plane, n),
-        )
-
-    def pass_weight(n, i):
-        arrived = half(weights[i][1].at[flip(plane, n)])
-        return remote(
-            arrived, arrived, hsend_sem.at[n - 1, i], hrecv_sem.at[n - 1, i], 1 - me_s, me_b
-        )
-
     def payload(n):
         k = lax.rem(me_b + n, KV)
         chip = me_s * KV + k
@@ -216,10 +362,9 @@
         return carry
 
     lax.fori_loop(0, KV, send_payload, 0)
-    for n in (1, 2, 3):
-        share_grad(n).start()
-        for i in range(3):
-            share_weight(n, i).start()
+    for i in range(3):
+        share_weight(1, (0, 2, 1)[i]).start()
+        share_weight(2, (1, 2, 0)[i]).start()
 
     def arrival(t):
         return pltpu.make_async_copy(pay.at[0], in_ref.at[t], recv_sem.at[t])
@@ -247,6 +392,37 @@
         def _():
             arrival(t + 1).wait()
             forward(t + 1).start()
+
+        @pl.when(t == GRAD_STEPS[0])
+        def _():
+            for step in (-1, 1):
+                pass_on(line, step, True)
+
+        for j in (1, 2):
+
+            @pl.when(t == GRAD_STEPS[j])
+            def _():
+                pass_distance(j)
+
+        @pl.when(t == HOP_STEP)
+        def _():
+            for n, i in ((1, 0), (2, 1)):
+                share_weight(n, i).wait_recv()
+                diagonal(n, i).start()
+                pass_weight(n, i).start()
+
+        @pl.when(t == HOP_STEP + 1)
+        def _():
+            for n, i in ((1, 2), (2, 2)):
+                share_weight(n, i).wait_recv()
+                diagonal(n, i).start()
+                pass_weight(n, i).start()
+
+        @pl.when(t == HOP_STEP + 2)
+        def _():
+            for n, i in ((1, 1), (2, 0)):
+                share_weight(n, i).wait_recv()
+                pass_weight(n, i).start()
 
         forward(t).wait_recv()
         mine = in_ref[t]
@@ -317,10 +493,13 @@
         return carry
 
     lax.fori_loop(0, steps, step, 0)
-    for n in (1, 2, 3):
-        for i in range(3):
-            share_weight(n, i).wait_recv()
-            pass_weight(n, i).start()
+    diagonal_in(2, 0).wait()
+    pass_weight(3, 0).start()
+    diagonal_in(1, 1).wait()
+    pass_weight(3, 1).start()
+    diagonal_in(1, 2).wait()
+    diagonal_in(2, 2).wait()
+    pass_weight(3, 2).start()
 
     def finish(t, carry):
         k, chip, mine = payload(t)
@@ -364,11 +543,25 @@
         return carry
 
     lax.fori_loop(0, KV, gather, 0)
+    pass_distance(3)
+    for k in range(4):
+
+        @pl.when((k <= line) & (line < 3))
+        def _():
+            along(k, 1, False).wait_send()
+
+        @pl.when((k >= line) & (line > 0))
+        def _():
+            along(k, -1, False).wait_send()
+
     for n in (1, 2, 3):
-        share_grad(n).wait()
+        for i in range(3):
+            pass_weight(n, i).wait()
+    for n in (1, 2):
         for i in range(3):
             share_weight(n, i).wait_send()
-            pass_weight(n, i).wait()
+        diagonal(n, n - 1).wait_send()
+        diagonal(n, 2).wait_send()
 
 
 def attention_forward(
@@ -410,12 +603,14 @@
             dma((steps,)),
             dma((steps,)),
             dma((KV,)),
-            dma((3,)),
-            dma((3,)),
+            dma((2, 4)),
+            dma((4,)),
+            dma((2, 3)),
+            dma((2, 3)),
             dma((3, 3)),
             dma((3, 3)),
-            dma((3, 3)),
-            dma((3, 3)),
+            dma((2, 3)),
+            dma((2, 3)),
         ],
         compiler_params=pltpu.CompilerParams(
             collective_id=0, has_side_effects=True, vmem_limit_bytes=VMEM_LIMIT
@@ -474,7 +669,7 @@
 
     def give_mix(n):
         return remote(
-            mix_ref.at[n - 1],
+            mix_ref.at[flip(line, n)],
             mix_in.at[n - 1],
             msend_sem.at[n - 1],
             mrecv_sem.at[n - 1],
@@ -514,9 +709,10 @@
         return carry
 
     lax.fori_loop(0, KV, send_grad, 0)
-    for n in (1, 2, 3):
+    for n in (2, 1):
         give_mix(n).start()
-        for i in range(3):
+    for i in range(3):
+        for n in (1, 2):
             give_weight(n, i).start()
     dkv[...] = jnp.zeros_like(dkv)
     wide = 2 * tok
@@ -635,16 +831,16 @@
         return carry
 
     lax.fori_loop(0, KV, gather, 0)
-    for n in (1, 2, 3):
+    for n in (1, 2):
         give_mix(n).wait()
         for i in range(3):
             give_weight(n, i).wait()
 
 
 def attention_backward(
-    blocks, d_o, kv, kvt, q_two, out_t, stat, cos_all, sin_all, mix, dwg, dwu, dwd
+    blocks, vectors, mix, dwg, dwu, dwd
 ):
-    tok = q_two.shape[1]
+    tok = vectors[0].shape[0]
     steps = blocks // 2
     vm = pl.BlockSpec(memory_space=pltpu.VMEM)
     hbm = pl.BlockSpec(memory_space=pl.ANY)
@@ -653,12 +849,12 @@
         functools.partial(attention_backward_kernel, blocks),
         out_shape=(
             jax.ShapeDtypeStruct((KV, tok, 4 * HD), BF16),
-            jax.ShapeDtypeStruct(mix.shape, BF16),
-            jax.ShapeDtypeStruct((3, *dwg.shape[1:]), BF16),
-            jax.ShapeDtypeStruct((3, *dwu.shape[1:]), BF16),
-            jax.ShapeDtypeStruct((3, *dwd.shape[1:]), BF16),
+            jax.ShapeDtypeStruct((2, *mix.shape[1:]), BF16),
+            jax.ShapeDtypeStruct((2, *dwg.shape[1:]), BF16),
+            jax.ShapeDtypeStruct((2, *dwu.shape[1:]), BF16),
+            jax.ShapeDtypeStruct((2, *dwd.shape[1:]), BF16),
         ),
-        in_specs=[vm] * 8 + [hbm] * 4,
+        in_specs=[vm] * len(vectors) + [hbm] * 4,
         out_specs=(vm,) + (hbm,) * 4,
         scratch_shapes=[
             pltpu.VMEM((steps, tok, 2 * HD), BF16),
@@ -672,16 +868,16 @@
             dma((steps,)),
             dma((steps,)),
             dma((KV,)),
-            dma((3,)),
-            dma((3,)),
-            dma((3, 3)),
-            dma((3, 3)),
+            dma((2,)),
+            dma((2,)),
+            dma((2, 3)),
+            dma((2, 3)),
         ],
         compiler_params=pltpu.CompilerParams(
             collective_id=1, has_side_effects=True, vmem_limit_bytes=VMEM_LIMIT
         ),
         name="attention_backward",
-    )(d_o, kv, kvt, q_two, out_t, stat, cos_all, sin_all, mix, dwg, dwu, dwd)
+    )(*vectors, mix, dwg, dwu, dwd)
 
 
 def mixture_kernel(
@@ -700,6 +896,9 @@
     dwg_out,
     dwu_out,
     dwd_out,
+    dwg_in,
+    dwu_in,
+    dwd_in,
     x_in,
     x_t,
     g_in,
@@ -726,6 +925,8 @@
     psend_sem,
     precv_sem,
     store_sem,
+    wsend_sem,
+    wrecv_sem,
 ):
     me_s = lax.axis_index("seq")
     me_b = lax.axis_index("blk")
@@ -733,8 +934,9 @@
     tok, d = g_in.shape[1:]
     ff = wg.shape[2]
     barrier = pltpu.get_barrier_semaphore()
-    places = [(me_s, flip(line, n) * 4 + plane) for n in (1, 2, 3)] + [(1 - me_s, me_b)]
-    for place in places:
+    sibling = (1 - me_s, me_b)
+    opposite = (me_s, line * 4 + flip(plane, 3))
+    for place in [(me_s, flip(line, n) * 4 + plane) for n in (1, 2, 3)] + [sibling, opposite]:
         pl.semaphore_signal(barrier, inc=1, device_id=place, device_id_type=MESH)
 
     owns = ((wg_ref, wg_all, wg), (wu_ref, wu_all, wu), (wd_ref, wd_all, wd))
@@ -750,24 +952,35 @@
         for n in (1, 2, 3):
             load_other(i, flip(plane, n)).start()
 
-    def load_grad(n):
-        src = g_ref if n == 0 else g_all.at[flip(line, n)]
-        return pltpu.make_async_copy(src, g_in.at[n], gload_sem.at[n])
-
-    for n in range(4):
-        load_grad(n).start()
-    pl.semaphore_wait(barrier, 4)
-
-    def spread(n):
+    def load_grad(k):
+        return pltpu.make_async_copy(g_all.at[k], g_in.at[k], gload_sem.at[k])
+
+    pltpu.make_async_copy(g_ref, g_in.at[line], gload_sem.at[line]).start()
+    for n in (1, 2, 3):
+        load_grad(flip(line, n)).start()
+    x_in[line] = x_ref[...]
+    pl.semaphore_wait(barrier, 5)
+
+    def along(k, step):
+        at = 0 if step < 0 else 1
         return remote(
-            x_ref, x_in.at[n], send_sem.at[n - 1], recv_sem.at[n - 1], *places[n - 1]
+            x_in.at[k],
+            x_in.at[k],
+            send_sem.at[at, k],
+            recv_sem.at[k],
+            me_s,
+            (line + step) * 4 + plane,
         )
 
-    for n in (1, 2, 3):
-        spread(n).start()
-    x_in[0] = x_ref[...]
-    for n in range(4):
-        load_grad(n).wait()
+    def pass_on(k, step):
+        @pl.when((line + step >= 0) & (line + step < 4))
+        def _():
+            along(k, step).start()
+
+    for step in (-1, 1):
+        pass_on(line, step)
+    for k in range(4):
+        load_grad(k).wait()
 
     def load_wait(e, carry):
         for i in range(3):
@@ -776,10 +989,18 @@
 
     lane = lax.broadcasted_iota(jnp.int32, (tok, 128), 1)
 
-    def block(n, carry):
-        @pl.when(n > 0)
-        def _():
-            pltpu.make_async_copy(x_ref, x_in.at[n], recv_sem.at[jnp.maximum(n - 1, 0)]).wait()
+    def place_of(j):
+        return jnp.where(line < 2, lax.rem(line + j, 4), lax.rem(line + 4 - j, 4))
+
+    def block(j, carry):
+        n = place_of(j)
+        for step in (-1, 1):
+            k = line - step * j
+
+            @pl.when((j > 0) & (k >= 0) & (k < 4))
+            def _():
+                pltpu.make_async_copy(x_ref, x_in.at[k], recv_sem.at[k]).wait()
+                pass_on(k, step)
 
         acc_o[...] = jnp.zeros_like(acc_o)
         acc_d[...] = jnp.zeros_like(acc_d)
@@ -787,7 +1008,7 @@
         rows = pl.ds(pl.multiple_of(n * tok, tok), tok)
 
         def expert(e, carry):
-            @pl.when(n == 0)
+            @pl.when(j == 0)
             def _():
                 load_wait(e, 0)
 
@@ -816,33 +1037,27 @@
 
         lax.fori_loop(0, 4, expert, 0)
 
-        @pl.when(n == 0)
+        @pl.when(j == 0)
         def _():
             mix_own[...] = acc_o[...]
             d_in[:, :d] = acc_d[...]
             d_in[:, d:] = acc_c[...]
 
-        for m in (1, 2, 3):
-
-            @pl.when(n == m)
-            def _():
-                mix_peer[m - 1] = acc_o[...].astype(BF16)
-                d_send[m - 1, :, :d] = acc_d[...].astype(BF16)
-                high = acc_c[...].astype(BF16).astype(F32)
-                rest = acc_c[...] - high
-                d_send[m - 1, :, d:] = (high + pltpu.roll(rest, 32, 1)).astype(BF16)
-                give_back(m).start()
+        @pl.when(j > 0)
+        def _():
+            mix_peer[n] = acc_o[...].astype(BF16)
+            d_send[n, :, :d] = acc_d[...].astype(BF16)
+            high = acc_c[...].astype(BF16).astype(F32)
+            rest = acc_c[...] - high
+            d_send[n, :, d:] = (high + pltpu.roll(rest, 32, 1)).astype(BF16)
+            give_back(n).start()
 
         x_t[:, rows] = jnp.transpose(x_in[n, :, :d].astype(F32)).astype(BF16)
         return carry
 
     def give_back(n):
         return remote(
-            d_send.at[n - 1],
-            d_recv.at[n - 1],
-            bsend_sem.at[n - 1],
-            brecv_sem.at[n - 1],
-            *places[n - 1],
+            d_send.at[n], d_recv.at[line], bsend_sem.at[n], brecv_sem.at[line], me_s, n * 4 + plane
         )
 
     lax.fori_loop(0, 4, block, 0)
@@ -857,14 +1072,38 @@
     def swap(i, e):
         src = (wg.at[e, pl.ds(0, half)], wu.at[e, pl.ds(0, half)], wd.at[e, pl.ds(0, dhalf)])[i]
         dst = (xg, xu, xd)[i].at[e]
-        return remote(src, dst, psend_sem.at[i, e], precv_sem.at[i, e], *places[3])
+        return remote(src, dst, psend_sem.at[i, e], precv_sem.at[i, e], *sibling)
 
     def store(i, e):
         return pltpu.make_async_copy(
             (xg, xu, xd)[i].at[e], (dwg_out, dwu_out, dwd_out)[i].at[e], store_sem.at[i, e]
         )
 
-    def give(e, carry):
+    def turn_of(n):
+        return jnp.where(
+            n == 0, flip(plane, 3), jnp.where(n == 1, flip(plane, 2), jnp.where(n == 2, flip(plane, 1), plane))
+        )
+
+    def opposed(i):
+        return remote(
+            (xg, xu, xd)[i].at[flip(plane, 3)],
+            (dwg_in, dwu_in, dwd_in)[i],
+            wsend_sem.at[i],
+            wrecv_sem.at[i],
+            *opposite,
+        )
+
+    def finished(i, n, e):
+        @pl.when(n == 0)
+        def _():
+            opposed(i).start()
+
+        @pl.when(n > 0)
+        def _():
+            store(i, e).start()
+
+    def give(n, carry):
+        e = turn_of(n)
         left = x_t[pl.ds(theirs, half), :]
         wg[e, :half, :] = mm(left, dg[e]).astype(BF16)
         swap(0, e).start()
@@ -876,41 +1115,59 @@
 
     lax.fori_loop(0, 4, give, 0)
 
-    def keep(e, carry):
+    def keep(n, carry):
+        e = turn_of(n)
+
         left = x_t[pl.ds(mine, half), :]
         own = mm(left, dg[e])
         swap(0, e).wait_recv()
         xg[e] = (own + xg[e].astype(F32)).astype(BF16)
-        store(0, e).start()
+        finished(0, n, e)
         own = mm(left, du[e])
         swap(1, e).wait_recv()
         xu[e] = (own + xu[e].astype(F32)).astype(BF16)
-        store(1, e).start()
+        finished(1, n, e)
         own = mm(hc[e, :, pl.ds(dmine, dhalf)], g_rows[...], TN)
         swap(2, e).wait_recv()
         xd[e] = (own + xd[e].astype(F32)).astype(BF16)
-        store(2, e).start()
+        finished(2, n, e)
         return carry
 
     lax.fori_loop(0, 4, keep, 0)
 
     for n in (1, 2, 3):
-        give_back(n).wait_recv()
-        d_in[:, :d] += d_recv[n - 1, :, :d].astype(F32)
-        tail = d_recv[n - 1, :, d:].astype(F32)
+        k = flip(line, n)
+        pltpu.make_async_copy(d_send.at[k], d_recv.at[k], brecv_sem.at[k]).wait()
+        d_in[:, :d] += d_recv[k, :, :d].astype(F32)
+        tail = d_recv[k, :, d:].astype(F32)
         both = tail + pltpu.roll(tail, 96, 1)
         d_in[:, d:] += jnp.where(lane < 32, both, 0.0)
     for n in (1, 2, 3):
-        spread(n).wait_send()
-        give_back(n).wait_send()
-
-    def finish(e, carry):
+        give_back(flip(line, n)).wait_send()
+    for k in range(4):
+
+        @pl.when((k <= line) & (line < 3))
+        def _():
+            along(k, 1).wait_send()
+
+        @pl.when((k >= line) & (line > 0))
+        def _():
+            along(k, -1).wait_send()
+
+    def finish(n, carry):
+        e = turn_of(n)
         for i in range(3):
             swap(i, e).wait_send()
-            store(i, e).wait()
+
+            @pl.when(n > 0)
+            def _():
+                store(i, e).wait()
+
         return carry
 
     lax.fori_loop(0, 4, finish, 0)
+    for i in range(3):
+        opposed(i).wait()
 
 
 def mixture(x, g, w_gate, w_up, w_down, g_all, wg_all, wu_all, wd_all):
@@ -924,14 +1181,17 @@
         mixture_kernel,
         out_shape=(
             jax.ShapeDtypeStruct((tok, d), F32),
-            jax.ShapeDtypeStruct((3, tok, d), BF16),
+            jax.ShapeDtypeStruct((4, tok, d), BF16),
             jax.ShapeDtypeStruct((tok, d + 128), F32),
             jax.ShapeDtypeStruct((4, d // 2, ff), BF16),
             jax.ShapeDtypeStruct((4, d // 2, ff), BF16),
             jax.ShapeDtypeStruct((4, ff // 2, d), BF16),
+            jax.ShapeDtypeStruct((d // 2, ff), BF16),
+            jax.ShapeDtypeStruct((d // 2, ff), BF16),
+            jax.ShapeDtypeStruct((ff // 2, d), BF16),
         ),
         in_specs=[vm] + [hbm] * 8,
-        out_specs=(vm, vm, vm, hbm, hbm, hbm),
+        out_specs=(vm,) * 3 + (hbm,) * 6,
         scratch_shapes=[
             vmem((4, tok, d + 128), BF16),
             vmem((d, 4 * tok), BF16),
@@ -945,127 +1205,28 @@
             vmem((tok, d), F32),
             vmem((tok, d), F32),
             vmem((tok, 128), F32),
-            vmem((3, tok, d + 128), BF16),
-            vmem((3, tok, d + 128), BF16),
+            vmem((4, tok, d + 128), BF16),
+            vmem((4, tok, d + 128), BF16),
             vmem((4, d // 2, ff), BF16),
             vmem((4, d // 2, ff), BF16),
             vmem((4, ff // 2, d), BF16),
             dma((3, 4)),
             dma((4,)),
-            dma((3,)),
-            dma((3,)),
-            dma((3,)),
-            dma((3,)),
+            dma((2, 4)),
+            dma((4,)),
+            dma((4,)),
+            dma((4,)),
             dma((3, 4)),
             dma((3, 4)),
             dma((3, 4)),
+            dma((3,)),
+            dma((3,)),
         ],
         compiler_params=pltpu.CompilerParams(
             collective_id=2, has_side_effects=True, vmem_limit_bytes=VMEM_LIMIT
         ),
         name="mixture",
     )(x, g, w_gate, w_up, w_down, g_all, wg_all, wu_all, wd_all)
-
-
-STAGES = 6
-
-
-class Summed:
-    def __init__(self, refs, send_sem, recv_sem, fin):
-        self.out, self.arrived, self.acc, self.part, self.plane_in, self.line_in = refs
-        self.send_sem, self.recv_sem, self.fin = send_sem, recv_sem, fin
-        self.me_s = lax.axis_index("seq")
-        me_b = lax.axis_index("blk")
-        self.line, self.plane = me_b // 4, lax.rem(me_b, 4)
-        self.sibling = [(1 - self.me_s, me_b)]
-        self.planes = [(self.me_s, self.line * 4 + flip(self.plane, n)) for n in (1, 2, 3)]
-        self.lines = [(self.me_s, flip(self.line, n) * 4 + self.plane) for n in (1, 2, 3)]
-        rows = fin.shape[0]
-        self.half, self.quarter, self.piece = rows // 2, rows // 8, rows // 32
-
-    def rows(self, start, size):
-        return pl.ds(pl.multiple_of(start, size), size)
-
-    def halves(self):
-        theirs = self.rows((1 - self.me_s) * self.half, self.half)
-        return theirs, self.rows(self.me_s * self.half, self.half)
-
-    def copy(self, stage, n):
-        sems = self.send_sem.at[stage, n], self.recv_sem.at[stage, n]
-        base = self.me_s * self.half
-        if stage == 0:
-            return remote(self.out, self.arrived, *sems, *self.sibling[n])
-        if stage == 1:
-            src = self.part.at[self.rows(flip(self.plane, n + 1) * self.quarter, self.quarter)]
-            return remote(src, self.plane_in.at[n], *sems, *self.planes[n])
-        if stage == 2:
-            at = self.plane * self.quarter + flip(self.line, n + 1) * self.piece
-            src = self.part.at[self.rows(at, self.piece)]
-            return remote(src, self.line_in.at[n], *sems, *self.lines[n])
-        if stage == 3:
-            at = base + self.plane * self.quarter + self.line * self.piece
-            part = self.fin.at[self.rows(at, self.piece)]
-            return remote(part, part, *sems, *self.lines[n])
-        if stage == 4:
-            part = self.fin.at[self.rows(base + self.plane * self.quarter, self.quarter)]
-            return remote(part, part, *sems, *self.planes[n])
-        part = self.fin.at[self.rows(base, self.half)]
-        return remote(part, part, *sems, *self.sibling[n])
-
-    def start(self, stage):
-        for n in range(1) if stage in (0, 5) else (2, 0, 1):
-            self.copy(stage, n).start()
-
-    def arrive(self, stage):
-        for n in range(1 if stage in (0, 5) else 3):
-            self.copy(stage, n).wait_recv()
-
-    def pair(self):
-        self.arrive(0)
-        self.part[...] = (self.acc[...] + self.arrived[...].astype(F32)).astype(BF16)
-        self.start(1)
-
-    def over_plane(self):
-        self.arrive(1)
-        here = self.rows(self.plane * self.quarter, self.quarter)
-        total = self.part[here, :].astype(F32)
-        for n in range(3):
-            total = total + self.plane_in[n].astype(F32)
-        self.part[here, :] = total.astype(BF16)
-        self.start(2)
-
-    def over_line(self):
-        self.arrive(2)
-        at = self.plane * self.quarter + self.line * self.piece
-        total = self.part[self.rows(at, self.piece), :].astype(F32)
-        for n in range(3):
-            total = total + self.line_in[n].astype(F32)
-        self.fin[self.rows(self.me_s * self.half + at, self.piece), :] = total.astype(BF16)
-        self.start(3)
-
-    def back(self, stage):
-        self.arrive(stage)
-        self.start(stage + 1)
-
-    def finish(self):
-        self.arrive(5)
-        for stage in range(STAGES):
-            for n in range(1 if stage in (0, 5) else 3):
-                self.copy(stage, n).wait_send()
-
-
-def summed_scratch(rows, width):
-    vmem, dma = pltpu.VMEM, pltpu.SemaphoreType.DMA
-    return [
-        vmem((rows // 2, width), BF16),
-        vmem((rows // 2, width), BF16),
-        vmem((rows // 2, width), F32),
-        vmem((rows // 2, width), BF16),
-        vmem((3, rows // 8, width), BF16),
-        vmem((3, rows // 32, width), BF16),
-        dma((STAGES, 3)),
-        dma((STAGES, 3)),
-    ]
 
 
 def tail_kernel(
@@ -1082,12 +1243,20 @@
     xl_ref,
     dlog_ref,
     dgain2_ref,
+    h1_ref,
+    mix_own,
+    mix_ref,
+    mix_near,
     eg_ref,
     eu_ref,
     ed_ref,
     eg_in,
     eu_in,
     ed_in,
+    eg_far,
+    eu_far,
+    ed_far,
+    res_ref,
     dx_ref,
     gsum_ref,
     fin_o,
@@ -1096,6 +1265,7 @@
     eg_out,
     eu_out,
     ed_out,
+    mix_in,
     d_all,
     ev,
     edv,
@@ -1106,6 +1276,8 @@
     erecv,
     gsend,
     grecv,
+    msend,
+    mrecv,
     *summing,
 ):
     me_s = lax.axis_index("seq")
@@ -1122,19 +1294,30 @@
     for place in [sibling, *planes, *lines]:
         pl.semaphore_signal(barrier, inc=1, device_id=place, device_id_type=MESH)
 
-    experts = ((eg_ref, eg_in, ev.at[0]), (eu_ref, eu_in, ev.at[1]), (ed_ref, ed_in, edv))
+    experts = (
+        (eg_ref, eg_in, eg_far, ev.at[0]),
+        (eu_ref, eu_in, eu_far, ev.at[1]),
+        (ed_ref, ed_in, ed_far, edv),
+    )
 
     def loads(i):
-        own, arrived, dst = experts[i]
+        own, arrived, far, dst = experts[i]
         return (
             pltpu.make_async_copy(own.at[plane], dst.at[0], load_sem.at[i, 0]),
-            pltpu.make_async_copy(arrived, dst.at[pl.ds(1, 3)], load_sem.at[i, 1]),
+            pltpu.make_async_copy(arrived, dst.at[pl.ds(1, 2)], load_sem.at[i, 1]),
+            pltpu.make_async_copy(far, dst.at[3], load_sem.at[i, 2]),
         )
 
     for i in range(3):
         for copy in loads(i):
             copy.start()
     pl.semaphore_wait(barrier, 7)
+    line = me_b // 4
+
+    far_mix = remote(mix_ref.at[flip(line, 3)], mix_in.at[2], msend, mrecv, *lines[2])
+    near_mix = pltpu.make_async_copy(mix_near, mix_in.at[pl.ds(0, 2)], load_sem.at[3, 0])
+    far_mix.start()
+    near_mix.start()
     theirs, mine = for_q.halves()
     for_out.out[:, :d] = mm(ao_ref[:, theirs], datt_ref[...], TN).astype(BF16)
     for_out.out[:, d:] = mm(xl_ref[:, theirs], dlog_ref[...], TN).astype(BF16)
@@ -1204,7 +1387,7 @@
     for i in range(3):
         for copy in loads(i):
             copy.wait()
-        terms = experts[i][2]
+        terms = experts[i][3]
         rows = outs[i].shape[0] // 2
         total = terms[0].astype(F32)
         for n in (1, 2, 3):
@@ -1226,6 +1409,12 @@
     gsum_ref[...] = gain_total(2)
     for item in sums:
         item.back(4)
+    result = h1_ref[...] + mix_own[...]
+    near_mix.wait()
+    far_mix.wait()
+    for n in range(3):
+        result = result + mix_in[n].astype(F32)
+    res_ref[...] = result.astype(BF16)
     for item in sums:
         item.finish()
     for i in range(3):
@@ -1235,7 +1424,7 @@
             gain_copy(s, n).wait_send()
 
 
-def tail(blocks_in, own, arrived):
+def tail(blocks_in, mix_peer, mix_near, own, arrived, far):
     tok, d = blocks_in[1].shape
     ff = own[0].shape[2]
     widths = (d + 128, H * HD, 2 * KV * HD)
@@ -1246,6 +1435,7 @@
     return pl.pallas_call(
         tail_kernel,
         out_shape=(
+            jax.ShapeDtypeStruct((tok, d), BF16),
             jax.ShapeDtypeStruct((tok, d), F32),
             jax.ShapeDtypeStruct((16, d), F32),
             *(jax.ShapeDtypeStruct((d, width), BF16) for width in widths),
@@ -1253,26 +1443,84 @@
             jax.ShapeDtypeStruct((d, ff), BF16),
             jax.ShapeDtypeStruct((ff, d), BF16),
         ),
-        in_specs=[vm] * len(blocks_in) + [hbm] * 6,
-        out_specs=(vm,) * 8,
+        in_specs=[vm] * len(blocks_in) + [hbm] * 11,
+        out_specs=(vm,) * 9,
         scratch_shapes=[
+            vmem((3, tok, d), BF16),
             vmem((tok, (H + 2 * KV) * HD), BF16),
             vmem((2, 4, d // 2, ff), BF16),
             vmem((4, ff // 2, d), BF16),
             vmem((3, 16, d), F32),
             vmem((7, 16, d), F32),
-            dma((3, 2)),
+            dma((4, 3)),
             dma((3,)),
             dma((3,)),
             dma((7,)),
             dma((7,)),
+            dma,
+            dma,
             *(ref for width in widths for ref in summed_scratch(d, width)),
         ],
         compiler_params=pltpu.CompilerParams(
             collective_id=3, has_side_effects=True, vmem_limit_bytes=VMEM_LIMIT
         ),
         name="tail",
-    )(*blocks_in, *own, *arrived)
+    )(*blocks_in, mix_peer, mix_near, *own, *arrived, *far)
+
+
+def widen_kernel(gains, o, q, kv, eg, eu, ed, n1, wq, wk, wv, wo, n2, wr, og, ou, od):
+    d = wq.shape[1]
+    half = wk.shape[1]
+    wq[...] = q[...].astype(F32)
+    wk[...] = kv[:, :half].astype(F32)
+    wv[...] = kv[:, half:].astype(F32)
+    wo[...] = o[:, :d].astype(F32)
+    wr[...] = o[:, d : d + wr.shape[1]].astype(F32)
+    og[0] = eg[...].astype(F32)
+    ou[0] = eu[...].astype(F32)
+    od[0] = ed[...].astype(F32)
+    n1[...] = jnp.sum(gains[:8], 0, keepdims=True)
+    n2[...] = jnp.sum(gains[8:], 0, keepdims=True)
+
+
+def widen(gains, o, q, kv, eg, eu, ed, experts):
+    d, ff = eg.shape
+    parts = 8
+
+    def block(shape):
+        return pl.BlockSpec((shape[0] // parts, shape[1]), lambda i: (i, 0))
+
+    def deep(shape):
+        return pl.BlockSpec((1, shape[0] // parts, shape[1]), lambda i: (0, i, 0))
+
+    flat = pl.BlockSpec((1, d), lambda i: (0, 0))
+    shapes = [(d, H * HD), (d, KV * HD), (d, KV * HD), (H * HD, d)]
+    return pl.pallas_call(
+        widen_kernel,
+        grid=(parts,),
+        out_shape=(
+            jax.ShapeDtypeStruct((1, d), F32),
+            *(jax.ShapeDtypeStruct(shape, F32) for shape in shapes),
+            jax.ShapeDtypeStruct((1, d), F32),
+            jax.ShapeDtypeStruct((d, experts), F32),
+            jax.ShapeDtypeStruct((1, d, ff), F32),
+            jax.ShapeDtypeStruct((1, d, ff), F32),
+            jax.ShapeDtypeStruct((1, ff, d), F32),
+        ),
+        in_specs=[pl.BlockSpec((16, d), lambda i: (0, 0))]
+        + [block(a.shape) for a in (o, q, kv, eg, eu, ed)],
+        out_specs=(
+            flat,
+            *(block(shape) for shape in shapes),
+            flat,
+            block((d, experts)),
+            deep((d, ff)),
+            deep((d, ff)),
+            deep((ff, d)),
+        ),
+        compiler_params=pltpu.CompilerParams(vmem_limit_bytes=VMEM_LIMIT),
+        name="widen",
+    )(gains, o, q, kv, eg, eu, ed)
 
 
 D = 1024
@@ -1630,7 +1878,7 @@
     gates = expo / jnp.sum(expo, -1, keepdims=True)
     combine = (rweight * gates).astype(BF16)
     sent = jnp.concatenate([xl, jnp.pad(combine, ((0, 0), (0, 128 - experts)))], 1)
-    mix_own, mix_peer, d_in, dwg, dwu, dwd = mixture(
+    mix_own, mix_peer, d_in, dwg, dwu, dwd, *far = mixture(
         sent, g_low, w_gate[0], w_up[0], w_down[0], *shared
     )
 
@@ -1645,10 +1893,15 @@
     grad_h1 = grad_out + grad_h1_norm
     grad_att = grad_h1.astype(BF16)
     grad_o = mm(grad_att, w_out, NT).astype(BF16)
-    got, mix_in, *arrived = attention_backward(
-        blocks, grad_o, *kept, cos_all, sin_all, mix_peer, dwg, dwu, dwd
-    )
-    result = h1 + mix_own + jnp.sum(mix_in.astype(F32), 0)
+    vectors = (
+        grad_o,
+        *kept,
+        cos_all,
+        sin_all,
+    )
+    got, mix_near, *arrived = attention_backward(
+        blocks, vectors, mix_peer, dwg, dwu, dwd
+    )
     blocks_in = (
         got,
         xa,
@@ -1663,23 +1916,24 @@
         xl,
         jnp.pad(grad_logits, ((0, 0), (0, 128 - experts))),
         gain2_terms,
-    )
-    grad_x, gains, d_out, d_query, d_kv, d_gate_w, d_up_w, d_down = tail(
-        blocks_in, (dwg, dwu, dwd), arrived
-    )
+        h1,
+        mix_own,
+    )
+    result, grad_x, gains, d_out, d_query, d_kv, d_gate_w, d_up_w, d_down = tail(
+        blocks_in, mix_peer, mix_near, (dwg, dwu, dwd), arrived, far
+    )
+    wide = widen(gains, d_out, d_query, d_kv, d_gate_w, d_up_w, d_down, experts)
+    d_gain1, d_query, d_key, d_value, d_out, d_gain2, *rest = wide
     return (
-        result.astype(BF16)[None],
+        result[None],
         grad_x[None],
-        jnp.sum(gains[:8], 0),
-        d_query.astype(F32),
-        d_kv[:, : KV * HD].astype(F32),
-        d_kv[:, KV * HD :].astype(F32),
-        d_out[:, :d].astype(F32),
-        jnp.sum(gains[8:], 0),
-        d_out[:, d : d + experts].astype(F32),
-        d_gate_w[None].astype(F32),
-        d_up_w[None].astype(F32),
-        d_down[None].astype(F32),
+        d_gain1[0],
+        d_query,
+        d_key,
+        d_value,
+        d_out,
+        d_gain2[0],
+        *rest,
     )
 
 

time: 460 us -> 400 us (0.87)
  Pallas kernels: 421 us -> 377 us
  other arithmetic: 27.8 us -> 9.07 us
    pallas_call x1, Pallas kernels: 114 us -> 71.2 us  [attention_backward(): pl.pallas_call(functools.partial(attention_backward_kernel, blocks), out_...]
    pallas_call x1, Pallas kernels: 108 us -> 88.9 us  [attention_forward(): pl.pallas_call(functools.partial(attention_forward_kernel, blocks), out_s...]
    convert_element_type x6 -> x0, other arithmetic: 14.4 us -> none  [the longest x1 4.16 us: per_device(): d_out[:, :d].astype(F32)]
    pallas_call x1 -> x2, Pallas kernels: 101 us -> 113 us  [the longest x1 102 us: tail(): pl.pallas_call(tail_kernel, out_shape=(jax.ShapeDtypeStruct((tok, d), BF1...]
    pallas_call x1, Pallas kernels: 97.1 us -> 103 us  [mixture(): pl.pallas_call(mixture_kernel, out_shape=(jax.ShapeDtypeStruct((tok, d),...]
where the time goes in v4:
time: 400 us; the launch traced here: 399 us
  Pallas kernels  377 us (94%)
  other arithmetic  9.07 us (2%)
  local copies, waits for them, and re-layouts  7.34 us (2%)
  matrix products  5.3 us (1%)
    pallas_call x1, Pallas kernels, mixture(): pl.pallas_call(mixture_kernel, out_shape=(jax.ShapeDtypeStruct((tok, d),...  103 us
    pallas_call x1, Pallas kernels, tail(): pl.pallas_call(tail_kernel, out_shape=(jax.ShapeDtypeStruct((tok, d), BF1...  102 us
    pallas_call x1, Pallas kernels, attention_forward(): pl.pallas_call(functools.partial(attention_forward_kernel, blocks), out_s...  88.9 us
    pallas_call x1, Pallas kernels, attention_backward(): pl.pallas_call(functools.partial(attention_backward_kernel, blocks), out_...  71.2 us
    pallas_call x1, Pallas kernels, widen(): pl.pallas_call(widen_kernel, grid=(parts,), out_shape=(jax.ShapeDtypeStru...  11.6 us

profile of v4, /device:TPU:0, one launch (start us, length us, event | category | flops | bytes accessed | tf_op | source)
XLA Modules:
  0.0 399.3 jit_solution(5252624024002666220)
XLA Ops:
  0.6 0.0 copy-start
  0.7 0.8 convert_reduce_fusion
  1.5 0.6 pad.11.seg_ref
  2.1 0.7 fusion.2
  2.8 0.7 select_reduce_fusion
  3.6 0.1 copy.40
  3.7 0.1 copy.42
  3.8 0.0 copy-start.5
  3.8 88.9 %attention_forward.1 = (bf16[256,1024]{1,0:T(8,128)(2,1)}, bf16[256,1024]{1,0:T(8,128)(2,1)}, bf16[8,512,128]{2,1,0:T(8,128)(2,1)}, bf16[8,128,512]{2,1,0:T(8,12...) custom-call(bf16[256,1024]{1,0:T(8,128)(2,1)} %bitcast.28, ...), custom_call_target="tpu_custom_call" | custom-call | tf_op jit(solution)/shard_map/attention_forward/pallas_call | solution.py:575
  92.8 0.0 copy-done
  92.8 0.0 copy-done.5
  92.8 0.0 copy-start.9
  92.8 0.0 copy-start.8
  92.8 1.9 multiply_reduce_fusion.1
  94.7 0.0 copy-start.2
  94.7 0.0 copy-done.9
  94.7 0.2 multiply_convert_fusion.xl_ref
  94.9 0.0 copy-start.3
  94.9 0.9 copy-done.3
  95.8 0.0 copy-done.8
  95.8 0.3 select_reduce_fusion.1
  96.1 0.1 copy.39
  96.2 0.2 fusion.4
  96.4 0.2 multiply_convert_fusion.2
  96.5 1.9 fusion.1.x_ref
  98.4 103.2 %mixture.1 = (f32[256,1024]{1,0:T(8,128)}, bf16[4,256,1024]{2,1,0:T(8,128)(2,1)}, f32[256,1152]{1,0:T(8,128)}, bf16[4,512,512]{2,1,0:T(8,128)(2,1)}, bf16[4,512,...) custom-call(bf16[256,1152]{1,0:T(8,128)(2,1)} %fusion.1.x_ref, ...), custom_call_target="tpu_custom_call" | custom-call | tf_op jit(solution)/shard_map/mixture/pallas_call | solution.py:1180
  201.7 1.1 multiply_reduce_fusion.2
  202.8 1.1 multiply_convert_fusion.1
  203.9 0.0 copy-start.4
  203.9 1.6 multiply_reduce_fusion
  205.6 0.7 pad.13.dlog_ref
  206.2 0.8 bitcast_reduce_fusion.dgain2_ref
  207.1 0.0 copy-done.2
  207.1 0.0 copy-done.4
  207.1 1.3 fusion.5
  208.4 0.0 copy-start.6
  208.4 1.5 convolution_convert_fusion.do_ref
  209.9 71.2 %attention_backward.1 = (bf16[8,256,256]{2,1,0:T(8,128)(2,1)}, bf16[2,256,1024]{2,1,0:T(8,128)(2,1)}, bf16[2,512,512]{2,1,0:T(8,128)(2,1)}, bf16[2,512,512]{2,1,0:T(8,128)(2,1)}, bf16[2,256,1024]{2,1,0:T(8,128)(2,1)}) custom-call(bf16[256,1024]{1,0:T(8,128)(2,1)} %convolution_convert_fusion.do_ref, bf16[8,512,128]{2,1,0:T(8,128)(2,1)} %get-tuple-element.62.kv_ref, ...), custom_call_target="tpu_custom_call" | custom-call | tf_op jit(solution)/shard_map/attention_backward/pallas_call | solution.py:848
  281.1 0.0 copy-done.6
  281.1 101.8 %tail.1 = (bf16[256,1024]{1,0:T(8,128)(2,1)}, f32[256,1024]{1,0:T(8,128)}, f32[16,1024]{1,0:T(8,128)}, bf16[1024,1152]{1,0:T(8,128)(2,1)}, bf16[1024,1024]{1,0:T...) custom-call(bf16[8,256,256]{2,1,0:T(8,128)(2,1)} %get-tuple-element., ...), custom_call_target="tpu_custom_call" | custom-call | tf_op jit(solution)/shard_map/tail/pallas_call | solution.py:1435
  382.9 0.0 copy-start.1
  382.9 11.6 %widen.1 = (f32[1,1024]{1,0:T(1,128)}, f32[1024,1024]{1,0:T(8,128)}, f32[1024,512]{1,0:T(8,128)}, f32[1024,512]{1,0:T(8,128)}, f32[1024,1024]{1,0:T(8,128)}, /*i...) custom-call(f32[16,1024]{1,0:T(8,128)} %get-tuple-element.83.gains, ...), custom_call_target="tpu_custom_call" | custom-call | tf_op jit(solution)/shard_map/widen/pallas_call | solution.py:1498
  394.5 0.0 copy-start.7
  394.5 1.9 copy.44
  396.4 1.9 copy.47
  398.3 0.0 copy-done.7
  398.3 1.0 copy.48
  399.2 0.0 copy-done.1
  (2 shorter events, 0.0 us)
Async XLA Ops:
  0.6 92.1 %copy-start = (bf16[1024,1024]{1,0:T(8,128)(2,1)S(1)}, bf16[1024,1024]{1,0:T(8,128)(2,1)}, u32[]{:S(2)}) copy-start(bf16[1024,1024]{1,0:T(8,128)(2,1)} %param.25) | copy-start | bytes 6291460
  3.8 89.0 %copy-start.5 = (bf16[1,256,1024]{2,1,0:T(8,128)(2,1)S(1)}, bf16[1,256,1024]{2,1,0:T(8,128)(2,1)}, u32[]{:S(2)}) copy-start(bf16[1,256,1024]{2,1,0:T(8,128)(2,1)} %param.17) | copy-start | bytes 1572868
  92.8 1.9 copy-start.9
  92.8 3.0 copy-start.8
  94.7 112.4 %copy-start.2 = (f32[256,1024]{1,0:T(8,128)}, f32[256,1024]{1,0:T(8,128)S(1)}, u32[]{:S(2)}) copy-start(f32[256,1024]{1,0:T(8,128)S(1)} %get-tuple-element.141.h1_ref) | copy-start | bytes 3145732
  94.9 0.9 copy-start.3
  203.9 3.2 copy-start.4
  208.4 72.7 %copy-start.6 = (bf16[256,1024]{1,0:T(8,128)(2,1)}, bf16[256,1024]{1,0:T(8,128)(2,1)S(1)}, u32[]{:S(2)}) copy-start(bf16[256,1024]{1,0:T(8,128)(2,1)S(1)} %get-tuple-element.136.datt_ref) | copy-start | bytes 1572868
  382.9 16.4 %copy-start.1 = (bf16[1024,1024]{1,0:T(8,128)(2,1)S(1)}, bf16[1024,1024]{1,0:T(8,128)(2,1)}, u32[]{:S(2)}) copy-start(bf16[1024,1024]{1,0:T(8,128)(2,1)} %param.25) | copy-start | bytes 6291460
  394.5 3.8 copy-start.7

commit v5 on v4

--- a/solution.py
+++ b/solution.py
@@ -638,6 +638,8 @@
     dwg_in,
     dwu_in,
     dwd_in,
+    turn,
+    turn_sem,
     in_ref,
     dkv,
     part,
@@ -660,6 +662,13 @@
     steps = blocks // 2
     sigma = me_b // KV
     kappa = lax.rem(me_b, KV)
+    tables_in = [
+        pltpu.make_async_copy(src.at[2 * t + me_s], turn.at[i, t], turn_sem.at[i, t])
+        for i, src in enumerate((cos_ref, sin_ref))
+        for t in range(steps)
+    ]
+    for copy in tables_in:
+        copy.start()
     greet_all(2, blocks, me_s, me_b)
 
     dest_core = lax.rem(me_b, 2)
@@ -709,11 +718,14 @@
         return carry
 
     lax.fori_loop(0, KV, send_grad, 0)
+    for copy in tables_in:
+        copy.wait()
     for n in (2, 1):
         give_mix(n).start()
     for i in range(3):
         for n in (1, 2):
             give_weight(n, i).start()
+    give_weight(3, 2).start()
     dkv[...] = jnp.zeros_like(dkv)
     wide = 2 * tok
     lane = lax.broadcasted_iota(jnp.int32, (1, wide), 1)
@@ -742,9 +754,8 @@
         swap(t).wait_recv()
         place = pl.ds(pl.multiple_of(me_s * tok, tok), tok)
         total = dkv[t, place, :] + xch[t]
-        owner = 2 * t + me_s
-        cosine = jnp.where(low, cos_ref[owner], 1.0)
-        sine = jnp.where(low, sin_ref[owner], 0.0)
+        cosine = jnp.where(low, turn[0, t], 1.0)
+        sine = jnp.where(low, turn[1, t], 0.0)
         back = total * cosine - rotate_pairs(total) * sine
         done[t, :, pl.ds(2 * HD, 2 * HD)] = back.astype(BF16)
         deliver(t, "start")
@@ -791,8 +802,7 @@
         dq = lax.fori_loop(0, t, lambda u, s: piece(u, s, False), dq)
         dq = piece(t, dq, True) * HD ** (-0.5)
         upright = jnp.transpose(jnp.concatenate([dq[:, :tok], dq[:, tok:]], 0))
-        owner = 2 * t + me_s
-        back = upright * cos_ref[owner] - rotate_pairs(upright) * sin_ref[owner]
+        back = upright * turn[0, t] - rotate_pairs(upright) * turn[1, t]
         done[t, :, pl.ds(0, 2 * HD)] = back.astype(BF16)
         part[t] = dkv[t, pl.ds(pl.multiple_of((1 - me_s) * tok, tok), tok), :]
         swap(t).start()
@@ -835,6 +845,7 @@
         give_mix(n).wait()
         for i in range(3):
             give_weight(n, i).wait()
+    give_weight(3, 2).wait()
 
 
 def attention_backward(
@@ -852,11 +863,13 @@
             jax.ShapeDtypeStruct((2, *mix.shape[1:]), BF16),
             jax.ShapeDtypeStruct((2, *dwg.shape[1:]), BF16),
             jax.ShapeDtypeStruct((2, *dwu.shape[1:]), BF16),
-            jax.ShapeDtypeStruct((2, *dwd.shape[1:]), BF16),
+            jax.ShapeDtypeStruct((3, *dwd.shape[1:]), BF16),
         ),
-        in_specs=[vm] * len(vectors) + [hbm] * 4,
+        in_specs=[vm] * (len(vectors) - 2) + [hbm] * 6,
         out_specs=(vm,) + (hbm,) * 4,
         scratch_shapes=[
+            pltpu.VMEM((2, steps, tok, 2 * HD), F32),
+            dma((2, steps)),
             pltpu.VMEM((steps, tok, 2 * HD), BF16),
             pltpu.VMEM((steps, 2 * tok, 2 * HD), F32),
             pltpu.VMEM((steps, tok, 2 * HD), F32),
@@ -870,8 +883,8 @@
             dma((KV,)),
             dma((2,)),
             dma((2,)),
-            dma((2, 3)),
-            dma((2, 3)),
+            dma((3, 3)),
+            dma((3, 3)),
         ],
         compiler_params=pltpu.CompilerParams(
             collective_id=1, has_side_effects=True, vmem_limit_bytes=VMEM_LIMIT
@@ -882,6 +895,12 @@
 
 def mixture_kernel(
     x_ref,
+    ao_ref,
+    gain_ref,
+    router_ref,
+    routes_ref,
+    weight_ref,
+    wo_ref,
     g_ref,
     wg_ref,
     wu_ref,
@@ -890,15 +909,26 @@
     wg_all,
     wu_all,
     wd_all,
-    mix_own,
+    res_ref,
     mix_peer,
-    d_in,
+    xl_ref,
+    dlog_ref,
+    dh_ref,
+    datt_ref,
+    do_ref,
+    dgain_ref,
     dwg_out,
     dwu_out,
     dwd_out,
     dwg_in,
     dwu_in,
-    dwd_in,
+    wr_ref,
+    rw_ref,
+    h1_ref,
+    gate_ref,
+    d_in,
+    d_c,
+    wo,
     x_in,
     x_t,
     g_in,
@@ -927,6 +957,7 @@
     store_sem,
     wsend_sem,
     wrecv_sem,
+    wo_sem,
 ):
     me_s = lax.axis_index("seq")
     me_b = lax.axis_index("blk")
@@ -947,7 +978,9 @@
     def load_other(i, e):
         return pltpu.make_async_copy(owns[i][1].at[e], owns[i][2].at[e], load_sem.at[i, e])
 
-    for i in range(3):
+    load_out = pltpu.make_async_copy(wo_ref, wo, wo_sem)
+    load_out.start()
+    for i in (2, 0, 1):
         load_own(i).start()
         for n in (1, 2, 3):
             load_other(i, flip(plane, n)).start()
@@ -958,7 +991,28 @@
     pltpu.make_async_copy(g_ref, g_in.at[line], gload_sem.at[line]).start()
     for n in (1, 2, 3):
         load_grad(flip(line, n)).start()
-    x_in[line] = x_ref[...]
+    lane = lax.broadcasted_iota(jnp.int32, (tok, 128), 1)
+    rw = jnp.zeros((tok, 128), F32)
+    for j in range(TOP):
+        rw += jnp.where(routes_ref[:, j : j + 1] == lane, weight_ref[:, j : j + 1], 0.0)
+    rw_ref[...] = rw
+    shape = (router_ref.shape[1], 128)
+    row, column = (lax.broadcasted_iota(jnp.int32, shape, i) for i in range(2))
+    wr_ref[...] = mm(router_ref[...], (row == column).astype(BF16)).astype(BF16)
+    load_out.wait()
+    xs = x_ref[...].astype(F32)
+    h1 = xs + mm(ao_ref[...], wo[...])
+    h1_ref[...] = h1
+    xl = (h1 * rms_scale(h1) * gain_ref[...]).astype(BF16)
+    xl_ref[...] = xl
+    logits = mm(xl, wr_ref[...])
+    routed = rw > 0.0
+    top = jnp.max(jnp.where(routed, logits, NEG), -1, keepdims=True)
+    expo = jnp.where(routed, jnp.exp(logits - top), 0.0)
+    gates = expo / jnp.sum(expo, -1, keepdims=True)
+    gate_ref[...] = gates
+    x_in[line, :, :d] = xl
+    x_in[line, :, d:] = (rw * gates).astype(BF16)
     pl.semaphore_wait(barrier, 5)
 
     def along(k, step):
@@ -981,27 +1035,30 @@
         pass_on(line, step)
     for k in range(4):
         load_grad(k).wait()
+    g_rows = g_in.reshape(4 * tok, d)
+
+    def grad_hidden(e, carry):
+        load_other(2, e).wait()
+        for part in range(2):
+            rows = slice(part * 2 * tok, (part + 1) * 2 * tok)
+            dg[e, rows, :] = mm(g_rows[rows, :], wd[e], NT).astype(BF16)
+        return carry
+
+    lax.fori_loop(0, 4, grad_hidden, 0)
 
     def load_wait(e, carry):
-        for i in range(3):
+        for i in range(2):
             load_other(i, e).wait()
         return carry
 
-    lane = lax.broadcasted_iota(jnp.int32, (tok, 128), 1)
+    def apart(k):
+        return lax.rem(k - line + 3, 4)
 
     def place_of(j):
         return jnp.where(line < 2, lax.rem(line + j, 4), lax.rem(line + 4 - j, 4))
 
     def block(j, carry):
         n = place_of(j)
-        for step in (-1, 1):
-            k = line - step * j
-
-            @pl.when((j > 0) & (k >= 0) & (k < 4))
-            def _():
-                pltpu.make_async_copy(x_ref, x_in.at[k], recv_sem.at[k]).wait()
-                pass_on(k, step)
-
         acc_o[...] = jnp.zeros_like(acc_o)
         acc_d[...] = jnp.zeros_like(acc_d)
         acc_c[...] = jnp.zeros_like(acc_c)
@@ -1011,6 +1068,14 @@
             @pl.when(j == 0)
             def _():
                 load_wait(e, 0)
+
+            for step in (-1, 1):
+                k = line - step * (j + 1)
+
+                @pl.when((e == 3) & (j < 3) & (k >= 0) & (k < 4))
+                def _():
+                    pltpu.make_async_copy(x_in.at[line], x_in.at[k], recv_sem.at[k]).wait()
+                    pass_on(k, step)
 
             x = x_in[n, :, :d]
             here = lane == line * 4 + e
@@ -1019,7 +1084,7 @@
             )
             gate = mm(x, wg[e])
             up = mm(x, wu[e])
-            dh = mm(g_in[n], wd[e], NT)
+            dh = dg[e, rows, :].astype(F32)
             sg = jax.nn.sigmoid(gate)
             act = gate * sg
             hidden = act * up
@@ -1039,17 +1104,18 @@
 
         @pl.when(j == 0)
         def _():
-            mix_own[...] = acc_o[...]
-            d_in[:, :d] = acc_d[...]
-            d_in[:, d:] = acc_c[...]
+            res_ref[...] = h1_ref[...] + acc_o[...]
+            d_in[...] = acc_d[...]
+            d_c[...] = acc_c[...]
 
         @pl.when(j > 0)
         def _():
             mix_peer[n] = acc_o[...].astype(BF16)
-            d_send[n, :, :d] = acc_d[...].astype(BF16)
+            to = apart(n)
+            d_send[to, :, :d] = acc_d[...].astype(BF16)
             high = acc_c[...].astype(BF16).astype(F32)
             rest = acc_c[...] - high
-            d_send[n, :, d:] = (high + pltpu.roll(rest, 32, 1)).astype(BF16)
+            d_send[to, :, d:] = (high + pltpu.roll(rest, 32, 1)).astype(BF16)
             give_back(n).start()
 
         x_t[:, rows] = jnp.transpose(x_in[n, :, :d].astype(F32)).astype(BF16)
@@ -1057,7 +1123,7 @@
 
     def give_back(n):
         return remote(
-            d_send.at[n], d_recv.at[line], bsend_sem.at[n], brecv_sem.at[line], me_s, n * 4 + plane
+            d_send.at[apart(n)], d_recv.at[lax.rem(line - n + 3, 4)], bsend_sem.at[n], brecv_sem.at[line], me_s, n * 4 + plane
         )
 
     lax.fori_loop(0, 4, block, 0)
@@ -1067,7 +1133,6 @@
     dtheirs = pl.multiple_of((1 - me_s) * dhalf, dhalf)
     mine = pl.multiple_of(me_s * half, half)
     dmine = pl.multiple_of(me_s * dhalf, dhalf)
-    g_rows = g_in.reshape(4 * tok, d)
 
     def swap(i, e):
         src = (wg.at[e, pl.ds(0, half)], wu.at[e, pl.ds(0, half)], wd.at[e, pl.ds(0, dhalf)])[i]
@@ -1087,13 +1152,17 @@
     def opposed(i):
         return remote(
             (xg, xu, xd)[i].at[flip(plane, 3)],
-            (dwg_in, dwu_in, dwd_in)[i],
+            (dwg_in, dwu_in)[i],
             wsend_sem.at[i],
             wrecv_sem.at[i],
             *opposite,
         )
 
     def finished(i, n, e):
+        if i == 2:
+            store(i, e).start()
+            return
+
         @pl.when(n == 0)
         def _():
             opposed(i).start()
@@ -1112,8 +1181,6 @@
         wd[e, :dhalf, :] = mm(hc[e, :, pl.ds(dtheirs, dhalf)], g_rows[...], TN).astype(BF16)
         swap(2, e).start()
         return carry
-
-    lax.fori_loop(0, 4, give, 0)
 
     def keep(n, carry):
         e = turn_of(n)
@@ -1133,15 +1200,39 @@
         finished(2, n, e)
         return carry
 
-    lax.fori_loop(0, 4, keep, 0)
+    give(0, 0)
+
+    def both(n, carry):
+        give(n, 0)
+        keep(n - 1, 0)
+        return carry
+
+    lax.fori_loop(1, 4, both, 0)
+    keep(3, 0)
 
     for n in (1, 2, 3):
         k = flip(line, n)
-        pltpu.make_async_copy(d_send.at[k], d_recv.at[k], brecv_sem.at[k]).wait()
-        d_in[:, :d] += d_recv[k, :, :d].astype(F32)
-        tail = d_recv[k, :, d:].astype(F32)
-        both = tail + pltpu.roll(tail, 96, 1)
-        d_in[:, d:] += jnp.where(lane < 32, both, 0.0)
+        at = apart(k)
+        pltpu.make_async_copy(d_send.at[at], d_recv.at[at], brecv_sem.at[k]).wait()
+        d_in[...] += d_recv[at, :, :d].astype(F32)
+        rest = d_recv[at, :, d:].astype(F32)
+        d_c[...] += jnp.where(lane < 32, rest + pltpu.roll(rest, 96, 1), 0.0)
+
+    gates = gate_ref[...]
+    d_gates = rw_ref[...] * d_c[...]
+    dlog = (gates * (d_gates - jnp.sum(gates * d_gates, -1, keepdims=True))).astype(BF16)
+    dlog_ref[...] = dlog
+    d_xl = d_in[...] + mm(dlog, wr_ref[...], NT)
+    h1 = h1_ref[...]
+    scale = rms_scale(h1)
+    scaled = d_xl * gain_ref[...]
+    inner = jnp.mean(scaled * h1, -1, keepdims=True)
+    d_h1 = g_in[line].astype(F32) + scale * scaled - h1 * scale**3 * inner
+    dgain_ref[...] = jnp.sum((d_xl * h1 * scale).reshape(tok // 8, 8, d), 0)
+    dh_ref[...] = d_h1
+    d_att = d_h1.astype(BF16)
+    datt_ref[...] = d_att
+    do_ref[...] = mm(d_att, wo[...], NT).astype(BF16)
     for n in (1, 2, 3):
         give_back(flip(line, n)).wait_send()
     for k in range(4):
@@ -1159,18 +1250,18 @@
         for i in range(3):
             swap(i, e).wait_send()
 
-            @pl.when(n > 0)
+            @pl.when((n > 0) | (i == 2))
             def _():
                 store(i, e).wait()
 
         return carry
 
     lax.fori_loop(0, 4, finish, 0)
-    for i in range(3):
+    for i in range(2):
         opposed(i).wait()
 
 
-def mixture(x, g, w_gate, w_up, w_down, g_all, wg_all, wu_all, wd_all):
+def mixture(vectors, w_out, g, w_gate, w_up, w_down, shared):
     tok, d = g.shape
     ff = w_gate.shape[1]
     vm = pl.BlockSpec(memory_space=pltpu.VMEM)
@@ -1182,17 +1273,28 @@
         out_shape=(
             jax.ShapeDtypeStruct((tok, d), F32),
             jax.ShapeDtypeStruct((4, tok, d), BF16),
-            jax.ShapeDtypeStruct((tok, d + 128), F32),
+            jax.ShapeDtypeStruct((tok, d), BF16),
+            jax.ShapeDtypeStruct((tok, 128), BF16),
+            jax.ShapeDtypeStruct((tok, d), F32),
+            jax.ShapeDtypeStruct((tok, d), BF16),
+            jax.ShapeDtypeStruct((tok, d), BF16),
+            jax.ShapeDtypeStruct((8, d), F32),
             jax.ShapeDtypeStruct((4, d // 2, ff), BF16),
             jax.ShapeDtypeStruct((4, d // 2, ff), BF16),
             jax.ShapeDtypeStruct((4, ff // 2, d), BF16),
             jax.ShapeDtypeStruct((d // 2, ff), BF16),
             jax.ShapeDtypeStruct((d // 2, ff), BF16),
-            jax.ShapeDtypeStruct((ff // 2, d), BF16),
         ),
-        in_specs=[vm] + [hbm] * 8,
-        out_specs=(vm,) * 3 + (hbm,) * 6,
+        in_specs=[vm] * 6 + [hbm] * 9,
+        out_specs=(vm,) * 8 + (hbm,) * 5,
         scratch_shapes=[
+            vmem((d, 128), BF16),
+            vmem((tok, 128), F32),
+            vmem((tok, d), F32),
+            vmem((tok, 128), F32),
+            vmem((tok, d), F32),
+            vmem((tok, 128), F32),
+            vmem((d, d), BF16),
             vmem((4, tok, d + 128), BF16),
             vmem((d, 4 * tok), BF16),
             vmem((4, tok, d), BF16),
@@ -1205,8 +1307,8 @@
             vmem((tok, d), F32),
             vmem((tok, d), F32),
             vmem((tok, 128), F32),
-            vmem((4, tok, d + 128), BF16),
-            vmem((4, tok, d + 128), BF16),
+            vmem((3, tok, d + 128), BF16),
+            vmem((3, tok, d + 128), BF16),
             vmem((4, d // 2, ff), BF16),
             vmem((4, d // 2, ff), BF16),
             vmem((4, ff // 2, d), BF16),
@@ -1219,14 +1321,15 @@
             dma((3, 4)),
             dma((3, 4)),
             dma((3, 4)),
-            dma((3,)),
-            dma((3,)),
+            dma((2,)),
+            dma((2,)),
+            dma,
         ],
         compiler_params=pltpu.CompilerParams(
             collective_id=2, has_side_effects=True, vmem_limit_bytes=VMEM_LIMIT
         ),
         name="mixture",
-    )(x, g, w_gate, w_up, w_down, g_all, wg_all, wu_all, wd_all)
+    )(*vectors, w_out, g, w_gate, w_up, w_down, *shared)
 
 
 def tail_kernel(
@@ -1235,16 +1338,15 @@
     x_ref,
     gain_ref,
     dh_ref,
-    wq_ref,
-    wk_ref,
-    wv_ref,
     ao_ref,
     datt_ref,
     xl_ref,
     dlog_ref,
     dgain2_ref,
-    h1_ref,
-    mix_own,
+    own_ref,
+    wq_any,
+    wk_any,
+    wv_any,
     mix_ref,
     mix_near,
     eg_ref,
@@ -1255,7 +1357,6 @@
     ed_in,
     eg_far,
     eu_far,
-    ed_far,
     res_ref,
     dx_ref,
     gsum_ref,
@@ -1266,6 +1367,9 @@
     eu_out,
     ed_out,
     mix_in,
+    wq_ref,
+    wk_ref,
+    wv_ref,
     d_all,
     ev,
     edv,
@@ -1297,17 +1401,26 @@
     experts = (
         (eg_ref, eg_in, eg_far, ev.at[0]),
         (eu_ref, eu_in, eu_far, ev.at[1]),
-        (ed_ref, ed_in, ed_far, edv),
+        (ed_ref, ed_in, None, edv),
     )
 
     def loads(i):
         own, arrived, far, dst = experts[i]
-        return (
+        near = arrived.shape[0]
+        copies = [
             pltpu.make_async_copy(own.at[plane], dst.at[0], load_sem.at[i, 0]),
-            pltpu.make_async_copy(arrived, dst.at[pl.ds(1, 2)], load_sem.at[i, 1]),
-            pltpu.make_async_copy(far, dst.at[3], load_sem.at[i, 2]),
-        )
-
+            pltpu.make_async_copy(arrived, dst.at[pl.ds(1, near)], load_sem.at[i, 1]),
+        ]
+        if far is not None:
+            copies.append(pltpu.make_async_copy(far, dst.at[3], load_sem.at[i, 2]))
+        return copies
+
+    projections = [
+        pltpu.make_async_copy(src, dst, load_sem.at[3, i + 1])
+        for i, (src, dst) in enumerate(((wq_any, wq_ref), (wk_any, wk_ref), (wv_any, wv_ref)))
+    ]
+    for copy in projections:
+        copy.start()
     for i in range(3):
         for copy in loads(i):
             copy.start()
@@ -1344,6 +1457,8 @@
         item.acc[...] = mm(xa_ref[:, mine], d_all[:, cols], TN)
         item.pair()
 
+    for copy in projections:
+        copy.wait()
     grad = (
         mm(d_all[:, : H * HD], wq_ref[...], NT)
         + mm(d_all[:, H * HD : (H + KV) * HD], wk_ref[...], NT)
@@ -1354,8 +1469,14 @@
     scaled = grad * gain_ref[...]
     inner = jnp.mean(scaled * xs, -1, keepdims=True)
     dx_ref[...] = dh_ref[...] + scale * scaled - xs * scale**3 * inner
-    gbuf[0, :8, :] = jnp.sum((grad * xs * scale).reshape(tok // 8, 8, d), 0)
-    gbuf[0, 8:, :] = dgain2_ref[...]
+    gains = (
+        jnp.sum(grad * xs * scale, 0, keepdims=True),
+        jnp.sum(dgain2_ref[...], 0, keepdims=True),
+    )
+    part = d // 4
+    gbuf[0] = jnp.concatenate(
+        [gain[:, i * part : (i + 1) * part] for gain in gains for i in range(4)], 0
+    )
 
     stages = [[sibling], planes, lines]
 
@@ -1409,7 +1530,7 @@
     gsum_ref[...] = gain_total(2)
     for item in sums:
         item.back(4)
-    result = h1_ref[...] + mix_own[...]
+    result = own_ref[...]
     near_mix.wait()
     far_mix.wait()
     for n in range(3):
@@ -1437,22 +1558,25 @@
         out_shape=(
             jax.ShapeDtypeStruct((tok, d), BF16),
             jax.ShapeDtypeStruct((tok, d), F32),
-            jax.ShapeDtypeStruct((16, d), F32),
+            jax.ShapeDtypeStruct((8, d // 4), F32),
             *(jax.ShapeDtypeStruct((d, width), BF16) for width in widths),
             jax.ShapeDtypeStruct((d, ff), BF16),
             jax.ShapeDtypeStruct((d, ff), BF16),
             jax.ShapeDtypeStruct((ff, d), BF16),
         ),
-        in_specs=[vm] * len(blocks_in) + [hbm] * 11,
+        in_specs=[vm] * (len(blocks_in) - 3) + [hbm] * 13,
         out_specs=(vm,) * 9,
         scratch_shapes=[
             vmem((3, tok, d), BF16),
+            vmem((d, H * HD), BF16),
+            vmem((d, KV * HD), BF16),
+            vmem((d, KV * HD), BF16),
             vmem((tok, (H + 2 * KV) * HD), BF16),
             vmem((2, 4, d // 2, ff), BF16),
             vmem((4, ff // 2, d), BF16),
-            vmem((3, 16, d), F32),
-            vmem((7, 16, d), F32),
-            dma((4, 3)),
+            vmem((3, 8, d // 4), F32),
+            vmem((7, 8, d // 4), F32),
+            dma((4, 4)),
             dma((3,)),
             dma((3,)),
             dma((7,)),
@@ -1468,7 +1592,9 @@
     )(*blocks_in, mix_peer, mix_near, *own, *arrived, *far)
 
 
-def widen_kernel(gains, o, q, kv, eg, eu, ed, n1, wq, wk, wv, wo, n2, wr, og, ou, od):
+def widen_kernel(
+    gains, o, q, kv, eg, eu, ed, res, dx, n1, wq, wk, wv, wo, n2, wr, og, ou, od, res_out, dx_out
+):
     d = wq.shape[1]
     half = wk.shape[1]
     wq[...] = q[...].astype(F32)
@@ -1479,12 +1605,15 @@
     og[0] = eg[...].astype(F32)
     ou[0] = eu[...].astype(F32)
     od[0] = ed[...].astype(F32)
-    n1[...] = jnp.sum(gains[:8], 0, keepdims=True)
-    n2[...] = jnp.sum(gains[8:], 0, keepdims=True)
-
-
-def widen(gains, o, q, kv, eg, eu, ed, experts):
+    n1[...] = jnp.concatenate([gains[i : i + 1, :] for i in range(4)], 1)
+    n2[...] = jnp.concatenate([gains[i : i + 1, :] for i in range(4, 8)], 1)
+    res_out[0] = res[...]
+    dx_out[0] = dx[...]
+
+
+def widen(gains, o, q, kv, eg, eu, ed, res, dx, experts):
     d, ff = eg.shape
+    tok = res.shape[0]
     parts = 8
 
     def block(shape):
@@ -1506,9 +1635,11 @@
             jax.ShapeDtypeStruct((1, d, ff), F32),
             jax.ShapeDtypeStruct((1, d, ff), F32),
             jax.ShapeDtypeStruct((1, ff, d), F32),
+            jax.ShapeDtypeStruct((1, tok, d), BF16),
+            jax.ShapeDtypeStruct((1, tok, d), F32),
         ),
-        in_specs=[pl.BlockSpec((16, d), lambda i: (0, 0))]
-        + [block(a.shape) for a in (o, q, kv, eg, eu, ed)],
+        in_specs=[pl.BlockSpec((8, d // 4), lambda i: (0, 0))]
+        + [block(a.shape) for a in (o, q, kv, eg, eu, ed, res, dx)],
         out_specs=(
             flat,
             *(block(shape) for shape in shapes),
@@ -1517,10 +1648,12 @@
             deep((d, ff)),
             deep((d, ff)),
             deep((ff, d)),
+            deep((tok, d)),
+            deep((tok, d)),
         ),
         compiler_params=pltpu.CompilerParams(vmem_limit_bytes=VMEM_LIMIT),
         name="widen",
-    )(gains, o, q, kv, eg, eu, ed)
+    )(gains, o, q, kv, eg, eu, ed, res, dx)
 
 
 D = 1024
@@ -1839,8 +1972,7 @@
     w_down,
     cotangent,
 ):
-    xs = tokens[0].astype(F32)
-    tok, d = xs.shape
+    tok, d = tokens[0].shape
     blocks = lax.axis_size("blk")
     experts = w_router.shape[1]
     cos_np, sin_np = tables(tok * blocks)
@@ -1866,33 +1998,16 @@
     )
     kept, shared = kept[:5], kept[5:]
 
-    h1 = xs + mm(att_low, w_out)
-    scale2 = rms_scale(h1)
-    xl = (h1 * scale2 * norm2_gain).astype(BF16)
-    logits = mm(xl, w_router)
-    chooser = routes[0][:, :, None] == jnp.arange(experts, dtype=jnp.int32)[None, None, :]
-    routed = jnp.any(chooser, 1)
-    rweight = jnp.sum(jnp.where(chooser, route_weight[0][:, :, None], 0.0), 1)
-    top = jnp.max(jnp.where(routed, logits, NEG), -1, keepdims=True)
-    expo = jnp.where(routed, jnp.exp(logits - top), 0.0)
-    gates = expo / jnp.sum(expo, -1, keepdims=True)
-    combine = (rweight * gates).astype(BF16)
-    sent = jnp.concatenate([xl, jnp.pad(combine, ((0, 0), (0, 128 - experts)))], 1)
-    mix_own, mix_peer, d_in, dwg, dwu, dwd, *far = mixture(
-        sent, g_low, w_gate[0], w_up[0], w_down[0], *shared
-    )
-
-    grad_out = g_low.astype(F32)
-    grad_gates = rweight * d_in[:, d : d + experts]
-    grad_logits = (
-        gates * (grad_gates - jnp.sum(gates * grad_gates, -1, keepdims=True))
-    ).astype(BF16)
-    grad_xl = d_in[:, :d] + mm(grad_logits, w_router, NT)
-    grad_h1_norm, unused = rms_back(h1, scale2, norm2_gain, grad_xl)
-    gain2_terms = jnp.sum((grad_xl * h1 * scale2).reshape(tok // 8, 8, d), 0)
-    grad_h1 = grad_out + grad_h1_norm
-    grad_att = grad_h1.astype(BF16)
-    grad_o = mm(grad_att, w_out, NT).astype(BF16)
+    own, mix_peer, xl, grad_logits, grad_h1, grad_att, grad_o, gain2_terms, *rest = mixture(
+        (tokens[0], att_low, norm2_gain[None], w_router, routes[0], route_weight[0]),
+        w_out,
+        g_low,
+        w_gate[0],
+        w_up[0],
+        w_down[0],
+        shared,
+    )
+    (dwg, dwu, dwd), far = rest[:3], rest[3:]
     vectors = (
         grad_o,
         *kept,
@@ -1908,25 +2023,24 @@
         tokens[0],
         gain1,
         grad_h1,
+        att_low,
+        grad_att,
+        xl,
+        grad_logits,
+        gain2_terms,
+        own,
         w_query,
         w_key,
         w_value,
-        att_low,
-        grad_att,
-        xl,
-        jnp.pad(grad_logits, ((0, 0), (0, 128 - experts))),
-        gain2_terms,
-        h1,
-        mix_own,
     )
     result, grad_x, gains, d_out, d_query, d_kv, d_gate_w, d_up_w, d_down = tail(
         blocks_in, mix_peer, mix_near, (dwg, dwu, dwd), arrived, far
     )
-    wide = widen(gains, d_out, d_query, d_kv, d_gate_w, d_up_w, d_down, experts)
-    d_gain1, d_query, d_key, d_value, d_out, d_gain2, *rest = wide
+    wide = widen(gains, d_out, d_query, d_kv, d_gate_w, d_up_w, d_down, result, grad_x, experts)
+    d_gain1, d_query, d_key, d_value, d_out, d_gain2, *rest, result, grad_x = wide
     return (
-        result[None],
-        grad_x[None],
+        result,
+        grad_x,
         d_gain1[0],
         d_query,
         d_key,

time: 400 us -> 379 us (0.948)
  other arithmetic: 9.07 us -> 0.7 us
  Pallas kernels: 377 us -> 370 us
  matrix products: 5.3 us -> 0 us
    pallas_call x1, Pallas kernels: 102 us -> 94.6 us  [tail(): pl.pallas_call(tail_kernel, out_shape=(jax.ShapeDtypeStruct((tok, d), BF1...]
    dot_general x4 -> x0, matrix products: 5.3 us -> none  [mm(): return lax.dot_general(a, b, dims, preferred_element_type=F32)]
where the time goes in v5:
time: 379 us; the launch traced here: 378 us
  Pallas kernels  370 us (98%)
  local copies, waits for them, and re-layouts  7.01 us (2%)
    pallas_call x1, Pallas kernels, mixture(): pl.pallas_call(mixture_kernel, out_shape=(jax.ShapeDtypeStruct((tok, d),...  100 us
    pallas_call x1, Pallas kernels, tail(): pl.pallas_call(tail_kernel, out_shape=(jax.ShapeDtypeStruct((tok, d), BF1...  94.6 us
    pallas_call x1, Pallas kernels, attention_forward(): pl.pallas_call(functools.partial(attention_forward_kernel, blocks), out_s...  88.9 us
    pallas_call x1, Pallas kernels, attention_backward(): pl.pallas_call(functools.partial(attention_backward_kernel, blocks), out_...  73.7 us
    pallas_call x1, Pallas kernels, widen(): pl.pallas_call(widen_kernel, grid=(parts,), out_shape=(jax.ShapeDtypeStru...  12.6 us

profile of v5, /device:TPU:0, one launch (start us, length us, event | category | flops | bytes accessed | tf_op | source)
XLA Modules:
  0.0 378.4 jit_solution(2888729107799587463)
XLA Ops:
  0.6 0.7 convert_reduce_fusion
  1.3 0.6 pad.4.seg_ref
  1.9 1.5 copy.29
  3.4 1.5 copy.30
  4.9 1.6 copy.31.router_ref
  6.5 88.9 %attention_forward.1 = (bf16[256,1024]{1,0:T(8,128)(2,1)}, bf16[256,1024]{1,0:T(8,128)(2,1)}, bf16[8,512,128]{2,1,0:T(8,128)(2,1)}, bf16[8,128,512]{2,1,0:T(8,12...) custom-call(bf16[256,1024]{1,0:T(8,128)(2,1)} %bitcast.12, ...), custom_call_target="tpu_custom_call" | custom-call | tf_op jit(solution)/shard_map/attention_forward/pallas_call | solution.py:575
  95.4 100.2 %mixture.1 = (f32[256,1024]{1,0:T(8,128)}, bf16[4,256,1024]{2,1,0:T(8,128)(2,1)}, bf16[256,1024]{1,0:T(8,128)(2,1)}, bf16[256,128]{1,0:T(8,128)(2,1)}, f32[256,1...) custom-call(bf16[256,1024]{1,0:T(8,128)(2,1)} %bitcast.13, ...), custom_call_target="tpu_custom_call" | custom-call | tf_op jit(solution)/shard_map/mixture/pallas_call | solution.py:1271
  195.6 73.7 %attention_backward.1 = (bf16[8,256,256]{2,1,0:T(8,128)(2,1)}, bf16[2,256,1024]{2,1,0:T(8,128)(2,1)}, bf16[2,512,512]{2,1,0:T(8,128)(2,1)}, bf16[2,512,512]{2,1,0:T(8,128)(2,1)}, bf16[3,256,1024]{2,1,0:T(8,128)(2,1)}) custom-call(bf16[256,1024]{1,0:T(8,128)(2,1)} %get-tuple-element.67.do_ref, bf16[8,512,128]{2,1,0:T(8,128)(2,1)} %get-tuple-element.68.kv_ref, ...), custom_call_target="tpu_custom_call" | custom-call | tf_op jit(solution)/shard_map/attention_backward/pallas_call | solution.py:859
  269.3 94.6 %tail.1 = (bf16[256,1024]{1,0:T(8,128)(2,1)}, f32[256,1024]{1,0:T(8,128)}, f32[8,256]{1,0:T(8,128)}, bf16[1024,1152]{1,0:T(8,128)(2,1)}, bf16[1024,1024]{1,0:T(8...) custom-call(bf16[8,256,256]{2,1,0:T(8,128)(2,1)} %get-tuple-element., ...), custom_call_target="tpu_custom_call" | custom-call | tf_op jit(solution)/shard_map/tail/pallas_call | solution.py:1556
  364.0 12.6 %widen.1 = (f32[1,1024]{1,0:T(1,128)}, f32[1024,1024]{1,0:T(8,128)}, f32[1024,512]{1,0:T(8,128)}, f32[1024,512]{1,0:T(8,128)}, f32[1024,1024]{1,0:T(8,128)}, /*i...) custom-call(f32[8,256]{1,0:T(8,128)} %get-tuple-element.91.gains, ...), custom_call_target="tpu_custom_call" | custom-call | tf_op jit(solution)/shard_map/widen/pallas_call | solution.py:1627
  376.6 1.8 copy.32

commit v6 on v5

--- a/solution.py
+++ b/solution.py
@@ -19,7 +19,7 @@
 BF16 = jnp.bfloat16
 MESH = pl.DeviceIdType.MESH
 VMEM_LIMIT = 60 * 2**20
-GRAD_STEPS = (1, 4, 6)
+GRAD_STEPS = (2, 5)
 HOP_STEP = 4
 NT = (((1,), (1,)), ((), ()))
 TN = (((0,), (0,)), ((), ()))
@@ -312,6 +312,10 @@
             arrived, arrived, hsend_sem.at[n - 1, i], hrecv_sem.at[n - 1, i], 1 - me_s, me_b
         )
 
+    share_weight(1, 0).start()
+    share_weight(2, 1).start()
+    for step in (-1, 1):
+        pass_on(line, step, True)
     tables_in = [
         pltpu.make_async_copy(src.at[me_b], turn.at[i], turn_sem.at[i])
         for i, src in enumerate((cos_ref, sin_ref))
@@ -362,7 +366,7 @@
         return carry
 
     lax.fori_loop(0, KV, send_payload, 0)
-    for i in range(3):
+    for i in (1, 2):
         share_weight(1, (0, 2, 1)[i]).start()
         share_weight(2, (1, 2, 0)[i]).start()
 
@@ -393,14 +397,9 @@
             arrival(t + 1).wait()
             forward(t + 1).start()
 
-        @pl.when(t == GRAD_STEPS[0])
-        def _():
-            for step in (-1, 1):
-                pass_on(line, step, True)
-
         for j in (1, 2):
 
-            @pl.when(t == GRAD_STEPS[j])
+            @pl.when(t == GRAD_STEPS[j - 1])
             def _():
                 pass_distance(j)
 
@@ -930,6 +929,8 @@
     d_c,
     wo,
     x_in,
+    c_in,
+    share_ref,
     x_t,
     g_in,
     wg,
@@ -943,6 +944,8 @@
     acc_c,
     d_send,
     d_recv,
+    c_send,
+    c_recv,
     xg,
     xu,
     xd,
@@ -958,12 +961,17 @@
     wsend_sem,
     wrecv_sem,
     wo_sem,
+    csend_sem,
+    crecv_sem,
+    ksend_sem,
+    krecv_sem,
 ):
     me_s = lax.axis_index("seq")
     me_b = lax.axis_index("blk")
     line, plane = me_b // 4, lax.rem(me_b, 4)
     tok, d = g_in.shape[1:]
     ff = wg.shape[2]
+    experts = router_ref.shape[0]
     barrier = pltpu.get_barrier_semaphore()
     sibling = (1 - me_s, me_b)
     opposite = (me_s, line * 4 + flip(plane, 3))
@@ -992,13 +1000,14 @@
     for n in (1, 2, 3):
         load_grad(flip(line, n)).start()
     lane = lax.broadcasted_iota(jnp.int32, (tok, 128), 1)
-    rw = jnp.zeros((tok, 128), F32)
+    number = lax.broadcasted_iota(jnp.int32, (128, tok), 0)
+    spread = jnp.zeros((128, tok), F32)
     for j in range(TOP):
-        rw += jnp.where(routes_ref[:, j : j + 1] == lane, weight_ref[:, j : j + 1], 0.0)
+        spread += jnp.where(routes_ref[j : j + 1, :] == number, weight_ref[j : j + 1, :], 0.0)
+    rw = jnp.transpose(spread)
     rw_ref[...] = rw
-    shape = (router_ref.shape[1], 128)
-    row, column = (lax.broadcasted_iota(jnp.int32, shape, i) for i in range(2))
-    wr_ref[...] = mm(router_ref[...], (row == column).astype(BF16)).astype(BF16)
+    row, column = (lax.broadcasted_iota(jnp.int32, (experts, 128), i) for i in range(2))
+    wr_ref[...] = mm(router_ref[...], (row == column).astype(BF16), TN).astype(BF16)
     load_out.wait()
     xs = x_ref[...].astype(F32)
     h1 = xs + mm(ao_ref[...], wo[...])
@@ -1011,8 +1020,8 @@
     expo = jnp.where(routed, jnp.exp(logits - top), 0.0)
     gates = expo / jnp.sum(expo, -1, keepdims=True)
     gate_ref[...] = gates
-    x_in[line, :, :d] = xl
-    x_in[line, :, d:] = (rw * gates).astype(BF16)
+    x_in[line] = xl
+    c_in[line] = jnp.transpose(rw * gates)[:experts].astype(BF16)
     pl.semaphore_wait(barrier, 5)
 
     def along(k, step):
@@ -1026,9 +1035,21 @@
             (line + step) * 4 + plane,
         )
 
+    def along_too(k, step):
+        at = 0 if step < 0 else 1
+        return remote(
+            c_in.at[k],
+            c_in.at[k],
+            csend_sem.at[at, k],
+            crecv_sem.at[k],
+            me_s,
+            (line + step) * 4 + plane,
+        )
+
     def pass_on(k, step):
         @pl.when((line + step >= 0) & (line + step < 4))
         def _():
+            along_too(k, step).start()
             along(k, step).start()
 
     for step in (-1, 1):
@@ -1059,6 +1080,8 @@
 
     def block(j, carry):
         n = place_of(j)
+        filler = jnp.zeros((128 - experts, tok), F32)
+        share_ref[...] = jnp.transpose(jnp.concatenate([c_in[n].astype(F32), filler], 0))
         acc_o[...] = jnp.zeros_like(acc_o)
         acc_d[...] = jnp.zeros_like(acc_d)
         acc_c[...] = jnp.zeros_like(acc_c)
@@ -1074,14 +1097,13 @@
 
                 @pl.when((e == 3) & (j < 3) & (k >= 0) & (k < 4))
                 def _():
+                    pltpu.make_async_copy(c_in.at[line], c_in.at[k], crecv_sem.at[k]).wait()
                     pltpu.make_async_copy(x_in.at[line], x_in.at[k], recv_sem.at[k]).wait()
                     pass_on(k, step)
 
-            x = x_in[n, :, :d]
+            x = x_in[n]
             here = lane == line * 4 + e
-            share = jnp.sum(
-                jnp.where(here, x_in[n, :, d:].astype(F32), 0.0), 1, keepdims=True
-            )
+            share = jnp.sum(jnp.where(here, share_ref[...], 0.0), 1, keepdims=True)
             gate = mm(x, wg[e])
             up = mm(x, wu[e])
             dh = dg[e, rows, :].astype(F32)
@@ -1112,14 +1134,26 @@
         def _():
             mix_peer[n] = acc_o[...].astype(BF16)
             to = apart(n)
-            d_send[to, :, :d] = acc_d[...].astype(BF16)
-            high = acc_c[...].astype(BF16).astype(F32)
-            rest = acc_c[...] - high
-            d_send[to, :, d:] = (high + pltpu.roll(rest, 32, 1)).astype(BF16)
+            d_send[to] = acc_d[...].astype(BF16)
+            turned = jnp.transpose(acc_c[...])[:experts]
+            high = turned.astype(BF16)
+            c_send[to, :experts, :] = high
+            c_send[to, experts:, :] = (turned - high.astype(F32)).astype(BF16)
+            give_back_too(n).start()
             give_back(n).start()
 
-        x_t[:, rows] = jnp.transpose(x_in[n, :, :d].astype(F32)).astype(BF16)
+        x_t[:, rows] = jnp.transpose(x_in[n].astype(F32)).astype(BF16)
         return carry
+
+    def give_back_too(n):
+        return remote(
+            c_send.at[apart(n)],
+            c_recv.at[lax.rem(line - n + 3, 4)],
+            ksend_sem.at[n],
+            krecv_sem.at[line],
+            me_s,
+            n * 4 + plane,
+        )
 
     def give_back(n):
         return remote(
@@ -1210,13 +1244,16 @@
     lax.fori_loop(1, 4, both, 0)
     keep(3, 0)
 
+    from_line = jnp.zeros((experts, tok), F32)
     for n in (1, 2, 3):
         k = flip(line, n)
         at = apart(k)
+        pltpu.make_async_copy(c_send.at[at], c_recv.at[at], krecv_sem.at[k]).wait()
+        from_line += c_recv[at, :experts, :].astype(F32) + c_recv[at, experts:, :].astype(F32)
         pltpu.make_async_copy(d_send.at[at], d_recv.at[at], brecv_sem.at[k]).wait()
-        d_in[...] += d_recv[at, :, :d].astype(F32)
-        rest = d_recv[at, :, d:].astype(F32)
-        d_c[...] += jnp.where(lane < 32, rest + pltpu.roll(rest, 96, 1), 0.0)
+        d_in[...] += d_recv[at].astype(F32)
+    filler = jnp.zeros((128 - experts, tok), F32)
+    d_c[...] += jnp.transpose(jnp.concatenate([from_line, filler], 0))
 
     gates = gate_ref[...]
     d_gates = rw_ref[...] * d_c[...]
@@ -1235,15 +1272,18 @@
     do_ref[...] = mm(d_att, wo[...], NT).astype(BF16)
     for n in (1, 2, 3):
         give_back(flip(line, n)).wait_send()
+        give_back_too(flip(line, n)).wait_send()
     for k in range(4):
 
         @pl.when((k <= line) & (line < 3))
         def _():
             along(k, 1).wait_send()
+            along_too(k, 1).wait_send()
 
         @pl.when((k >= line) & (line > 0))
         def _():
             along(k, -1).wait_send()
+            along_too(k, -1).wait_send()
 
     def finish(n, carry):
         e = turn_of(n)
@@ -1264,6 +1304,7 @@
 def mixture(vectors, w_out, g, w_gate, w_up, w_down, shared):
     tok, d = g.shape
     ff = w_gate.shape[1]
+    experts = vectors[3].shape[0]
     vm = pl.BlockSpec(memory_space=pltpu.VMEM)
     hbm = pl.BlockSpec(memory_space=pl.ANY)
     dma = pltpu.SemaphoreType.DMA
@@ -1295,7 +1336,9 @@
             vmem((tok, d), F32),
             vmem((tok, 128), F32),
             vmem((d, d), BF16),
-            vmem((4, tok, d + 128), BF16),
+            vmem((4, tok, d), BF16),
+            vmem((4, experts, tok), BF16),
+            vmem((tok, 128), F32),
             vmem((d, 4 * tok), BF16),
             vmem((4, tok, d), BF16),
             vmem((4, d, ff), BF16),
@@ -1307,8 +1350,10 @@
             vmem((tok, d), F32),
             vmem((tok, d), F32),
             vmem((tok, 128), F32),
-            vmem((3, tok, d + 128), BF16),
-            vmem((3, tok, d + 128), BF16),
+            vmem((3, tok, d), BF16),
+            vmem((3, tok, d), BF16),
+            vmem((3, 2 * experts, tok), BF16),
+            vmem((3, 2 * experts, tok), BF16),
             vmem((4, d // 2, ff), BF16),
             vmem((4, d // 2, ff), BF16),
             vmem((4, ff // 2, d), BF16),
@@ -1324,6 +1369,10 @@
             dma((2,)),
             dma((2,)),
             dma,
+            dma((2, 4)),
+            dma((4,)),
+            dma((4,)),
+            dma((4,)),
         ],
         compiler_params=pltpu.CompilerParams(
             collective_id=2, has_side_effects=True, vmem_limit_bytes=VMEM_LIMIT
@@ -1601,7 +1650,7 @@
     wk[...] = kv[:, :half].astype(F32)
     wv[...] = kv[:, half:].astype(F32)
     wo[...] = o[:, :d].astype(F32)
-    wr[...] = o[:, d : d + wr.shape[1]].astype(F32)
+    wr[...] = jnp.transpose(o[:, d:].astype(F32))[: wr.shape[0]]
     og[0] = eg[...].astype(F32)
     ou[0] = eu[...].astype(F32)
     od[0] = ed[...].astype(F32)
@@ -1614,7 +1663,7 @@
 def widen(gains, o, q, kv, eg, eu, ed, res, dx, experts):
     d, ff = eg.shape
     tok = res.shape[0]
-    parts = 8
+    parts = 4
 
     def block(shape):
         return pl.BlockSpec((shape[0] // parts, shape[1]), lambda i: (i, 0))
@@ -1631,7 +1680,7 @@
             jax.ShapeDtypeStruct((1, d), F32),
             *(jax.ShapeDtypeStruct(shape, F32) for shape in shapes),
             jax.ShapeDtypeStruct((1, d), F32),
-            jax.ShapeDtypeStruct((d, experts), F32),
+            jax.ShapeDtypeStruct((experts, d), F32),
             jax.ShapeDtypeStruct((1, d, ff), F32),
             jax.ShapeDtypeStruct((1, d, ff), F32),
             jax.ShapeDtypeStruct((1, ff, d), F32),
@@ -1644,7 +1693,7 @@
             flat,
             *(block(shape) for shape in shapes),
             flat,
-            block((d, experts)),
+            pl.BlockSpec((experts, d // parts), lambda i: (0, i)),
             deep((d, ff)),
             deep((d, ff)),
             deep((ff, d)),
@@ -1999,7 +2048,7 @@
     kept, shared = kept[:5], kept[5:]
 
     own, mix_peer, xl, grad_logits, grad_h1, grad_att, grad_o, gain2_terms, *rest = mixture(
-        (tokens[0], att_low, norm2_gain[None], w_router, routes[0], route_weight[0]),
+        (tokens[0], att_low, norm2_gain[None], w_router.T, routes[0].T, route_weight[0].T),
         w_out,
         g_low,
         w_gate[0],
@@ -2037,7 +2086,7 @@
         blocks_in, mix_peer, mix_near, (dwg, dwu, dwd), arrived, far
     )
     wide = widen(gains, d_out, d_query, d_kv, d_gate_w, d_up_w, d_down, result, grad_x, experts)
-    d_gain1, d_query, d_key, d_value, d_out, d_gain2, *rest, result, grad_x = wide
+    d_gain1, d_query, d_key, d_value, d_out, d_gain2, d_router, *rest, result, grad_x = wide
     return (
         result,
         grad_x,
@@ -2047,6 +2096,7 @@
         d_value,
         d_out,
         d_gain2[0],
+        d_router.T,
         *rest,
     )
 

time: 379 us -> 362 us (0.955)
  Pallas kernels: 370 us -> 360 us
  local copies, waits for them, and re-layouts: 7.01 us -> 0.6 us
    pallas_call x1, Pallas kernels: 100 us -> 92.7 us  [mixture(): pl.pallas_call(mixture_kernel, out_shape=(jax.ShapeDtypeStruct((tok, d),...]
    unnamed x4 -> x0, local copies, waits for them, and re-layouts: 6.41 us -> none
    pallas_call x1, Pallas kernels: 88.9 us -> 84.3 us  [attention_forward(): pl.pallas_call(functools.partial(attention_forward_kernel, blocks), out_s...]
where the time goes in v6:
time: 362 us
  Pallas kernels  360 us (99%)
    pallas_call x1, Pallas kernels, tail(): pl.pallas_call(tail_kernel, out_shape=(jax.ShapeDtypeStruct((tok, d), BF1...  95.4 us
    pallas_call x1, Pallas kernels, mixture(): pl.pallas_call(mixture_kernel, out_shape=(jax.ShapeDtypeStruct((tok, d),...  92.7 us
    pallas_call x1, Pallas kernels, attention_forward(): pl.pallas_call(functools.partial(attention_forward_kernel, blocks), out_s...  84.3 us
    pallas_call x1, Pallas kernels, attention_backward(): pl.pallas_call(functools.partial(attention_backward_kernel, blocks), out_...  76.2 us
    pallas_call x1, Pallas kernels, widen(): pl.pallas_call(widen_kernel, grid=(parts,), out_shape=(jax.ShapeDtypeStru...  11.5 us

profile of v6, /device:TPU:0, one launch (start us, length us, event | category | flops | bytes accessed | tf_op | source)
XLA Modules:
  0.0 362.2 jit_solution(6000737631469175423)
XLA Ops:
  0.6 0.7 convert_reduce_fusion
  1.3 0.6 pad.4.seg_ref
  1.9 84.3 %attention_forward.1 = (bf16[256,1024]{1,0:T(8,128)(2,1)}, bf16[256,1024]{1,0:T(8,128)(2,1)}, bf16[8,512,128]{2,1,0:T(8,128)(2,1)}, bf16[8,128,512]{2,1,0:T(8,12...) custom-call(bf16[256,1024]{1,0:T(8,128)(2,1)} %bitcast.18, ...), custom_call_target="tpu_custom_call" | custom-call | tf_op jit(solution)/shard_map/attention_forward/pallas_call | solution.py:574
  86.2 92.7 %mixture.1 = (f32[256,1024]{1,0:T(8,128)}, bf16[4,256,1024]{2,1,0:T(8,128)(2,1)}, bf16[256,1024]{1,0:T(8,128)(2,1)}, bf16[256,128]{1,0:T(8,128)(2,1)}, f32[256,1...) custom-call(bf16[256,1024]{1,0:T(8,128)(2,1)} %bitcast.19, ...), custom_call_target="tpu_custom_call" | custom-call | tf_op jit(solution)/shard_map/mixture/pallas_call | solution.py:1312
  178.9 76.2 %attention_backward.1 = (bf16[8,256,256]{2,1,0:T(8,128)(2,1)}, bf16[2,256,1024]{2,1,0:T(8,128)(2,1)}, bf16[2,512,512]{2,1,0:T(8,128)(2,1)}, bf16[2,512,512]{2,1,0:T(8,128)(2,1)}, bf16[3,256,1024]{2,1,0:T(8,128)(2,1)}) custom-call(bf16[256,1024]{1,0:T(8,128)(2,1)} %get-tuple-element.67.do_ref, bf16[8,512,128]{2,1,0:T(8,128)(2,1)} %get-tuple-element.68.kv_ref, ...), custom_call_target="tpu_custom_call" | custom-call | tf_op jit(solution)/shard_map/attention_backward/pallas_call | solution.py:858
  255.1 95.4 %tail.1 = (bf16[256,1024]{1,0:T(8,128)(2,1)}, f32[256,1024]{1,0:T(8,128)}, f32[8,256]{1,0:T(8,128)}, bf16[1024,1152]{1,0:T(8,128)(2,1)}, bf16[1024,1024]{1,0:T(8...) custom-call(bf16[8,256,256]{2,1,0:T(8,128)(2,1)} %get-tuple-element., ...), custom_call_target="tpu_custom_call" | custom-call | tf_op jit(solution)/shard_map/tail/pallas_call | solution.py:1605
  350.5 11.5 %widen.1 = (f32[1,1024]{1,0:T(1,128)}, f32[1024,1024]{1,0:T(8,128)}, f32[1024,512]{1,0:T(8,128)}, f32[1024,512]{1,0:T(8,128)}, f32[1024,1024]{1,0:T(8,128)}, /*i...) custom-call(f32[8,256]{1,0:T(8,128)} %get-tuple-element.91.gains, ...), custom_call_target="tpu_custom_call" | custom-call | tf_op jit(solution)/shard_map/widen/pallas_call | solution.py:1676

commit v7 on v6

--- a/solution.py
+++ b/solution.py
@@ -196,15 +196,21 @@
     wd_ref,
     o_ref,
     xa_ref,
+    kv_any,
+    kvt_any,
+    q_any,
+    ot_any,
+    stat_any,
+    g_all,
+    wg_all,
+    wu_all,
+    wd_all,
     kv_ref,
     kvt_ref,
     q_ref,
     ot_ref,
     stat_ref,
-    g_all,
-    wg_all,
-    wu_all,
-    wd_all,
+    kept_sem,
     pay,
     turn,
     in_ref,
@@ -370,6 +376,18 @@
         share_weight(1, (0, 2, 1)[i]).start()
         share_weight(2, (1, 2, 0)[i]).start()
 
+    kept = (
+        (kv_ref, kv_any),
+        (kvt_ref, kvt_any),
+        (q_ref, q_any),
+        (ot_ref, ot_any),
+        (stat_ref, stat_any),
+    )
+
+    def keep(i, t):
+        src, dst = kept[i]
+        return pltpu.make_async_copy(src.at[t], dst.at[t], kept_sem.at[i, t])
+
     def arrival(t):
         return pltpu.make_async_copy(pay.at[0], in_ref.at[t], recv_sem.at[t])
 
@@ -477,6 +495,8 @@
         stat_ref[t] = jnp.where(rows == 0, lse, start.astype(F32))
         upright = jnp.concatenate([out_t[:, :tok], out_t[:, tok:]], 0)
         obuf[t] = jnp.transpose(upright).astype(BF16)
+        for i in range(5):
+            keep(i, t).start()
         owner = 2 * t + me_s
         home = (sigma == me_s) & (owner == me_b)
         place = o_ref.at[:, pl.ds(pl.multiple_of(kappa * 2 * HD, 2 * HD), 2 * HD)]
@@ -515,6 +535,8 @@
 
     def finish_steps(t, carry):
         forward(t).wait_send()
+        for i in range(5):
+            keep(i, t).wait()
         owner = 2 * t + me_s
         home = (sigma == me_s) & (owner == me_b)
 
@@ -587,8 +609,14 @@
             jax.ShapeDtypeStruct((4, *w_down.shape), BF16),
         ),
         in_specs=[vm] * 6 + [hbm] * 6,
-        out_specs=(vm,) * 7 + (hbm,) * 4,
+        out_specs=(vm,) * 2 + (hbm,) * 9,
         scratch_shapes=[
+            pltpu.VMEM((steps, 2 * tok, 2 * HD), BF16),
+            pltpu.VMEM((steps, 2 * HD, 2 * tok), BF16),
+            pltpu.VMEM((steps, tok, 2 * HD), BF16),
+            pltpu.VMEM((steps, HD, 2 * tok), F32),
+            pltpu.VMEM((steps, 8, 2 * tok), F32),
+            dma((5, steps)),
             pltpu.VMEM((KV, tok + 16, 4 * HD), BF16),
             pltpu.VMEM((2, tok, 2 * HD), F32),
             pltpu.VMEM((steps, tok + 16, 4 * HD), BF16),
@@ -621,11 +649,11 @@
 def attention_backward_kernel(
     blocks,
     do_ref,
-    kv_ref,
-    kvt_ref,
-    q_ref,
-    ot_ref,
-    stat_ref,
+    kv_any,
+    kvt_any,
+    q_any,
+    ot_any,
+    stat_any,
     cos_ref,
     sin_ref,
     mix_ref,
@@ -637,6 +665,12 @@
     dwg_in,
     dwu_in,
     dwd_in,
+    kv_ref,
+    kvt_ref,
+    q_ref,
+    ot_ref,
+    stat_ref,
+    kept_sem,
     turn,
     turn_sem,
     in_ref,
@@ -666,6 +700,10 @@
         for i, src in enumerate((cos_ref, sin_ref))
         for t in range(steps)
     ]
+    kept = ((q_any, q_ref), (kv_any, kv_ref), (kvt_any, kvt_ref), (ot_any, ot_ref), (stat_any, stat_ref))
+    tables_in += [
+        pltpu.make_async_copy(src, dst, kept_sem.at[i]) for i, (src, dst) in enumerate(kept)
+    ]
     for copy in tables_in:
         copy.start()
     greet_all(2, blocks, me_s, me_b)
@@ -864,9 +902,11 @@
             jax.ShapeDtypeStruct((2, *dwu.shape[1:]), BF16),
             jax.ShapeDtypeStruct((3, *dwd.shape[1:]), BF16),
         ),
-        in_specs=[vm] * (len(vectors) - 2) + [hbm] * 6,
+        in_specs=[vm] + [hbm] * (len(vectors) + 3),
         out_specs=(vm,) + (hbm,) * 4,
         scratch_shapes=[
+            *(pltpu.VMEM(a.shape, a.dtype) for a in vectors[1:6]),
+            dma((5,)),
             pltpu.VMEM((2, steps, tok, 2 * HD), F32),
             dma((2, steps)),
             pltpu.VMEM((steps, tok, 2 * HD), BF16),
@@ -908,9 +948,9 @@
     wg_all,
     wu_all,
     wd_all,
-    res_ref,
-    mix_peer,
-    xl_ref,
+    res_any,
+    mix_any,
+    xl_any,
     dlog_ref,
     dh_ref,
     datt_ref,
@@ -921,6 +961,10 @@
     dwd_out,
     dwg_in,
     dwu_in,
+    res_ref,
+    mix_peer,
+    xl_ref,
+    out_sem,
     wr_ref,
     rw_ref,
     h1_ref,
@@ -1014,6 +1058,9 @@
     h1_ref[...] = h1
     xl = (h1 * rms_scale(h1) * gain_ref[...]).astype(BF16)
     xl_ref[...] = xl
+    store_xl = pltpu.make_async_copy(xl_ref, xl_any, out_sem.at[3])
+    store_xl.start()
+    store_res = pltpu.make_async_copy(res_ref, res_any, out_sem.at[4])
     logits = mm(xl, wr_ref[...])
     routed = rw > 0.0
     top = jnp.max(jnp.where(routed, logits, NEG), -1, keepdims=True)
@@ -1074,6 +1121,9 @@
 
     def apart(k):
         return lax.rem(k - line + 3, 4)
+
+    def store_mix(n):
+        return pltpu.make_async_copy(mix_peer.at[apart(n)], mix_any.at[n], out_sem.at[apart(n)])
 
     def place_of(j):
         return jnp.where(line < 2, lax.rem(line + j, 4), lax.rem(line + 4 - j, 4))
@@ -1127,13 +1177,15 @@
         @pl.when(j == 0)
         def _():
             res_ref[...] = h1_ref[...] + acc_o[...]
+            store_res.start()
             d_in[...] = acc_d[...]
             d_c[...] = acc_c[...]
 
         @pl.when(j > 0)
         def _():
-            mix_peer[n] = acc_o[...].astype(BF16)
             to = apart(n)
+            mix_peer[to] = acc_o[...].astype(BF16)
+            store_mix(n).start()
             d_send[to] = acc_d[...].astype(BF16)
             turned = jnp.transpose(acc_c[...])[:experts]
             high = turned.astype(BF16)
@@ -1273,6 +1325,9 @@
     for n in (1, 2, 3):
         give_back(flip(line, n)).wait_send()
         give_back_too(flip(line, n)).wait_send()
+        store_mix(flip(line, n)).wait()
+    store_xl.wait()
+    store_res.wait()
     for k in range(4):
 
         @pl.when((k <= line) & (line < 3))
@@ -1327,8 +1382,12 @@
             jax.ShapeDtypeStruct((d // 2, ff), BF16),
         ),
         in_specs=[vm] * 6 + [hbm] * 9,
-        out_specs=(vm,) * 8 + (hbm,) * 5,
+        out_specs=(hbm,) * 3 + (vm,) * 5 + (hbm,) * 5,
         scratch_shapes=[
+            vmem((tok, d), F32),
+            vmem((3, tok, d), BF16),
+            vmem((tok, d), BF16),
+            dma((5,)),
             vmem((d, 128), BF16),
             vmem((tok, 128), F32),
             vmem((tok, d), F32),
@@ -1384,15 +1443,15 @@
 def tail_kernel(
     got,
     xa_ref,
-    x_ref,
     gain_ref,
-    dh_ref,
     ao_ref,
     datt_ref,
     xl_ref,
     dlog_ref,
     dgain2_ref,
-    own_ref,
+    x_any,
+    dh_any,
+    own_any,
     wq_any,
     wk_any,
     wv_any,
@@ -1409,12 +1468,23 @@
     res_ref,
     dx_ref,
     gsum_ref,
+    o_any,
+    q_any,
+    kv_any,
+    eg_any,
+    eu_any,
+    ed_any,
     fin_o,
     fin_q,
     fin_kv,
     eg_out,
     eu_out,
     ed_out,
+    store_sem,
+    x_ref,
+    dh_ref,
+    own_ref,
+    late_sem,
     mix_in,
     wq_ref,
     wk_ref,
@@ -1468,6 +1538,23 @@
         pltpu.make_async_copy(src, dst, load_sem.at[3, i + 1])
         for i, (src, dst) in enumerate(((wq_any, wq_ref), (wk_any, wk_ref), (wv_any, wv_ref)))
     ]
+    projections += [
+        pltpu.make_async_copy(src, dst, late_sem.at[i])
+        for i, (src, dst) in enumerate(((x_any, x_ref), (dh_any, dh_ref), (own_any, own_ref)))
+    ]
+    stores = [
+        pltpu.make_async_copy(src, dst, store_sem.at[i])
+        for i, (src, dst) in enumerate(
+            (
+                (fin_o, o_any),
+                (fin_q, q_any),
+                (fin_kv, kv_any),
+                (eg_out, eg_any),
+                (eu_out, eu_any),
+                (ed_out, ed_any),
+            )
+        )
+    ]
     for copy in projections:
         copy.start()
     for i in range(3):
@@ -1577,6 +1664,9 @@
     for_q.back(3)
     for_kv.back(3)
     gsum_ref[...] = gain_total(2)
+    for i in range(3):
+        expert_swap(i).wait()
+        stores[3 + i].start()
     for item in sums:
         item.back(4)
     result = own_ref[...]
@@ -1585,10 +1675,11 @@
     for n in range(3):
         result = result + mix_in[n].astype(F32)
     res_ref[...] = result.astype(BF16)
-    for item in sums:
+    for item, store in zip(sums, stores):
         item.finish()
-    for i in range(3):
-        expert_swap(i).wait()
+        store.start()
+    for store in stores:
+        store.wait()
     for s in range(3):
         for n in range(len(stages[s])):
             gain_copy(s, n).wait_send()
@@ -1613,9 +1704,18 @@
             jax.ShapeDtypeStruct((d, ff), BF16),
             jax.ShapeDtypeStruct((ff, d), BF16),
         ),
-        in_specs=[vm] * (len(blocks_in) - 3) + [hbm] * 13,
-        out_specs=(vm,) * 9,
+        in_specs=[vm] * (len(blocks_in) - 6) + [hbm] * 16,
+        out_specs=(vm,) * 3 + (hbm,) * 6,
         scratch_shapes=[
+            *(vmem((d, width), BF16) for width in widths),
+            vmem((d, ff), BF16),
+            vmem((d, ff), BF16),
+            vmem((ff, d), BF16),
+            dma((6,)),
+            vmem((tok, d), BF16),
+            vmem((tok, d), F32),
+            vmem((tok, d), F32),
+            dma((3,)),
             vmem((3, tok, d), BF16),
             vmem((d, H * HD), BF16),
             vmem((d, KV * HD), BF16),
@@ -2069,14 +2169,14 @@
     blocks_in = (
         got,
         xa,
-        tokens[0],
         gain1,
-        grad_h1,
         att_low,
         grad_att,
         xl,
         grad_logits,
         gain2_terms,
+        tokens[0],
+        grad_h1,
         own,
         w_query,
         w_key,

time: 362 us -> 357 us (0.986)
  Pallas kernels: 360 us -> 354 us
where the time goes in v7:
time: 357 us
  Pallas kernels  354 us (99%)
    pallas_call x1, Pallas kernels, tail(): pl.pallas_call(tail_kernel, out_shape=(jax.ShapeDtypeStruct((tok, d), BF1...  92.9 us
    pallas_call x1, Pallas kernels, mixture(): pl.pallas_call(mixture_kernel, out_shape=(jax.ShapeDtypeStruct((tok, d),...  91.3 us
    pallas_call x1, Pallas kernels, attention_forward(): pl.pallas_call(functools.partial(attention_forward_kernel, blocks), out_s...  83.4 us
    pallas_call x1, Pallas kernels, attention_backward(): pl.pallas_call(functools.partial(attention_backward_kernel, blocks), out_...  75.4 us
    pallas_call x1, Pallas kernels, widen(): pl.pallas_call(widen_kernel, grid=(parts,), out_shape=(jax.ShapeDtypeStru...  11.5 us

profile of v7, /device:TPU:0, one launch (start us, length us, event | category | flops | bytes accessed | tf_op | source)
XLA Modules:
  0.0 356.6 jit_solution(5667145976730350777)
XLA Ops:
  0.6 0.7 convert_reduce_fusion
  1.3 0.6 pad.4.seg_ref
  1.9 83.4 %attention_forward.1 = (bf16[256,1024]{1,0:T(8,128)(2,1)}, bf16[256,1024]{1,0:T(8,128)(2,1)}, bf16[8,512,128]{2,1,0:T(8,128)(2,1)}, bf16[8,128,512]{2,1,0:T(8,12...) custom-call(bf16[256,1024]{1,0:T(8,128)(2,1)} %bitcast.18, ...), custom_call_target="tpu_custom_call" | custom-call | tf_op jit(solution)/shard_map/attention_forward/pallas_call | solution.py:596
  85.3 91.3 %mixture.1 = (f32[256,1024]{1,0:T(8,128)}, bf16[4,256,1024]{2,1,0:T(8,128)(2,1)}, bf16[256,1024]{1,0:T(8,128)(2,1)}, bf16[256,128]{1,0:T(8,128)(2,1)}, f32[256,1...) custom-call(bf16[256,1024]{1,0:T(8,128)(2,1)} %bitcast.19, ...), custom_call_target="tpu_custom_call" | custom-call | tf_op jit(solution)/shard_map/mixture/pallas_call | solution.py:1367
  176.6 75.4 %attention_backward.1 = (bf16[8,256,256]{2,1,0:T(8,128)(2,1)}, bf16[2,256,1024]{2,1,0:T(8,128)(2,1)}, bf16[2,512,512]{2,1,0:T(8,128)(2,1)}, bf16[2,512,512]{2,1,0:T(8,128)(2,1)}, bf16[3,256,1024]{2,1,0:T(8,128)(2,1)}) custom-call(bf16[256,1024]{1,0:T(8,128)(2,1)} %get-tuple-element.67.do_ref, bf16[8,512,128]{2,1,0:T(8,128)(2,1)} %get-tuple-element.68.kv_any, ...), custom_call_target="tpu_custom_call" | custom-call | tf_op jit(solution)/shard_map/attention_backward/pallas_call | solution.py:896
  252.0 92.9 %tail.1 = (bf16[256,1024]{1,0:T(8,128)(2,1)}, f32[256,1024]{1,0:T(8,128)}, f32[8,256]{1,0:T(8,128)}, bf16[1024,1152]{1,0:T(8,128)(2,1)}, bf16[1024,1024]{1,0:T(8...) custom-call(bf16[8,256,256]{2,1,0:T(8,128)(2,1)} %get-tuple-element., ...), custom_call_target="tpu_custom_call" | custom-call | tf_op jit(solution)/shard_map/tail/pallas_call | solution.py:1696
  344.9 11.5 %widen.1 = (f32[1,1024]{1,0:T(1,128)}, f32[1024,1024]{1,0:T(8,128)}, f32[1024,512]{1,0:T(8,128)}, f32[1024,512]{1,0:T(8,128)}, f32[1024,1024]{1,0:T(8,128)}, /*i...) custom-call(f32[8,256]{1,0:T(8,128)} %get-tuple-element.91.gains, ...), custom_call_target="tpu_custom_call" | custom-call | tf_op jit(solution)/shard_map/widen/pallas_call | solution.py:1776

commit v8 on v7

--- a/solution.py
+++ b/solution.py
@@ -1145,7 +1145,7 @@
             for step in (-1, 1):
                 k = line - step * (j + 1)
 
-                @pl.when((e == 3) & (j < 3) & (k >= 0) & (k < 4))
+                @pl.when((e == 3) & (j == 0) & (k >= 0) & (k < 4))
                 def _():
                     pltpu.make_async_copy(c_in.at[line], c_in.at[k], crecv_sem.at[k]).wait()
                     pltpu.make_async_copy(x_in.at[line], x_in.at[k], recv_sem.at[k]).wait()
@@ -1193,6 +1193,15 @@
             c_send[to, experts:, :] = (turned - high.astype(F32)).astype(BF16)
             give_back_too(n).start()
             give_back(n).start()
+
+        for step in (-1, 1):
+            k = line - step * (j + 1)
+
+            @pl.when((j > 0) & (j < 3) & (k >= 0) & (k < 4))
+            def _():
+                pltpu.make_async_copy(c_in.at[line], c_in.at[k], crecv_sem.at[k]).wait()
+                pltpu.make_async_copy(x_in.at[line], x_in.at[k], recv_sem.at[k]).wait()
+                pass_on(k, step)
 
         x_t[:, rows] = jnp.transpose(x_in[n].astype(F32)).astype(BF16)
         return carry

time: 357 us -> 355 us (level)
  no operation moved by 1% of the time
where the time goes in v8:
time: 355 us; the launch traced here: 354 us
  Pallas kernels  352 us (99%)
    pallas_call x1, Pallas kernels, tail(): pl.pallas_call(tail_kernel, out_shape=(jax.ShapeDtypeStruct((tok, d), BF1...  91.9 us
    pallas_call x1, Pallas kernels, mixture(): pl.pallas_call(mixture_kernel, out_shape=(jax.ShapeDtypeStruct((tok, d),...  90.3 us
    pallas_call x1, Pallas kernels, attention_forward(): pl.pallas_call(functools.partial(attention_forward_kernel, blocks), out_s...  83.4 us
    pallas_call x1, Pallas kernels, attention_backward(): pl.pallas_call(functools.partial(attention_backward_kernel, blocks), out_...  75.1 us
    pallas_call x1, Pallas kernels, widen(): pl.pallas_call(widen_kernel, grid=(parts,), out_shape=(jax.ShapeDtypeStru...  11.5 us

profile of v8, /device:TPU:0, one launch (start us, length us, event | category | flops | bytes accessed | tf_op | source)
XLA Modules:
  0.0 354.3 jit_solution(14753875707077999076)
XLA Ops:
  0.6 0.7 convert_reduce_fusion
  1.3 0.6 pad.4.seg_ref
  1.9 83.4 %attention_forward.1 = (bf16[256,1024]{1,0:T(8,128)(2,1)}, bf16[256,1024]{1,0:T(8,128)(2,1)}, bf16[8,512,128]{2,1,0:T(8,128)(2,1)}, bf16[8,128,512]{2,1,0:T(8,12...) custom-call(bf16[256,1024]{1,0:T(8,128)(2,1)} %bitcast.18, ...), custom_call_target="tpu_custom_call" | custom-call | tf_op jit(solution)/shard_map/attention_forward/pallas_call | solution.py:596
  85.3 90.3 %mixture.1 = (f32[256,1024]{1,0:T(8,128)}, bf16[4,256,1024]{2,1,0:T(8,128)(2,1)}, bf16[256,1024]{1,0:T(8,128)(2,1)}, bf16[256,128]{1,0:T(8,128)(2,1)}, f32[256,1...) custom-call(bf16[256,1024]{1,0:T(8,128)(2,1)} %bitcast.19, ...), custom_call_target="tpu_custom_call" | custom-call | tf_op jit(solution)/shard_map/mixture/pallas_call | solution.py:1376
  175.6 75.1 %attention_backward.1 = (bf16[8,256,256]{2,1,0:T(8,128)(2,1)}, bf16[2,256,1024]{2,1,0:T(8,128)(2,1)}, bf16[2,512,512]{2,1,0:T(8,128)(2,1)}, bf16[2,512,512]{2,1,0:T(8,128)(2,1)}, bf16[3,256,1024]{2,1,0:T(8,128)(2,1)}) custom-call(bf16[256,1024]{1,0:T(8,128)(2,1)} %get-tuple-element.67.do_ref, bf16[8,512,128]{2,1,0:T(8,128)(2,1)} %get-tuple-element.68.kv_any, ...), custom_call_target="tpu_custom_call" | custom-call | tf_op jit(solution)/shard_map/attention_backward/pallas_call | solution.py:896
  250.7 91.9 %tail.1 = (bf16[256,1024]{1,0:T(8,128)(2,1)}, f32[256,1024]{1,0:T(8,128)}, f32[8,256]{1,0:T(8,128)}, bf16[1024,1152]{1,0:T(8,128)(2,1)}, bf16[1024,1024]{1,0:T(8...) custom-call(bf16[8,256,256]{2,1,0:T(8,128)(2,1)} %get-tuple-element., ...), custom_call_target="tpu_custom_call" | custom-call | tf_op jit(solution)/shard_map/tail/pallas_call | solution.py:1705
  342.6 11.5 %widen.1 = (f32[1,1024]{1,0:T(1,128)}, f32[1024,1024]{1,0:T(8,128)}, f32[1024,512]{1,0:T(8,128)}, f32[1024,512]{1,0:T(8,128)}, f32[1024,1024]{1,0:T(8,128)}, /*i...) custom-call(f32[8,256]{1,0:T(8,128)} %get-tuple-element.91.gains, ...), custom_call_target="tpu_custom_call" | custom-call | tf_op jit(solution)/shard_map/widen/pallas_call | solution.py:1785
